TPU v7x, 32 devices: a whole 2x2x4 slice. The times are simulated.
32 devices in a mesh: feat: 16 (over z, x, core), node: 2 (over y).
Axes of the slice: x: 2, y: 2, z: 4, core: 2. Of those that a mesh axis runs over, the one named last changes fastest.
Arguments:
- feats: bfloat16 [1024, 8192], P('feat', 'node'), may hold values from -6 to 6
- weight: bfloat16 [1024, 256], replicated, may hold values from -0.1875 to 0.1875
- tile_row: int32 [16, 2, 8], P('feat', 'node'), may hold values from 0 to 1, as said below
- tile_col: int32 [16, 2, 8], P('feat', 'node'), may hold values from 0 to 3
- tile_block: int32 [16, 2, 8], P('feat', 'node'), may hold values from 0 to 7, each once within a row
- tile_count: int32 [16, 2], P('feat', 'node'), may hold values from 2 to 8, as said below
- edge_blocks: bfloat16 [16, 2, 8, 128, 128], P('feat', 'node'), may hold values from -0.375 to 0.375
- cotangent: bfloat16 [256, 8192], P(None, ('node', 'feat')), may hold values from -0.06591797 to 0.06591797
Outputs:
- act: bfloat16 [256, 8192], P(None, ('node', 'feat'))
- weight_grad: float32 [1024, 256], P(('feat', 'node'))
Inputs may be any that keep to these rules, and one draw needn't show every extreme that they name: Within one device block the pairs (tile_row, tile_col) of its 8 slots name every tile position once. Within one device block tile_block names each of its 8 blocks once. Slots s at or after tile_count of their block are unused; some block uses all 8 slots.
All inputs are finite; a program needn't handle non-finite values.
Results may differ from a plain program's by a relative error of at most 0.012.
Values may be sent and summed in bfloat16 or wider, within the bound.
No kernel may reach another device: no remote copies, remote signals or barrier semaphores. Data moves between devices by JAX's collectives and lax.ppermute only.
A program may use at most 64 MiB of HBM per device.

v0:
```python
import jax
import jax.numpy as jnp
from jax import lax
from jax.sharding import PartitionSpec as P

root_half = 0.7071067811865476
inv_root_two_pi = 0.3989422804014327


def dense_adjacency(row_tile, col_tile, block_index, live_count, blocks, row_tiles, col_tiles):
    slot_total = row_tile.shape[0]
    tile_size = blocks.shape[-1]
    position = row_tile * col_tiles + col_tile
    places = jnp.arange(row_tiles * col_tiles, dtype=jnp.int32)
    active = jnp.arange(slot_total, dtype=jnp.int32) < live_count
    matches = (position[None, :] == places[:, None]) & active[None, :]
    chosen = jnp.sum(jnp.where(matches, block_index[None, :], 0), axis=1)
    filled = jnp.any(matches, axis=1)
    picked = jnp.take(blocks, chosen, axis=0) * filled[:, None, None].astype(blocks.dtype)
    layout = picked.reshape(row_tiles, col_tiles, tile_size, tile_size)
    return layout.transpose(0, 2, 1, 3).reshape(row_tiles * tile_size, col_tiles * tile_size)


def gelu_parts(preact):
    normal_cdf = 0.5 * (1.0 + lax.erf(preact * root_half))
    normal_pdf = jnp.exp(-0.5 * preact * preact) * inv_root_two_pi
    return (preact * normal_cdf, normal_cdf + preact * normal_pdf)


def two_part(values):
    upper = lax.optimization_barrier(values.astype(jnp.bfloat16))
    lower = (values - upper.astype(jnp.float32)).astype(jnp.bfloat16)
    return (upper, lower)


def split_dot(left, right, dims, left_split):
    if left_split:
        left_hi, left_lo = two_part(left)
        right_hi, right_lo = two_part(right)
        total = lax.dot_general(left_hi, right_hi, dims, preferred_element_type=jnp.float32)
        total = total + lax.dot_general(left_hi, right_lo, dims, preferred_element_type=jnp.float32)
        return total + lax.dot_general(left_lo, right_hi, dims, preferred_element_type=jnp.float32)
    right_hi, right_lo = two_part(right)
    total = lax.dot_general(left, right_hi, dims, preferred_element_type=jnp.float32)
    return total + lax.dot_general(left, right_lo, dims, preferred_element_type=jnp.float32)


def per_device(feats, weight, tile_row, tile_col, tile_block, tile_count, edge_blocks, cotangent):
    feat_devices = lax.axis_size("feat")
    part_width, shard_nodes = feats.shape
    own_rows = shard_nodes // feat_devices
    tile_size = edge_blocks.shape[-1]
    row_tiles = own_rows // tile_size
    slot_total = edge_blocks.shape[2]
    adjacency = dense_adjacency(
        tile_row[0, 0],
        tile_col[0, 0],
        tile_block[0, 0],
        tile_count[0, 0],
        edge_blocks[0, 0],
        row_tiles,
        slot_total // row_tiles,
    )
    by_dest = feats.reshape(part_width, feat_devices, own_rows)
    contract_last = (((1,), (1,)), ((), ()))
    contract_first = (((0,), (0,)), ((), ()))
    local_rows = lax.all_to_all(by_dest, "feat", split_axis=1, concat_axis=0, tiled=True)[:, 0, :]
    hidden = lax.dot_general(
        lax.all_gather(local_rows, "node", axis=1, tiled=True),
        adjacency,
        contract_last,
        preferred_element_type=jnp.float32,
    )
    preact = split_dot(weight, hidden, contract_first, False)
    output, derivative = gelu_parts(preact)
    pre_grad = cotangent.astype(jnp.float32) * derivative
    weight_grad = lax.psum_scatter(
        split_dot(hidden, pre_grad, contract_last, True),
        ("feat", "node"),
        scatter_dimension=0,
        tiled=True,
    )
    return (output.astype(jnp.bfloat16), weight_grad)


def solution(mesh):
    return jax.shard_map(
        per_device,
        mesh=mesh,
        in_specs=(
            P("feat", "node"),
            P(),
            P("feat", "node", None),
            P("feat", "node", None),
            P("feat", "node", None),
            P("feat", "node"),
            P("feat", "node", None, None, None),
            P(None, ("node", "feat")),
        ),
        out_specs=(P(None, ("node", "feat")), P(("feat", "node"), None)),
        check_vma=False,
    )
```

profile of v0, /device:TPU:0, one launch (start us, length us, event | category | flops | bytes accessed | tf_op | source)
XLA Modules:
  0.0 199.0 jit_solution(8842081481812544927)
XLA Ops:
  7.2 0.0 copy-start
  7.2 2.0 copy.39
  9.1 7.4 %all-to-all-start = ((bf16[64,16,256]{2,0,1:T(8,128)(2,1)}), bf16[64,16,256]{2,0,1:T(8,128)(2,1)S(1)}, u32[]{:S(2)}, u32[]{:S(2)}) async-start(bf16[64,16,256]{2,0,1:T(8,128)(2,1)} %bitcast.38), calls=%async_computation | async-start | bytes 1048576 | tf_op jit(solution)/shard_map/all_to_all | solution.py:67
  16.5 0.0 copy-start.5
  16.5 0.0 copy-start.6
  16.5 0.0 all-gather.2.cloned.1.call-start
  17.2 0.0 copy-done.5
  17.2 0.0 copy-done.6
  17.3 13.7 %all-to-all-done = bf16[64,16,256]{2,0,1:T(8,128)(2,1)S(1)} async-done(((bf16[64,16,256]{2,0,1:T(8,128)(2,1)}), bf16[64,16,256]{2,0,1:T(8,128)(2,1)S(1)}, u32[]{:S(2)}, u32[]{:S(2)}) %all-to-all-start) | async-done | bytes 524320 | tf_op jit(solution)/shard_map/all_to_all | solution.py:67
  31.0 0.8 copy-done.1
  31.8 0.0 all-gather.2.cloned.1.call-update
  31.8 0.0 copy-start.2
  31.8 0.0 reduce-scatter.2.cloned.1.call-start
  31.9 0.1 fusion.10
  32.0 0.1 reshape.62
  32.1 0.1 select_reduce_fusion
  32.2 0.1 reduce_sum.14
  32.3 0.0 copy-done.3
  32.3 0.1 copy.25
  32.4 0.3 copy-done.2
  32.8 0.6 gather_fusion
  33.4 0.2 fusion.8
  33.6 19.0 %all-gather.2.cloned.1.call-done = bf16[1024,512]{1,0:T(8,128)(2,1)} async-done(((bf16[1024,256]{1,0:T(8,128)(2,1)}), bf16[1024,512]{1,0:T(8,128)(2,1)}) %all-gather.2.cloned.1.call-update) | async-done | bytes 1048592 | tf_op jit(solution)/shard_map/all_gather | solution.py:69
  52.7 1.7 fusion.14
  54.4 0.3 fusion.15
  54.7 0.4 fusion.13
  55.1 0.4 fusion.16
  55.4 0.4 convolution_add_fusion.1
  55.9 1.4 convolution_add_fusion
  57.3 0.0 reduce-scatter.2.cloned.1.call-update
  57.3 0.8 copy.26
  58.0 134.1 %reduce-scatter.2.cloned.1.call-done = f32[32,256]{1,0:T(8,128)} async-done(((f32[1024,256]{1,0:T(8,128)}), f32[32,256]{1,0:T(8,128)}) %reduce-scatter.2.cloned.1.call-update) | async-done | bytes 32784 | tf_op jit(solution)/shard_map/reduce_scatter | solution.py:77
  (11 shorter events, 0.0 us)
Async XLA Ops:
  7.2 47.2 %copy-start = (bf16[1024,256]{1,0:T(8,128)(2,1)S(1)}, bf16[1024,256]{1,0:T(8,128)(2,1)}, u32[]{:S(2)}) copy-start(bf16[1024,256]{1,0:T(8,128)(2,1)} %param.9) | copy-start | bytes 1572868
  9.1 21.8 %all-to-all-start = ((bf16[64,16,256]{2,0,1:T(8,128)(2,1)}), bf16[64,16,256]{2,0,1:T(8,128)(2,1)S(1)}, u32[]{:S(2)}, u32[]{:S(2)}) async-start(bf16[64,16,256]{2,0,1:T(8,128)(2,1)} %bitcast.38), calls=%async_computation | async-start | bytes 1048576 | tf_op jit(solution)/shard_map/all_to_all | solution.py:67
  16.5 0.7 copy-start.5
  16.5 0.7 copy-start.6
  16.5 36.1 %all-gather.2.cloned.1.call-start = ((), (), s32[]{:S(2)}) async-start(), calls=%async_computation.2 | async-start | bytes 1572864 | tf_op jit(solution)/shard_map/all_gather | solution.py:69
  31.0 0.8 copy-start.1
  31.0 1.1 copy-start.4
  31.0 1.3 copy-start.3
  31.8 1.0 copy-start.2
  31.8 160.4 %reduce-scatter.2.cloned.1.call-start = ((), (), s32[]{:S(2)}) async-start(), calls=%async_computation.3 | async-start | bytes 1081344 | tf_op jit(solution)/shard_map/reduce_scatter | solution.py:77
Sparse Core Ops, SparseCore 0:
  31.9 20.7 all-gather.1
  57.4 134.7 reduce-scatter.1
where the time goes:
time: 199 us
  waiting for transfers between devices  167 us (84%)
  between operations  14.8 us (7%)
  starting transfers between devices  7.44 us (4%)
  local copies, waits for them, and re-layouts  4.76 us (2%)
  matrix products  4.55 us (2%)
    reduce_scatter x1, waiting for transfers between devices, per_device(): lax.psum_scatter(split_dot(hidden, pre_grad, contract_last, True), ('feat...  134 us
    all_gather x1, waiting for transfers between devices, per_device(): lax.all_gather(local_rows, 'node', axis=1, tiled=True)  19 us
    all_to_all x1, waiting for transfers between devices, per_device(): lax.all_to_all(by_dest, 'feat', split_axis=1, concat_axis=0, tiled=True)  13.7 us
    all_to_all x1, starting transfers between devices, per_device(): lax.all_to_all(by_dest, 'feat', split_axis=1, concat_axis=0, tiled=True)  7.36 us
  transfers between devices with their start and end apart: 3, of which 3 were waited for; matrix products, arithmetic and copies ran while one was open for 1% of the time, Pallas kernels for 0%

commit v1 on v0

v1 whole, which is shorter than its diff:
```python
import jax
import jax.numpy as jnp
from jax import lax
from jax.sharding import Mesh, PartitionSpec as P

root_half = 0.7071067811865476
inv_root_two_pi = 0.3989422804014327

SWAP = ((0, 1), (1, 0))
TRANSPOSE = ((0, 0), (1, 2), (2, 1), (3, 3))


def dense_adjacency(row_tile, col_tile, block_index, live_count, blocks, row_tiles, col_tiles):
    slot_total = row_tile.shape[0]
    tile_size = blocks.shape[-1]
    position = row_tile * col_tiles + col_tile
    places = jnp.arange(row_tiles * col_tiles, dtype=jnp.int32)
    active = jnp.arange(slot_total, dtype=jnp.int32) < live_count
    matches = (position[None, :] == places[:, None]) & active[None, :]
    chosen = jnp.sum(jnp.where(matches, block_index[None, :], 0), axis=1)
    filled = jnp.any(matches, axis=1)
    picked = jnp.take(blocks, chosen, axis=0) * filled[:, None, None].astype(blocks.dtype)
    layout = picked.reshape(row_tiles, col_tiles, tile_size, tile_size)
    return layout.transpose(0, 2, 1, 3).reshape(row_tiles * tile_size, col_tiles * tile_size)


def gelu_parts(preact):
    normal_cdf = 0.5 * (1.0 + lax.erf(preact * root_half))
    normal_pdf = jnp.exp(-0.5 * preact * preact) * inv_root_two_pi
    return (preact * normal_cdf, normal_cdf + preact * normal_pdf)


def dot(left, right, left_dim, right_dim):
    return lax.dot_general(
        left, right, (((left_dim,), (right_dim,)), ((), ())), preferred_element_type=jnp.float32
    )


def per_device(feats, weight, tile_row, tile_col, tile_block, tile_count, edge_blocks, cotangent):
    columns = lax.axis_size("col")
    pairs = lax.axis_size("hi")
    core = lax.axis_index("core")
    width, shard_nodes = feats.shape
    rows = shard_nodes // (2 * columns)
    hidden = weight.shape[1]
    tile_size = edge_blocks.shape[-1]
    row_tiles = rows // tile_size
    slot_total = edge_blocks.shape[2]
    bf16 = jnp.bfloat16

    by_dest = feats.reshape(width, 2 * columns, rows)
    arrived = lax.all_to_all(by_dest, ("col", "lo"), split_axis=1, concat_axis=0, tiled=True)
    arrived = arrived.reshape(columns, 2, width, rows)

    adjacency = dense_adjacency(
        tile_row[0, 0], tile_col[0, 0], tile_block[0, 0], tile_count[0, 0], edge_blocks[0, 0],
        row_tiles, slot_total // row_tiles,
    )
    adjacency = lax.ppermute(adjacency, ("core", "lo"), TRANSPOSE)
    cot = lax.ppermute(cotangent, ("core", "lo"), TRANSPOSE)

    own_weight = lax.dynamic_index_in_dim(
        weight.reshape(columns, 2, width, hidden), core, 1, keepdims=False
    ).reshape(columns * width, hidden)
    nodes = arrived.transpose(0, 2, 1, 3).reshape(columns * width, 2 * rows)
    part = dot(own_weight, nodes, 0, 0)
    other = lax.ppermute(part.astype(bf16), "core", SWAP)
    projected = (part + other.astype(jnp.float32)).astype(bf16)
    if pairs > 1:
        projected = lax.all_gather(projected, "hi", axis=1, tiled=True)
    preact = dot(projected, adjacency, 1, 1)
    output, derivative = gelu_parts(preact)
    pre_grad = (cot.astype(jnp.float32) * derivative).astype(bf16)
    node_part = dot(pre_grad, adjacency, 1, 0)
    if pairs > 1:
        node_part = lax.psum_scatter(node_part, "hi", scatter_dimension=1, tiled=True)
    node_other = lax.ppermute(node_part.astype(bf16), "core", SWAP)
    node_grad = (node_part + node_other.astype(jnp.float32)).astype(bf16)
    terms = dot(nodes, node_grad, 1, 1)
    share = width // (2 * pairs)
    if pairs > 1:
        terms = terms.reshape(columns, pairs, 2 * share, hidden)
        terms = lax.psum_scatter(terms, "hi", scatter_dimension=1, tiled=True)
    terms = terms.astype(bf16).reshape(2 * columns, share, hidden)
    act = lax.ppermute(output.astype(bf16), ("core", "lo"), TRANSPOSE)
    terms = lax.all_to_all(terms, ("col", "lo"), split_axis=0, concat_axis=0, tiled=True)
    weight_grad = jnp.sum(terms.astype(jnp.float32), axis=0)
    return (act, weight_grad)


def solution(mesh):
    n_feat, n_node = mesh.shape["feat"], mesh.shape["node"]
    fine = Mesh(
        mesh.devices.reshape(n_feat // 2, 2, n_node // 2, 2), ("col", "core", "hi", "lo")
    )
    feat, node = ("col", "core"), ("hi", "lo")
    return jax.shard_map(
        per_device,
        mesh=fine,
        in_specs=(
            P(feat, node),
            P(),
            P(feat, node, None),
            P(feat, node, None),
            P(feat, node, None),
            P(feat, node),
            P(feat, node, None, None, None),
            P(None, node + feat),
        ),
        out_specs=(P(None, node + feat), P(feat + node, None)),
        check_vma=False,
    )
```

time: 199 us -> 52.9 us (0.27)
  waiting for transfers between devices: 167 us -> 22.1 us
  between operations: 14.8 us -> 1.49 us
  starting transfers between devices: 7.44 us -> 19.8 us
  matrix products: 4.55 us -> 1.23 us
    reduce_scatter x1 -> x0, waiting for transfers between devices: 134 us -> none  [per_device(): lax.psum_scatter(split_dot(hidden, pre_grad, contract_last, True), ('feat...]
    all_gather x1 -> x0, waiting for transfers between devices: 19 us -> none  [per_device(): lax.all_gather(local_rows, 'node', axis=1, tiled=True)]
    ppermute x0 -> x5, starting transfers between devices: none -> 7.09 us  [the longest x1 5.01 us: per_device(): node_other = lax.ppermute(node_part.astype(bf16), 'core', SWAP)]
    all_to_all x1 -> x2, waiting for transfers between devices: 13.7 us -> 20.5 us  [the longest x1 11.1 us: per_device(): lax.all_to_all(by_dest, ('col', 'lo'), split_axis=1, concat_axis=0, tiled...]
    all_to_all x1 -> x2, starting transfers between devices: 7.36 us -> 12.8 us  [the longest x1 8.44 us: per_device(): lax.all_to_all(by_dest, ('col', 'lo'), split_axis=1, concat_axis=0, tiled...]
    dot_general x6 -> x4, matrix products: 4.55 us -> 1.23 us  [dot(): lax.dot_general(left, right, (((left_dim,), (right_dim,)), ((), ())), pre...]
  transfers between devices with their start and end apart: 3 -> 7, of which waited for: 3 -> 4; matrix products, arithmetic and copies ran while one was open for 1% -> 5% of each run, Pallas kernels for 0% -> 0%
where the time goes in v1:
time: 52.9 us; the launch traced here: 52.5 us
  waiting for transfers between devices  22.1 us (42%)
  starting transfers between devices  19.8 us (37%)
  local copies, waits for them, and re-layouts  6.71 us (13%)
  between operations  1.49 us (3%)
  matrix products  1.23 us (2%)
  other arithmetic  1.17 us (2%)
    all_to_all x1, waiting for transfers between devices, per_device(): lax.all_to_all(by_dest, ('col', 'lo'), split_axis=1, concat_axis=0, tiled...  11.1 us
    all_to_all x1, waiting for transfers between devices, per_device(): lax.all_to_all(terms, ('col', 'lo'), split_axis=0, concat_axis=0, tiled=T...  9.49 us
    all_to_all x1, starting transfers between devices, per_device(): lax.all_to_all(by_dest, ('col', 'lo'), split_axis=1, concat_axis=0, tiled...  8.44 us
    ppermute x1, starting transfers between devices, per_device(): node_other = lax.ppermute(node_part.astype(bf16), 'core', SWAP)  5.01 us
    all_to_all x1, starting transfers between devices, per_device(): lax.all_to_all(terms, ('col', 'lo'), split_axis=0, concat_axis=0, tiled=T...  4.31 us
    unnamed x15, local copies, waits for them, and re-layouts  2.59 us
    reshape x1, local copies, waits for them, and re-layouts, per_device(): by_dest = feats.reshape(width, 2 * columns, rows)  1.95 us
    dot_general x4, matrix products, dot(): lax.dot_general(left, right, (((left_dim,), (right_dim,)), ((), ())), pre...  1.23 us
  transfers between devices with their start and end apart: 7, of which 4 were waited for; matrix products, arithmetic and copies ran while one was open for 5% of the time, Pallas kernels for 0%

profile of v1, /device:TPU:0, one launch (start us, length us, event | category | flops | bytes accessed | tf_op | source)
XLA Modules:
  0.0 52.5 jit_solution(3801260876668322899)
XLA Ops:
  0.6 0.0 copy-start
  0.6 1.9 %copy.35 = bf16[8,16,8,256]{3,2,0,1:T(8,128)(2,1)} copy(bf16[8,16,8,256]{3,2,1,0:T(8,128)(2,1)} %bitcast.49) | data formatting | bytes 1048576 | tf_op jit(solution)/shard_map/reshape | solution.py:51
  2.6 8.4 %all-to-all-start = ((bf16[64,16,256]{2,0,1:T(8,128)(2,1)}), bf16[64,16,256]{2,0,1:T(8,128)(2,1)S(1)}, u32[]{:S(2)}, u32[]{:S(2)}) async-start(bf16[64,16,256]{2,0,1:T(8,128)(2,1)} %bitcast.38), calls=%async_computation | async-start | bytes 1048576 | tf_op jit(solution)/shard_map/all_to_all | solution.py:52
  11.7 0.6 %copy-done.4 = s32[1,1,8]{2,1,0:T(1,128)S(1)} copy-done((s32[1,1,8]{2,1,0:T(1,128)S(1)}, s32[1,1,8]{2,1,0:T(1,128)}, u32[]{:S(2)}) %copy-start.4) | copy-done | bytes 56
  12.4 0.0 copy-done.5
  12.4 0.1 fusion.14
  12.5 0.1 reshape.83
  12.6 0.7 %copy-done.2 = s32[1,1,8]{2,1,0:T(1,128)S(1)} copy-done((s32[1,1,8]{2,1,0:T(1,128)S(1)}, s32[1,1,8]{2,1,0:T(1,128)}, u32[]{:S(2)}) %copy-start.2) | copy-done | bytes 56
  13.2 0.1 select_reduce_fusion
  13.4 0.1 reduce_sum.23
  13.5 0.6 %gather_fusion = bf16[8,128,128]{2,1,0:T(8,128)(2,1)S(1)} fusion(bf16[8,128,128]{2,1,0:T(8,128)(2,1)S(1)} %bitcast.50, s32[1024]{0:T(1024)S(1)} %pad_clamp_fusion), kind=kCustom, calls=%fused_computation | custom fusion | bytes 524320 | tf_op jit(solution)/shard_map/jit(_take)/gather | solution.py:22
  14.1 0.2 fusion.8
  14.4 0.7 %collective-permute-start.1 = (bf16[256,512]{1,0:T(8,128)(2,1)S(1)}, bf16[256,512]{1,0:T(8,128)(2,1)S(1)}, u32[]{:S(2)}, u32[]{:S(2)}) collective-permute-start(bf16[256,512]{1,0:T(8,128)(2,1)S(1)} %bitcast.51), channel_id=1, source_target_pairs={{0,0},{1,2},{2,1},{3,3},{4,4},{5,6},{6,5},{7,7},{8,8},{9,10},{10,9... | collective-permute-start | bytes 786440 | tf_op jit(solution)/shard_map/ppermute | solution.py:59
  15.1 11.1 %all-to-all-done = bf16[64,16,256]{2,0,1:T(8,128)(2,1)S(1)} async-done(((bf16[64,16,256]{2,0,1:T(8,128)(2,1)}), bf16[64,16,256]{2,0,1:T(8,128)(2,1)S(1)}, u32[]{:S(2)}, u32[]{:S(2)}) %all-to-all-start) | async-done | bytes 524320 | tf_op jit(solution)/shard_map/all_to_all | solution.py:52
  26.2 0.5 %copy.24 = bf16[8,64,2,256]{3,2,1,0:T(2,128)(2,1)S(1)} copy(bf16[8,64,2,256]{3,1,2,0:T(8,128)(2,1)S(1)} %bitcast.44) | data formatting | bytes 1048576 | tf_op jit(solution)/shard_map/transpose | solution.py:65
  26.7 0.1 copy.28
  26.8 0.3 fusion.18
  27.2 0.1 collective-permute-start
  27.2 0.5 copy-done.3
  27.7 0.7 %collective-permute-start.3 = (bf16[256,256]{1,0:T(8,128)(2,1)S(1)}, bf16[256,256]{1,0:T(8,128)(2,1)S(1)}, u32[]{:S(2)}, u32[]{:S(2)}) collective-permute-start(bf16[256,256]{1,0:T(8,128)(2,1)S(1)} %copy-done.3), channel_id=1, source_target_pairs={{0,0},{1,2},{2,1},{3,3},{4,4},{5,6},{6,5},{7,7},{8,8},{9,10},{10,9... | collective-permute-start | bytes 393224 | tf_op jit(solution)/shard_map/ppermute | solution.py:60
  28.4 0.4 collective-permute-done
  28.8 0.3 multiply_convert_fusion
  29.1 0.3 fusion.19
  29.4 5.0 %collective-permute-start.4 = (bf16[256,512]{1,0:T(8,128)(2,1)S(1)}, bf16[256,512]{1,0:T(8,128)(2,1)S(1)}, u32[]{:S(2)}, u32[]{:S(2)}) collective-permute-start(bf16[256,512]{1,0:T(8,128)(2,1)S(1)} %get-tuple-element.6), channel_id=1, source_target_pairs={{0,2},{2,0},{1,3},{3,1},{4,6},{6,4},{5,7},{7,5},{8,10},{10,8},{9,1... | collective-permute-start | bytes 786440 | tf_op jit(solution)/shard_map/ppermute | solution.py:77
  34.4 1.2 %collective-permute-done.4 = bf16[256,512]{1,0:T(8,128)(2,1)S(1)} collective-permute-done((bf16[256,512]{1,0:T(8,128)(2,1)S(1)}, bf16[256,512]{1,0:T(8,128)(2,1)S(1)}, u32[]{:S(2)}, u32[]{:S(2)}) %collective-permute-start.4) | collective-permute-done | bytes 262176 | tf_op jit(solution)/shard_map/ppermute | solution.py:77
  35.5 0.3 fusion
  35.9 0.8 %copy.26 = bf16[512,256]{1,0:T(8,128)(2,1)} copy(bf16[512,256]{0,1:T(8,128)(2,1)S(1)} %fusion) | data formatting | bytes 524288 | tf_op jit(solution)/shard_map/convert_element_type | solution.py:84
  36.7 4.3 %all-to-all-start.1 = ((bf16[16,32,256]{2,1,0:T(8,128)(2,1)}), bf16[16,32,256]{2,1,0:T(8,128)(2,1)S(1)}, u32[]{:S(2)}, u32[]{:S(2)}) async-start(bf16[16,32,256]{2,1,0:T(8,128)(2,1)} %bitcast.15), calls=%async_computation.1 | async-start | bytes 524288 | tf_op jit(solution)/shard_map/all_to_all | solution.py:86
  41.0 0.7 %collective-permute-start.2 = (bf16[256,256]{1,0:T(8,128)(2,1)S(1)}, bf16[256,256]{1,0:T(8,128)(2,1)S(1)}, u32[]{:S(2)}, u32[]{:S(2)}) collective-permute-start(bf16[256,256]{1,0:T(8,128)(2,1)S(1)} %get-tuple-element.4), channel_id=1, source_target_pairs={{0,0},{1,2},{2,1},{3,3},{4,4},{5,6},{6,5},{7,7},{8,8},{9,10},{10,9... | collective-permute-start | bytes 393224 | tf_op jit(solution)/shard_map/ppermute | solution.py:85
  41.7 9.5 %all-to-all-done.1 = bf16[16,32,256]{2,1,0:T(8,128)(2,1)S(1)} async-done(((bf16[16,32,256]{2,1,0:T(8,128)(2,1)}), bf16[16,32,256]{2,1,0:T(8,128)(2,1)S(1)}, u32[]{:S(2)}, u32[]{:S(2)}) %all-to-all-start.1) | async-done | bytes 262176 | tf_op jit(solution)/shard_map/all_to_all | solution.py:86
  51.2 0.7 %convert_reduce_fusion = f32[32,256]{1,0:T(8,128)} fusion(bf16[16,32,256]{2,1,0:T(8,128)(2,1)S(1)} %all-to-all-done.1), kind=kLoop, calls=%fused_computation.4 | loop fusion | flops 253952 | bytes 294912 | tf_op jit(solution)/shard_map/reduce_sum | solution.py:87
  51.9 0.7 %copy.39 = bf16[256,256]{1,0:T(8,128)(2,1)} copy(bf16[256,256]{1,0:T(8,128)(2,1)S(1)} %collective-permute-done.2) | data formatting | bytes 262144
  (18 shorter events, 0.1 us)
Async XLA Ops:
  0.6 14.5 %copy-start = (bf16[1024,256]{1,0:T(8,128)(2,1)S(1)}, bf16[1024,256]{1,0:T(8,128)(2,1)}, u32[]{:S(2)}) copy-start(bf16[1024,256]{1,0:T(8,128)(2,1)} %param.9) | copy-start | bytes 1572868
  2.6 10.9 %copy-start.1 = (bf16[1,1,8,128,128]{4,3,2,1,0:T(8,128)(2,1)S(1)}, bf16[1,1,8,128,128]{4,3,2,1,0:T(8,128)(2,1)}, u32[]{:S(2)}) copy-start(bf16[1,1,8,128,128]{4,3,2,1,0:T(8,128)(2,1)} %param.14) | copy-start | bytes 786436
  2.6 23.6 %all-to-all-start = ((bf16[64,16,256]{2,0,1:T(8,128)(2,1)}), bf16[64,16,256]{2,0,1:T(8,128)(2,1)S(1)}, u32[]{:S(2)}, u32[]{:S(2)}) async-start(bf16[64,16,256]{2,0,1:T(8,128)(2,1)} %bitcast.38), calls=%async_computation | async-start | bytes 1048576 | tf_op jit(solution)/shard_map/all_to_all | solution.py:52
  11.7 0.7 %copy-start.4 = (s32[1,1,8]{2,1,0:T(1,128)S(1)}, s32[1,1,8]{2,1,0:T(1,128)}, u32[]{:S(2)}) copy-start(s32[1,1,8]{2,1,0:T(1,128)} %param.11) | copy-start | bytes 100
  11.7 0.7 %copy-start.5 = (s32[1,1,8]{2,1,0:T(1,128)S(1)}, s32[1,1,8]{2,1,0:T(1,128)}, u32[]{:S(2)}) copy-start(s32[1,1,8]{2,1,0:T(1,128)} %param.10) | copy-start | bytes 100
  12.6 0.7 %copy-start.2 = (s32[1,1,8]{2,1,0:T(1,128)S(1)}, s32[1,1,8]{2,1,0:T(1,128)}, u32[]{:S(2)}) copy-start(s32[1,1,8]{2,1,0:T(1,128)} %param.12) | copy-start | bytes 100
  14.4 14.0 %collective-permute-start.1 = (bf16[256,512]{1,0:T(8,128)(2,1)S(1)}, bf16[256,512]{1,0:T(8,128)(2,1)S(1)}, u32[]{:S(2)}, u32[]{:S(2)}) collective-permute-start(bf16[256,512]{1,0:T(8,128)(2,1)S(1)} %bitcast.51), channel_id=1, source_target_pairs={{0,0},{1,2},{2,1},{3,3},{4,4},{5,6},{6,5},{7,7},{8,8},{9,10},{10,9... | collective-permute-start | bytes 786440 | tf_op jit(solution)/shard_map/ppermute | solution.py:59
  26.8 0.9 %copy-start.3 = (bf16[256,256]{1,0:T(8,128)(2,1)S(1)}, bf16[256,256]{1,0:T(8,128)(2,1)}, u32[]{:S(2)}) copy-start(bf16[256,256]{1,0:T(8,128)(2,1)} %param.15) | copy-start | bytes 393220
  27.2 1.6 %collective-permute-start = (bf16[256,512]{1,0:T(8,128)(2,1)S(1)}, bf16[256,512]{1,0:T(8,128)(2,1)S(1)}, u32[]{:S(2)}, u32[]{:S(2)}) collective-permute-start(bf16[256,512]{1,0:T(8,128)(2,1)S(1)} %get-tuple-element.2), channel_id=1, source_target_pairs={{0,2},{2,0},{1,3},{3,1},{4,6},{6,4},{5,7},{7,5},{8,10},{10,8},{9,1... | collective-permute-start | bytes 786440 | tf_op jit(solution)/shard_map/ppermute | solution.py:67
  27.7 1.3 %collective-permute-start.3 = (bf16[256,256]{1,0:T(8,128)(2,1)S(1)}, bf16[256,256]{1,0:T(8,128)(2,1)S(1)}, u32[]{:S(2)}, u32[]{:S(2)}) collective-permute-start(bf16[256,256]{1,0:T(8,128)(2,1)S(1)} %copy-done.3), channel_id=1, source_target_pairs={{0,0},{1,2},{2,1},{3,3},{4,4},{5,6},{6,5},{7,7},{8,8},{9,10},{10,9... | collective-permute-start | bytes 393224 | tf_op jit(solution)/shard_map/ppermute | solution.py:60
  29.4 6.2 %collective-permute-start.4 = (bf16[256,512]{1,0:T(8,128)(2,1)S(1)}, bf16[256,512]{1,0:T(8,128)(2,1)S(1)}, u32[]{:S(2)}, u32[]{:S(2)}) collective-permute-start(bf16[256,512]{1,0:T(8,128)(2,1)S(1)} %get-tuple-element.6), channel_id=1, source_target_pairs={{0,2},{2,0},{1,3},{3,1},{4,6},{6,4},{5,7},{7,5},{8,10},{10,8},{9,1... | collective-permute-start | bytes 786440 | tf_op jit(solution)/shard_map/ppermute | solution.py:77
  36.7 14.5 %all-to-all-start.1 = ((bf16[16,32,256]{2,1,0:T(8,128)(2,1)}), bf16[16,32,256]{2,1,0:T(8,128)(2,1)S(1)}, u32[]{:S(2)}, u32[]{:S(2)}) async-start(bf16[16,32,256]{2,1,0:T(8,128)(2,1)} %bitcast.15), calls=%async_computation.1 | async-start | bytes 524288 | tf_op jit(solution)/shard_map/all_to_all | solution.py:86
  41.0 0.7 %collective-permute-start.2 = (bf16[256,256]{1,0:T(8,128)(2,1)S(1)}, bf16[256,256]{1,0:T(8,128)(2,1)S(1)}, u32[]{:S(2)}, u32[]{:S(2)}) collective-permute-start(bf16[256,256]{1,0:T(8,128)(2,1)S(1)} %get-tuple-element.4), channel_id=1, source_target_pairs={{0,0},{1,2},{2,1},{3,3},{4,4},{5,6},{6,5},{7,7},{8,8},{9,10},{10,9... | collective-permute-start | bytes 393224 | tf_op jit(solution)/shard_map/ppermute | solution.py:85

commit v2 on v1

v2 whole, which is shorter than its diff:
```python
import functools

import jax
import jax.numpy as jnp
from jax import lax
from jax.experimental import pallas as pl
from jax.experimental.pallas import tpu as pltpu
from jax.sharding import Mesh, PartitionSpec as P

root_half = 0.7071067811865476
inv_root_two_pi = 0.3989422804014327

SWAP = ((0, 1), (1, 0))
TRANSPOSE = ((0, 0), (1, 2), (2, 1), (3, 3))
VMEM = pl.BlockSpec(memory_space=pltpu.VMEM)
SMEM = pl.BlockSpec(memory_space=pltpu.SMEM)
ANY = pl.BlockSpec(memory_space=pl.ANY)
PARAMS = pltpu.CompilerParams(vmem_limit_bytes=24 * 1024 * 1024)


def dot(left, right, left_dim, right_dim):
    return lax.dot_general(
        left, right, (((left_dim,), (right_dim,)), ((), ())), preferred_element_type=jnp.float32
    )


def chunk_kernel(feats, chunks, sems):
    count, _, rows = chunks.shape
    copies = [
        pltpu.make_async_copy(feats.at[:, pl.ds(at * rows, rows)], chunks.at[at], sems.at[at])
        for at in range(count)
    ]
    for copy in copies:
        copy.start()
    for copy in copies:
        copy.wait()


def by_destination(feats, count):
    width, nodes = feats.shape
    return pl.pallas_call(
        chunk_kernel,
        out_shape=jax.ShapeDtypeStruct((count, width, nodes // count), feats.dtype),
        in_specs=[ANY],
        out_specs=ANY,
        scratch_shapes=[pltpu.SemaphoreType.DMA((count,))],
        compiler_params=PARAMS,
        name="by_destination",
    )(feats)


def adjacency_kernel(row_tile, col_tile, block_index, live, blocks, out):
    slots, tile, _ = blocks.shape
    for slot in range(slots):
        row = pl.multiple_of(row_tile[slot] * tile, tile)
        col = pl.multiple_of(col_tile[slot] * tile, tile)
        block = blocks[block_index[slot]]
        out[pl.ds(row, tile), pl.ds(col, tile)] = jnp.where(
            slot < live[0], block, jnp.zeros_like(block)
        )


def dense_adjacency(row_tile, col_tile, block_index, live, blocks, rows):
    slots, tile, _ = blocks.shape
    return pl.pallas_call(
        adjacency_kernel,
        out_shape=jax.ShapeDtypeStruct((rows, slots * tile * tile // rows), blocks.dtype),
        in_specs=[SMEM, SMEM, SMEM, SMEM, VMEM],
        out_specs=VMEM,
        compiler_params=PARAMS,
        name="dense_adjacency",
    )(row_tile, col_tile, block_index, live, blocks)


def project_kernel(weight, arrived, part, part_out):
    columns, places, width, rows = arrived.shape
    for place in range(places):
        nodes = arrived[:, place].reshape(columns * width, rows)
        value = dot(weight[...], nodes, 1, 0)
        part[:, place * rows : (place + 1) * rows] = value
        part_out[:, place * rows : (place + 1) * rows] = value.astype(part_out.dtype)


def project(weight, arrived):
    hidden = weight.shape[0]
    columns, places, width, rows = arrived.shape
    shape = (hidden, places * rows)
    return pl.pallas_call(
        project_kernel,
        out_shape=(
            jax.ShapeDtypeStruct(shape, jnp.float32),
            jax.ShapeDtypeStruct(shape, jnp.bfloat16),
        ),
        in_specs=[VMEM, VMEM],
        out_specs=(VMEM, VMEM),
        compiler_params=PARAMS,
        name="project",
    )(weight, arrived)


def block_kernel(*refs):
    *projected, adjacency, cotangent, act, terms, terms_out = refs
    if len(projected) == 2:
        part, other = projected
        nodes = (part[...] + other[...].astype(jnp.float32)).astype(jnp.bfloat16)
    else:
        nodes = projected[0][...]
    preact = dot(nodes, adjacency[...], 1, 1)
    normal_cdf = 0.5 * (1.0 + lax.erf(preact * root_half))
    normal_pdf = jnp.exp(-0.5 * preact * preact) * inv_root_two_pi
    act[...] = (preact * normal_cdf).astype(act.dtype)
    derivative = normal_cdf + preact * normal_pdf
    pre_grad = (cotangent[...].astype(jnp.float32) * derivative).astype(jnp.bfloat16)
    value = dot(pre_grad, adjacency[...], 1, 0)
    terms[...] = value
    terms_out[...] = value.astype(terms_out.dtype)


def block(projected, adjacency, cotangent):
    hidden, rows = cotangent.shape
    shape = (hidden, adjacency.shape[1])
    return pl.pallas_call(
        block_kernel,
        out_shape=(
            jax.ShapeDtypeStruct((hidden, rows), jnp.bfloat16),
            jax.ShapeDtypeStruct(shape, jnp.float32),
            jax.ShapeDtypeStruct(shape, jnp.bfloat16),
        ),
        in_specs=[VMEM] * (len(projected) + 2),
        out_specs=(VMEM,) * 3,
        compiler_params=PARAMS,
        name="block",
    )(*projected, adjacency, cotangent)


def gradient_kernel(arrived, part, other, terms):
    columns, places, width, rows = arrived.shape
    node_grad = (part[...] + other[...].astype(jnp.float32)).astype(jnp.bfloat16)
    total = None
    for place in range(places):
        nodes = arrived[:, place].reshape(columns * width, rows)
        value = dot(nodes, node_grad[:, place * rows : (place + 1) * rows], 1, 1)
        total = value if total is None else total + value
    terms[...] = total.astype(terms.dtype)


def gradient(arrived, part, other, dtype):
    columns, places, width, rows = arrived.shape
    return pl.pallas_call(
        gradient_kernel,
        out_shape=jax.ShapeDtypeStruct((columns * width, part.shape[0]), dtype),
        in_specs=[VMEM] * 3,
        out_specs=VMEM,
        compiler_params=PARAMS,
        name="gradient",
    )(arrived, part, other)


def per_device(feats, weight, tile_row, tile_col, tile_block, tile_count, edge_blocks, cotangent):
    columns = lax.axis_size("col")
    pairs = lax.axis_size("hi")
    core = lax.axis_index("core")
    width, shard_nodes = feats.shape
    rows = shard_nodes // (2 * columns)
    hidden = weight.shape[1]
    bf16 = jnp.bfloat16

    chunks = by_destination(feats, 2 * columns)
    arrived = lax.all_to_all(chunks, ("col", "lo"), split_axis=0, concat_axis=0, tiled=True)
    arrived = arrived.reshape(columns, 2, width, rows)

    cot = lax.ppermute(cotangent, ("core", "lo"), TRANSPOSE)
    adjacency = dense_adjacency(
        tile_row[0, 0], tile_col[0, 0], tile_block[0, 0], tile_count[0], edge_blocks[0, 0], rows
    )
    adjacency = lax.ppermute(adjacency, ("core", "lo"), TRANSPOSE)
    own_weight = lax.dynamic_index_in_dim(
        weight.reshape(columns, 2, width, hidden), core, 1, keepdims=False
    ).reshape(columns * width, hidden).T
    arrived, cot, adjacency, own_weight = lax.optimization_barrier(
        (arrived, cot, adjacency, own_weight)
    )

    part, sent = project(own_weight, arrived)
    other = lax.ppermute(sent, "core", SWAP)
    projected = (part, other)
    if pairs > 1:
        total = (part + other.astype(jnp.float32)).astype(bf16)
        projected = (lax.all_gather(total, "hi", axis=1, tiled=True),)
    output, part, sent = block(projected, adjacency, cot)
    if pairs > 1:
        part = lax.psum_scatter(part, "hi", scatter_dimension=1, tiled=True)
        sent = part.astype(bf16)
    other = lax.ppermute(sent, "core", SWAP)
    terms = gradient(arrived, part, other, jnp.float32 if pairs > 1 else bf16)
    share = width // (2 * pairs)
    if pairs > 1:
        terms = terms.reshape(columns, pairs, 2 * share, hidden)
        terms = lax.psum_scatter(terms, "hi", scatter_dimension=1, tiled=True).astype(bf16)
    terms = terms.reshape(2 * columns, share, hidden)
    act = lax.ppermute(output, ("core", "lo"), TRANSPOSE)
    terms = lax.all_to_all(terms, ("col", "lo"), split_axis=0, concat_axis=0, tiled=True)
    weight_grad = jnp.sum(terms.astype(jnp.float32), axis=0)
    return (act, weight_grad)


def solution(mesh):
    n_feat, n_node = mesh.shape["feat"], mesh.shape["node"]
    fine = Mesh(
        mesh.devices.reshape(n_feat // 2, 2, n_node // 2, 2), ("col", "core", "hi", "lo")
    )
    feat, node = ("col", "core"), ("hi", "lo")
    return jax.shard_map(
        per_device,
        mesh=fine,
        in_specs=(
            P(feat, node),
            P(),
            P(feat, node, None),
            P(feat, node, None),
            P(feat, node, None),
            P(feat, node),
            P(feat, node, None, None, None),
            P(None, node + feat),
        ),
        out_specs=(P(None, node + feat), P(feat + node, None)),
        check_vma=False,
    )
```

time: 52.9 us -> 48.8 us (0.922)
  local copies, waits for them, and re-layouts: 6.71 us -> 2.59 us
  starting transfers between devices: 19.8 us -> 16.2 us
  Pallas kernels: 0 us -> 3.46 us
  waiting for transfers between devices: 22.1 us -> 24 us
  matrix products: 1.23 us -> 0 us
    ppermute x3, starting transfers between devices: 5.75 us -> 0.94 us  [the longest x1 0.67 us: per_device(): act = lax.ppermute(output, ('core', 'lo'), TRANSPOSE)]
    pallas_call x0 -> x5, Pallas kernels: none -> 3.46 us  [the longest x1 1.03 us: gradient(): pl.pallas_call(gradient_kernel, out_shape=jax.ShapeDtypeStruct((columns *...]
    reshape x1, local copies, waits for them, and re-layouts: 1.95 us -> 0.14 us  [per_device(): own_weight = lax.dynamic_index_in_dim(weight.reshape(columns, 2, width, h...]
    ppermute x3, waiting for transfers between devices: 1.52 us -> 2.92 us  [the longest x2 2.92 us: per_device(): other = lax.ppermute(sent, 'core', SWAP)]
    dot_general x4 -> x0, matrix products: 1.23 us -> none  [dot(): lax.dot_general(left, right, (((left_dim,), (right_dim,)), ((), ())), pre...]
    all_to_all x1, starting transfers between devices: 4.31 us -> 5.49 us  [per_device(): lax.all_to_all(terms, ('col', 'lo'), split_axis=0, concat_axis=0, tiled=T...]
    convert_element_type x2 -> x0, local copies, waits for them, and re-layouts: 0.92 us -> none  [the longest x1 0.84 us: per_device(): terms = terms.astype(bf16).reshape(2 * columns, share, hidden)]
    gather x1 -> x0, local copies, waits for them, and re-layouts: 0.6 us -> none  [dense_adjacency(): jnp.take(blocks, chosen, axis=0)]
  transfers between devices with their start and end apart: 7 -> 7, of which waited for: 4 -> 4; matrix products, arithmetic and copies ran while one was open for 5% -> 0% of each run, Pallas kernels for 0% -> 1%
where the time goes in v2:
time: 48.8 us; the launch traced here: 48.4 us
  waiting for transfers between devices  24 us (49%)
  starting transfers between devices  16.2 us (33%)
  Pallas kernels  3.46 us (7%)
  local copies, waits for them, and re-layouts  2.59 us (5%)
  between operations  1.48 us (3%)
  other arithmetic  0.66 us (1%)
    all_to_all x1, waiting for transfers between devices, per_device(): lax.all_to_all(chunks, ('col', 'lo'), split_axis=0, concat_axis=0, tiled=...  11.6 us
    all_to_all x1, waiting for transfers between devices, per_device(): lax.all_to_all(terms, ('col', 'lo'), split_axis=0, concat_axis=0, tiled=T...  9.49 us
    all_to_all x1, starting transfers between devices, per_device(): lax.all_to_all(chunks, ('col', 'lo'), split_axis=0, concat_axis=0, tiled=...  8.46 us
    all_to_all x1, starting transfers between devices, per_device(): lax.all_to_all(terms, ('col', 'lo'), split_axis=0, concat_axis=0, tiled=T...  5.49 us
    ppermute x2, waiting for transfers between devices, per_device(): other = lax.ppermute(sent, 'core', SWAP)  2.92 us
    unnamed x15, local copies, waits for them, and re-layouts  2.42 us
    pallas_call x1, Pallas kernels, gradient(): pl.pallas_call(gradient_kernel, out_shape=jax.ShapeDtypeStruct((columns *...  1.03 us
  transfers between devices with their start and end apart: 7, of which 4 were waited for; matrix products, arithmetic and copies ran while one was open for 0% of the time, Pallas kernels for 1%

profile of v2, /device:TPU:0, one launch (start us, length us, event | category | flops | bytes accessed | tf_op | source)
XLA Modules:
  0.0 48.4 jit_solution(7572280803667869787)
XLA Ops:
  0.6 0.0 copy-start
  0.6 0.0 copy-start.1
  0.7 1.1 %copy-done.1 = bf16[64,4096]{1,0:T(8,128)(2,1)S(1)} copy-done((bf16[64,4096]{1,0:T(8,128)(2,1)S(1)}, bf16[64,4096]{1,0:T(8,128)(2,1)}, u32[]{:S(2)}) %copy-start.1) | copy-done | bytes 524312
  1.7 0.9 %by_destination.1 = bf16[16,64,256]{2,1,0:T(8,128)(2,1)} custom-call(bf16[64,4096]{1,0:T(8,128)(2,1)S(1)} %copy-done.1), custom_call_target="tpu_custom_call" | custom-call | tf_op jit(solution)/shard_map/by_destination/pallas_call | solution.py:41
  2.7 0.0 copy-start.2
  2.7 8.5 %all-to-all-start = ((bf16[16,64,256]{2,1,0:T(8,128)(2,1)}), bf16[16,64,256]{2,1,0:T(8,128)(2,1)S(1)}, u32[]{:S(2)}, u32[]{:S(2)}) async-start(bf16[16,64,256]{2,1,0:T(8,128)(2,1)} %by_destination.1), calls=%async_computation | async-start | bytes 1048576 | tf_op jit(solution)/shard_map/all_to_all | solution.py:169
  11.8 0.0 copy-start.3
  11.8 0.0 copy-start.4
  11.8 0.0 copy-start.5
  11.9 0.6 %copy-done.3 = s32[1,1,8]{2,1,0:T(1,128)S(1)} copy-done((s32[1,1,8]{2,1,0:T(1,128)S(1)}, s32[1,1,8]{2,1,0:T(1,128)}, u32[]{:S(2)}) %copy-start.3) | copy-done | bytes 56
  12.5 0.0 copy-done.4
  12.5 0.0 copy-done.5
  12.5 0.6 %dense_adjacency.1 = bf16[256,512]{1,0:T(8,128)(2,1)S(1)} custom-call(s32[8]{0:T(128)S(1)} %bitcast.16, s32[8]{0:T(128)S(1)} %bitcast.17, s32[8]{0:T(128)S(1)} %bitcast.18, s32[1]{0:T(128)} %bitcast.10.live, bf16[8,128,128]{2,1,0:T(8,128)(2,1)S(1)} %bitcast.15), custom_call_target="tpu_custom_call" | custom-call | tf_op jit(solution)/shard_map/dense_adjacency/pallas_call | solution.py:65
  13.1 0.7 %collective-permute-start.1 = (bf16[256,512]{1,0:T(8,128)(2,1)S(1)}, bf16[256,512]{1,0:T(8,128)(2,1)S(1)}, u32[]{:S(2)}, u32[]{:S(2)}) collective-permute-start(bf16[256,512]{1,0:T(8,128)(2,1)S(1)} %dense_adjacency.1), channel_id=1, source_target_pairs={{0,0},{1,2},{2,1},{3,3},{4,4},{5,6},{6,5},{7,7},{8,8},{9,10},{10,9... | collective-permute-start | bytes 786440 | tf_op jit(solution)/shard_map/ppermute | solution.py:176
  13.8 0.7 %collective-permute-start = (bf16[256,256]{1,0:T(8,128)(2,1)S(1)}, bf16[256,256]{1,0:T(8,128)(2,1)S(1)}, u32[]{:S(2)}, u32[]{:S(2)}) collective-permute-start(bf16[256,256]{1,0:T(8,128)(2,1)S(1)} %copy-done.6), channel_id=1, source_target_pairs={{0,0},{1,2},{2,1},{3,3},{4,4},{5,6},{6,5},{7,7},{8,8},{9,10},{10,9... | collective-permute-start | bytes 393224 | tf_op jit(solution)/shard_map/ppermute | solution.py:172
  14.6 0.1 copy.12
  14.7 0.0 collective-permute-done.refs_3_
  14.7 0.0 collective-permute-done.1.refs_2_
  14.7 11.6 %all-to-all-done = bf16[16,64,256]{2,1,0:T(8,128)(2,1)S(1)} async-done(((bf16[16,64,256]{2,1,0:T(8,128)(2,1)}), bf16[16,64,256]{2,1,0:T(8,128)(2,1)S(1)}, u32[]{:S(2)}, u32[]{:S(2)}) %all-to-all-start) | async-done | bytes 524320 | tf_op jit(solution)/shard_map/all_to_all | solution.py:169
  26.3 0.3 project.1
  26.6 0.1 collective-permute-start.2
  26.7 1.5 %collective-permute-done.2.refs_1_ = bf16[256,512]{1,0:T(8,128)(2,1)S(1)} collective-permute-done((bf16[256,512]{1,0:T(8,128)(2,1)S(1)}, bf16[256,512]{1,0:T(8,128)(2,1)S(1)}, u32[]{:S(2)}, u32[]{:S(2)}) %collective-permute-start.2) | collective-permute-done | bytes 262176 | tf_op jit(solution)/shard_map/ppermute | solution.py:185
  28.2 0.6 %block.1 = (bf16[256,256]{1,0:T(8,128)(2,1)S(1)}, f32[256,512]{1,0:T(8,128)S(1)}, bf16[256,512]{1,0:T(8,128)(2,1)S(1)}) custom-call(f32[256,512]{1,0:T(8,128)S(1)} %get-tuple-element.13.refs_0_, bf16[256,512]{1,0:T(8,128)(2,1)S(1)} %collective-permute-done.2.refs_1_, bf16[256,512]{1,0:T(8,128)(2,1)S(1)} %collective-permute-done.1.refs_2_, ...), custom_call_target="tpu_custom_call" | custom-call | tf_op jit(solution)/shard_map/block/pallas_call | solution.py:122
  28.8 0.2 collective-permute-start.4
  29.0 1.4 %collective-permute-done.4.other = bf16[256,512]{1,0:T(8,128)(2,1)S(1)} collective-permute-done((bf16[256,512]{1,0:T(8,128)(2,1)S(1)}, bf16[256,512]{1,0:T(8,128)(2,1)S(1)}, u32[]{:S(2)}, u32[]{:S(2)}) %collective-permute-start.4) | collective-permute-done | bytes 262176 | tf_op jit(solution)/shard_map/ppermute | solution.py:194
  30.4 1.0 %gradient.1 = bf16[512,256]{1,0:T(8,128)(2,1)} custom-call(bf16[8,2,64,256]{3,2,1,0:T(8,128)(2,1)S(1)} %bitcast.13, f32[256,512]{1,0:T(8,128)S(1)} %get-tuple-element.18.part, bf16[256,512]{1,0:T(8,128)(2,1)S(1)} %collective-permute-done.4.other), custom_call_target="tpu_custom_call" | custom-call | tf_op jit(solution)/shard_map/gradient/pallas_call | solution.py:149
  31.4 5.5 %all-to-all-start.1 = ((bf16[16,32,256]{2,1,0:T(8,128)(2,1)}), bf16[16,32,256]{2,1,0:T(8,128)(2,1)S(1)}, u32[]{:S(2)}, u32[]{:S(2)}) async-start(bf16[16,32,256]{2,1,0:T(8,128)(2,1)} %bitcast.9), calls=%async_computation.1 | async-start | bytes 524288 | tf_op jit(solution)/shard_map/all_to_all | solution.py:202
  36.9 0.7 %collective-permute-start.3 = (bf16[256,256]{1,0:T(8,128)(2,1)S(1)}, bf16[256,256]{1,0:T(8,128)(2,1)S(1)}, u32[]{:S(2)}, u32[]{:S(2)}) collective-permute-start(bf16[256,256]{1,0:T(8,128)(2,1)S(1)} %get-tuple-element.17), channel_id=1, source_target_pairs={{0,0},{1,2},{2,1},{3,3},{4,4},{5,6},{6,5},{7,7},{8,8},{9,10},{10,9... | collective-permute-start | bytes 393224 | tf_op jit(solution)/shard_map/ppermute | solution.py:201
  37.6 0.0 collective-permute-done.3
  37.6 9.5 %all-to-all-done.1 = bf16[16,32,256]{2,1,0:T(8,128)(2,1)S(1)} async-done(((bf16[16,32,256]{2,1,0:T(8,128)(2,1)}), bf16[16,32,256]{2,1,0:T(8,128)(2,1)S(1)}, u32[]{:S(2)}, u32[]{:S(2)}) %all-to-all-start.1) | async-done | bytes 262176 | tf_op jit(solution)/shard_map/all_to_all | solution.py:202
  47.1 0.7 %convert_reduce_fusion = f32[32,256]{1,0:T(8,128)} fusion(bf16[16,32,256]{2,1,0:T(8,128)(2,1)S(1)} %all-to-all-done.1), kind=kLoop, calls=%fused_computation | loop fusion | flops 253952 | bytes 294912 | tf_op jit(solution)/shard_map/reduce_sum | solution.py:203
  47.8 0.7 %copy.15 = bf16[256,256]{1,0:T(8,128)(2,1)} copy(bf16[256,256]{1,0:T(8,128)(2,1)S(1)} %collective-permute-done.3) | data formatting | bytes 262144
  (5 shorter events, 0.0 us)
Async XLA Ops:
  0.6 13.9 %copy-start = (bf16[1024,256]{1,0:T(8,128)(2,1)S(1)}, bf16[1024,256]{1,0:T(8,128)(2,1)}, u32[]{:S(2)}) copy-start(bf16[1024,256]{1,0:T(8,128)(2,1)} %param.9) | copy-start | bytes 1572868
  0.6 1.1 %copy-start.1 = (bf16[64,4096]{1,0:T(8,128)(2,1)S(1)}, bf16[64,4096]{1,0:T(8,128)(2,1)}, u32[]{:S(2)}) copy-start(bf16[64,4096]{1,0:T(8,128)(2,1)} %feats.1) | copy-start | bytes 1572868
  2.7 9.2 %copy-start.2 = (bf16[1,1,8,128,128]{4,3,2,1,0:T(8,128)(2,1)S(1)}, bf16[1,1,8,128,128]{4,3,2,1,0:T(8,128)(2,1)}, u32[]{:S(2)}) copy-start(bf16[1,1,8,128,128]{4,3,2,1,0:T(8,128)(2,1)} %param.14) | copy-start | bytes 786436
  2.7 23.6 %all-to-all-start = ((bf16[16,64,256]{2,1,0:T(8,128)(2,1)}), bf16[16,64,256]{2,1,0:T(8,128)(2,1)S(1)}, u32[]{:S(2)}, u32[]{:S(2)}) async-start(bf16[16,64,256]{2,1,0:T(8,128)(2,1)} %by_destination.1), calls=%async_computation | async-start | bytes 1048576 | tf_op jit(solution)/shard_map/all_to_all | solution.py:169
  11.8 0.7 %copy-start.3 = (s32[1,1,8]{2,1,0:T(1,128)S(1)}, s32[1,1,8]{2,1,0:T(1,128)}, u32[]{:S(2)}) copy-start(s32[1,1,8]{2,1,0:T(1,128)} %param.10) | copy-start | bytes 100
  11.8 0.7 %copy-start.4 = (s32[1,1,8]{2,1,0:T(1,128)S(1)}, s32[1,1,8]{2,1,0:T(1,128)}, u32[]{:S(2)}) copy-start(s32[1,1,8]{2,1,0:T(1,128)} %param.11) | copy-start | bytes 100
  11.8 0.7 %copy-start.5 = (s32[1,1,8]{2,1,0:T(1,128)S(1)}, s32[1,1,8]{2,1,0:T(1,128)}, u32[]{:S(2)}) copy-start(s32[1,1,8]{2,1,0:T(1,128)} %param.12) | copy-start | bytes 100
  12.5 1.3 %copy-start.6 = (bf16[256,256]{1,0:T(8,128)(2,1)S(1)}, bf16[256,256]{1,0:T(8,128)(2,1)}, u32[]{:S(2)}) copy-start(bf16[256,256]{1,0:T(8,128)(2,1)} %param.15) | copy-start | bytes 393220
  13.1 1.6 %collective-permute-start.1 = (bf16[256,512]{1,0:T(8,128)(2,1)S(1)}, bf16[256,512]{1,0:T(8,128)(2,1)S(1)}, u32[]{:S(2)}, u32[]{:S(2)}) collective-permute-start(bf16[256,512]{1,0:T(8,128)(2,1)S(1)} %dense_adjacency.1), channel_id=1, source_target_pairs={{0,0},{1,2},{2,1},{3,3},{4,4},{5,6},{6,5},{7,7},{8,8},{9,10},{10,9... | collective-permute-start | bytes 786440 | tf_op jit(solution)/shard_map/ppermute | solution.py:176
  13.8 0.9 %collective-permute-start = (bf16[256,256]{1,0:T(8,128)(2,1)S(1)}, bf16[256,256]{1,0:T(8,128)(2,1)S(1)}, u32[]{:S(2)}, u32[]{:S(2)}) collective-permute-start(bf16[256,256]{1,0:T(8,128)(2,1)S(1)} %copy-done.6), channel_id=1, source_target_pairs={{0,0},{1,2},{2,1},{3,3},{4,4},{5,6},{6,5},{7,7},{8,8},{9,10},{10,9... | collective-permute-start | bytes 393224 | tf_op jit(solution)/shard_map/ppermute | solution.py:172
  26.6 1.6 %collective-permute-start.2 = (bf16[256,512]{1,0:T(8,128)(2,1)S(1)}, bf16[256,512]{1,0:T(8,128)(2,1)S(1)}, u32[]{:S(2)}, u32[]{:S(2)}) collective-permute-start(bf16[256,512]{1,0:T(8,128)(2,1)S(1)} %get-tuple-element.14), channel_id=1, source_target_pairs={{0,2},{2,0},{1,3},{3,1},{4,6},{6,4},{5,7},{7,5},{8,10},{10,8},{9,1... | collective-permute-start | bytes 786440 | tf_op jit(solution)/shard_map/ppermute | solution.py:185
  28.8 1.6 %collective-permute-start.4 = (bf16[256,512]{1,0:T(8,128)(2,1)S(1)}, bf16[256,512]{1,0:T(8,128)(2,1)S(1)}, u32[]{:S(2)}, u32[]{:S(2)}) collective-permute-start(bf16[256,512]{1,0:T(8,128)(2,1)S(1)} %get-tuple-element.19), channel_id=1, source_target_pairs={{0,2},{2,0},{1,3},{3,1},{4,6},{6,4},{5,7},{7,5},{8,10},{10,8},{9,1... | collective-permute-start | bytes 786440 | tf_op jit(solution)/shard_map/ppermute | solution.py:194
  31.4 15.7 %all-to-all-start.1 = ((bf16[16,32,256]{2,1,0:T(8,128)(2,1)}), bf16[16,32,256]{2,1,0:T(8,128)(2,1)S(1)}, u32[]{:S(2)}, u32[]{:S(2)}) async-start(bf16[16,32,256]{2,1,0:T(8,128)(2,1)} %bitcast.9), calls=%async_computation.1 | async-start | bytes 524288 | tf_op jit(solution)/shard_map/all_to_all | solution.py:202
  36.9 0.7 %collective-permute-start.3 = (bf16[256,256]{1,0:T(8,128)(2,1)S(1)}, bf16[256,256]{1,0:T(8,128)(2,1)S(1)}, u32[]{:S(2)}, u32[]{:S(2)}) collective-permute-start(bf16[256,256]{1,0:T(8,128)(2,1)S(1)} %get-tuple-element.17), channel_id=1, source_target_pairs={{0,0},{1,2},{2,1},{3,3},{4,4},{5,6},{6,5},{7,7},{8,8},{9,10},{10,9... | collective-permute-start | bytes 393224 | tf_op jit(solution)/shard_map/ppermute | solution.py:201

commit v3 on v2

v3 whole, which is shorter than its diff:
```python
import functools

import jax
import jax.numpy as jnp
from jax import lax
from jax.experimental import pallas as pl
from jax.experimental.pallas import tpu as pltpu
from jax.sharding import Mesh, PartitionSpec as P

root_half = 0.7071067811865476
inv_root_two_pi = 0.3989422804014327

SWAP = ((0, 1), (1, 0))
TRANSPOSE = ((0, 0), (1, 2), (2, 1), (3, 3))
VMEM = pl.BlockSpec(memory_space=pltpu.VMEM)
SMEM = pl.BlockSpec(memory_space=pltpu.SMEM)
ANY = pl.BlockSpec(memory_space=pl.ANY)
PARAMS = pltpu.CompilerParams(vmem_limit_bytes=24 * 1024 * 1024)


def dot(left, right, left_dim, right_dim):
    return lax.dot_general(
        left, right, (((left_dim,), (right_dim,)), ((), ())), preferred_element_type=jnp.float32
    )


def chunk_kernel(feats, chunks, held, in_sems, out_sems):
    places, columns, _, rows = chunks.shape
    spots = [(place, column) for column in range(columns) for place in range(places)]
    loads, stores = [], []
    for at, (place, column) in enumerate(spots):
        loads.append(
            pltpu.make_async_copy(
                feats.at[:, pl.ds(at * rows, rows)], held.at[place, column], in_sems.at[at]
            )
        )
        stores.append(
            pltpu.make_async_copy(held.at[place, column], chunks.at[place, column], out_sems.at[at])
        )
    for load in loads:
        load.start()
    for load, store in zip(loads, stores):
        load.wait()
        store.start()
    for store in stores:
        store.wait()


def by_destination(feats, places, columns):
    width, nodes = feats.shape
    shape = (places, columns, width, nodes // (places * columns))
    return pl.pallas_call(
        chunk_kernel,
        out_shape=jax.ShapeDtypeStruct(shape, feats.dtype),
        in_specs=[pl.BlockSpec(memory_space=pltpu.HBM)],
        out_specs=pl.BlockSpec(memory_space=pltpu.HBM),
        scratch_shapes=[
            pltpu.VMEM(shape, feats.dtype),
            pltpu.SemaphoreType.DMA((places * columns,)),
            pltpu.SemaphoreType.DMA((places * columns,)),
        ],
        compiler_params=pltpu.CompilerParams(vmem_limit_bytes=60 * 1024 * 1024),
        name="by_destination",
    )(feats)


def side_kernel(row_tile, col_tile, block_index, live, blocks, cotangent, out):
    slots, tile, _ = blocks.shape
    hidden, rows = cotangent.shape
    groups = out.shape[1] // rows
    part = hidden // groups
    for slot in range(slots):
        row = pl.multiple_of(row_tile[slot] * tile, tile)
        col = pl.multiple_of(col_tile[slot] * tile, tile)
        block = blocks[block_index[slot]]
        out[pl.ds(row, tile), pl.ds(col, tile)] = jnp.where(
            slot < live[0], block, jnp.zeros_like(block)
        )
    for group in range(groups):
        out[rows : rows + part, group * rows : (group + 1) * rows] = cotangent[
            group * part : (group + 1) * part, :
        ]


def side_inputs(row_tile, col_tile, block_index, live, blocks, cotangent):
    slots, tile, _ = blocks.shape
    hidden, rows = cotangent.shape
    cluster = slots * tile * tile // rows
    return pl.pallas_call(
        side_kernel,
        out_shape=jax.ShapeDtypeStruct((rows + hidden * rows // cluster, cluster), blocks.dtype),
        in_specs=[SMEM] * 4 + [VMEM] * 2,
        out_specs=VMEM,
        compiler_params=PARAMS,
        name="side_inputs",
    )(row_tile, col_tile, block_index, live, blocks, cotangent)


def project_kernel(weight, arrived, part, part_out):
    places, columns, width, rows = arrived.shape
    for place in range(places):
        nodes = arrived[place].reshape(columns * width, rows)
        value = dot(weight[...], nodes, 1, 0)
        part[:, place * rows : (place + 1) * rows] = value
        part_out[:, place * rows : (place + 1) * rows] = value.astype(part_out.dtype)


def project(weight, arrived):
    hidden = weight.shape[0]
    places, columns, width, rows = arrived.shape
    shape = (hidden, places * rows)
    return pl.pallas_call(
        project_kernel,
        out_shape=(
            jax.ShapeDtypeStruct(shape, jnp.float32),
            jax.ShapeDtypeStruct(shape, jnp.bfloat16),
        ),
        in_specs=[VMEM, VMEM],
        out_specs=(VMEM, VMEM),
        compiler_params=PARAMS,
        name="project",
    )(weight, arrived)


def block_kernel(*refs):
    *projected, side, act, terms, terms_out = refs
    hidden, rows = act.shape
    groups = side.shape[1] // rows
    part = hidden // groups
    if len(projected) == 2:
        nodes = (projected[0][...] + projected[1][...].astype(jnp.float32)).astype(jnp.bfloat16)
    else:
        nodes = projected[0][...]
    adjacency = side[:rows, :]
    preact = dot(nodes, adjacency, 1, 1)
    normal_cdf = 0.5 * (1.0 + lax.erf(preact * root_half))
    normal_pdf = jnp.exp(-0.5 * preact * preact) * inv_root_two_pi
    act[...] = (preact * normal_cdf).astype(act.dtype)
    derivative = normal_cdf + preact * normal_pdf
    cotangent = jnp.concatenate(
        [side[rows : rows + part, group * rows : (group + 1) * rows] for group in range(groups)], 0
    )
    pre_grad = (cotangent.astype(jnp.float32) * derivative).astype(jnp.bfloat16)
    value = dot(pre_grad, adjacency, 1, 0)
    terms[...] = value
    terms_out[...] = value.astype(terms_out.dtype)


def block(projected, side, rows):
    hidden, cluster = projected[0].shape
    return pl.pallas_call(
        block_kernel,
        out_shape=(
            jax.ShapeDtypeStruct((hidden, rows), jnp.bfloat16),
            jax.ShapeDtypeStruct((hidden, cluster), jnp.float32),
            jax.ShapeDtypeStruct((hidden, cluster), jnp.bfloat16),
        ),
        in_specs=[VMEM] * (len(projected) + 1),
        out_specs=(VMEM,) * 3,
        compiler_params=PARAMS,
        name="block",
    )(*projected, side)


def gradient_kernel(arrived, part, other, terms, held, sems):
    places, columns, width, rows = arrived.shape
    count = held.shape[0]
    size = columns // count
    node_grad = (part[...] + other[...].astype(jnp.float32)).astype(jnp.bfloat16)
    copies = []
    for group in range(count):
        total = None
        for place in range(places):
            nodes = arrived[place, group * size : (group + 1) * size].reshape(size * width, rows)
            value = dot(nodes, node_grad[:, place * rows : (place + 1) * rows], 1, 1)
            total = value if total is None else total + value
        if len(terms.shape) == 2:
            held[group] = total
            target = terms.at[pl.ds(group * size * width, size * width)]
        else:
            share = terms.shape[2]
            total = total.astype(terms.dtype).reshape(size, places, share, total.shape[1])
            for place in range(places):
                held[group, place] = total[:, place]
            target = terms.at[:, pl.ds(group * size, size)]
        copies.append(pltpu.make_async_copy(held.at[group], target, sems.at[group]))
        copies[-1].start()
    for copy in copies:
        copy.wait()


def gradient(arrived, part, other, shape, dtype):
    count = 2
    if len(shape) == 2:
        held = (count, shape[0] // count, shape[1])
    else:
        held = (count, shape[0], shape[1] // count) + shape[2:]
    return pl.pallas_call(
        gradient_kernel,
        out_shape=jax.ShapeDtypeStruct(shape, dtype),
        in_specs=[VMEM] * 3,
        out_specs=ANY,
        scratch_shapes=[pltpu.VMEM(held, dtype), pltpu.SemaphoreType.DMA((count,))],
        compiler_params=PARAMS,
        name="gradient",
    )(arrived, part, other)


def finish_kernel(terms, act, total_out, act_out, total, sems):
    act_copy = pltpu.make_async_copy(act, act_out, sems.at[0])
    act_copy.start()
    total[...] = jnp.sum(terms[...].astype(jnp.float32), axis=0)
    total_copy = pltpu.make_async_copy(total, total_out, sems.at[1])
    total_copy.start()
    act_copy.wait()
    total_copy.wait()


def finish(terms, act):
    return pl.pallas_call(
        finish_kernel,
        out_shape=(
            jax.ShapeDtypeStruct(terms.shape[1:], jnp.float32),
            jax.ShapeDtypeStruct(act.shape, act.dtype),
        ),
        in_specs=[VMEM, ANY],
        out_specs=(ANY, ANY),
        scratch_shapes=[
            pltpu.VMEM(terms.shape[1:], jnp.float32),
            pltpu.SemaphoreType.DMA((2,)),
        ],
        compiler_params=PARAMS,
        name="finish",
    )(terms, act)


def per_device(feats, weight, tile_row, tile_col, tile_block, tile_count, edge_blocks, cotangent):
    columns = lax.axis_size("col")
    pairs = lax.axis_size("hi")
    core = lax.axis_index("core")
    width, shard_nodes = feats.shape
    rows = shard_nodes // (2 * columns)
    hidden = weight.shape[1]
    bf16 = jnp.bfloat16

    chunks = by_destination(feats, 2, columns).reshape(2 * columns, width, rows)
    arrived = lax.all_to_all(chunks, ("lo", "col"), split_axis=0, concat_axis=0, tiled=True)
    arrived = arrived.reshape(2, columns, width, rows)

    side = side_inputs(
        tile_row[0, 0], tile_col[0, 0], tile_block[0, 0], tile_count[0], edge_blocks[0, 0], cotangent
    )
    side = lax.ppermute(side, ("core", "lo"), TRANSPOSE)
    own_weight = lax.dynamic_index_in_dim(
        weight.reshape(columns, 2, width, hidden), core, 1, keepdims=False
    ).reshape(columns * width, hidden).T
    arrived, side, own_weight = lax.optimization_barrier((arrived, side, own_weight))

    part, sent = project(own_weight, arrived)
    other = lax.ppermute(sent, "core", SWAP)
    projected = (part, other)
    if pairs > 1:
        total = (part + other.astype(jnp.float32)).astype(bf16)
        projected = (lax.all_gather(total, "hi", axis=1, tiled=True),)
    output, part, sent = block(projected, side, rows)
    if pairs > 1:
        part = lax.psum_scatter(part, "hi", scatter_dimension=1, tiled=True)
        sent = part.astype(bf16)
    other = lax.ppermute(sent, "core", SWAP)
    act = lax.ppermute(output, ("core", "lo"), TRANSPOSE)
    share = width // (2 * pairs)
    if pairs > 1:
        terms = gradient(arrived, part, other, (columns * width, hidden), jnp.float32)
        terms = terms.reshape(columns, pairs, 2, share, hidden)
        terms = lax.psum_scatter(terms, "hi", scatter_dimension=1, tiled=True).astype(bf16)
        terms = terms[:, 0].transpose(1, 0, 2, 3)
    else:
        terms = gradient(arrived, part, other, (2, columns, share, hidden), bf16)
    terms = terms.reshape(2 * columns, share, hidden)
    terms = lax.all_to_all(terms, ("lo", "col"), split_axis=0, concat_axis=0, tiled=True)
    weight_grad, act = finish(terms, act)
    return (act, weight_grad)


def solution(mesh):
    n_feat, n_node = mesh.shape["feat"], mesh.shape["node"]
    fine = Mesh(
        mesh.devices.reshape(n_feat // 2, 2, n_node // 2, 2), ("col", "core", "hi", "lo")
    )
    feat, node = ("col", "core"), ("hi", "lo")
    return jax.shard_map(
        per_device,
        mesh=fine,
        in_specs=(
            P(feat, node),
            P(),
            P(feat, node, None),
            P(feat, node, None),
            P(feat, node, None),
            P(feat, node),
            P(feat, node, None, None, None),
            P(None, node + feat),
        ),
        out_specs=(P(None, node + feat), P(feat + node, None)),
        check_vma=False,
    )
```

time: 48.8 us -> 47.1 us (0.965)
  local copies, waits for them, and re-layouts: 2.59 us -> 0.83 us
  Pallas kernels: 3.46 us -> 5.18 us
  starting transfers between devices: 16.2 us -> 14.6 us
  waiting for transfers between devices: 24 us -> 24.7 us
  other arithmetic: 0.66 us -> 0 us
    unnamed x15 -> x12, local copies, waits for them, and re-layouts: 2.42 us -> 0.67 us
    pallas_call x3 -> x4, Pallas kernels: 2.59 us -> 4.31 us  [the longest x1 1.95 us: by_destination(): pl.pallas_call(chunk_kernel, out_shape=jax.ShapeDtypeStruct(shape, feats....]
    all_to_all x2, starting transfers between devices: 14 us -> 13 us  [the longest x1 8.46 us: per_device(): lax.all_to_all(chunks, ('lo', 'col'), split_axis=0, concat_axis=0, tiled=...]
    all_to_all x2, waiting for transfers between devices: 21.1 us -> 21.7 us  [the longest x1 12.3 us: per_device(): lax.all_to_all(chunks, ('lo', 'col'), split_axis=0, concat_axis=0, tiled=...]
    ppermute x2 -> x1, starting transfers between devices: 1.35 us -> 0.69 us  [per_device(): side = lax.ppermute(side, ('core', 'lo'), TRANSPOSE)]
    reduce_sum x1 -> x0, other arithmetic: 0.66 us -> none  [per_device(): weight_grad = jnp.sum(terms.astype(jnp.float32), axis=0)]
  transfers between devices with their start and end apart: 7 -> 6, of which waited for: 4 -> 4; matrix products, arithmetic and copies ran while one was open for 0% -> 0% of each run, Pallas kernels for 1% -> 1%
where the time goes in v3:
time: 47.1 us; the launch traced here: 46.7 us
  waiting for transfers between devices  24.7 us (52%)
  starting transfers between devices  14.6 us (31%)
  Pallas kernels  5.18 us (11%)
  between operations  1.47 us (3%)
  local copies, waits for them, and re-layouts  0.83 us (2%)
    all_to_all x1, waiting for transfers between devices, per_device(): lax.all_to_all(chunks, ('lo', 'col'), split_axis=0, concat_axis=0, tiled=...  12.3 us
    all_to_all x1, waiting for transfers between devices, per_device(): lax.all_to_all(terms, ('lo', 'col'), split_axis=0, concat_axis=0, tiled=T...  9.48 us
    all_to_all x1, starting transfers between devices, per_device(): lax.all_to_all(chunks, ('lo', 'col'), split_axis=0, concat_axis=0, tiled=...  8.46 us
    all_to_all x1, starting transfers between devices, per_device(): lax.all_to_all(terms, ('lo', 'col'), split_axis=0, concat_axis=0, tiled=T...  4.51 us
    ppermute x2, waiting for transfers between devices, per_device(): other = lax.ppermute(sent, 'core', SWAP)  2.92 us
    pallas_call x1, Pallas kernels, by_destination(): pl.pallas_call(chunk_kernel, out_shape=jax.ShapeDtypeStruct(shape, feats....  1.95 us
    pallas_call x1, Pallas kernels, gradient(): pl.pallas_call(gradient_kernel, out_shape=jax.ShapeDtypeStruct(shape, dty...  1.05 us
  transfers between devices with their start and end apart: 6, of which 4 were waited for; matrix products, arithmetic and copies ran while one was open for 0% of the time, Pallas kernels for 1%

profile of v3, /device:TPU:0, one launch (start us, length us, event | category | flops | bytes accessed | tf_op | source)
XLA Modules:
  0.0 46.7 jit_solution(6902799453895245776)
XLA Ops:
  0.6 0.0 copy-start
  0.6 1.9 %by_destination.1 = bf16[2,8,64,256]{3,2,1,0:T(8,128)(2,1)} custom-call(bf16[64,4096]{1,0:T(8,128)(2,1)} %feats.1), custom_call_target="tpu_custom_call" | custom-call | tf_op jit(solution)/shard_map/by_destination/pallas_call | solution.py:52
  2.6 0.0 copy-start.1
  2.6 0.0 copy-start.2
  2.6 8.5 %all-to-all-start = ((bf16[16,64,256]{2,1,0:T(8,128)(2,1)}), bf16[16,64,256]{2,1,0:T(8,128)(2,1)S(1)}, u32[]{:S(2)}, u32[]{:S(2)}) async-start(bf16[16,64,256]{2,1,0:T(8,128)(2,1)} %bitcast.20), calls=%async_computation | async-start | bytes 1048576 | tf_op jit(solution)/shard_map/all_to_all | solution.py:247
  11.7 0.0 copy-start.3
  11.7 0.0 copy-start.4
  11.8 0.0 copy-start.5
  11.8 0.0 copy-done.1
  11.8 0.0 copy-done.2
  11.8 0.6 %copy-done.3 = s32[1,1,8]{2,1,0:T(1,128)S(1)} copy-done((s32[1,1,8]{2,1,0:T(1,128)S(1)}, s32[1,1,8]{2,1,0:T(1,128)}, u32[]{:S(2)}) %copy-start.3) | copy-done | bytes 56
  12.4 0.0 copy-done.4
  12.4 0.0 copy-done.5
  12.4 0.6 %side_inputs.1 = bf16[384,512]{1,0:T(8,128)(2,1)S(1)} custom-call(s32[8]{0:T(128)S(1)} %bitcast.17, s32[8]{0:T(128)S(1)} %bitcast.18, s32[8]{0:T(128)S(1)} %bitcast.19, s32[1]{0:T(128)} %bitcast.11.live, bf16[8,128,128]{2,1,0:T(8,128)(2,1)S(1)} %bitcast.16, bf16[256,256]{1,0:T(8,128)(2,1)S(1)} %copy-done.2), custom_call_target="tpu_custom_call" | custom-call | tf_op jit(solution)/shard_map/side_inputs/pallas_call | solution.py:89
  13.1 0.7 %collective-permute-start = (bf16[384,512]{1,0:T(8,128)(2,1)S(1)}, bf16[384,512]{1,0:T(8,128)(2,1)S(1)}, u32[]{:S(2)}, u32[]{:S(2)}) collective-permute-start(bf16[384,512]{1,0:T(8,128)(2,1)S(1)} %side_inputs.1), channel_id=1, source_target_pairs={{0,0},{1,2},{2,1},{3,3},{4,4},{5,6},{6,5},{7,7},{8,8},{9,10},{10,9... | collective-permute-start | bytes 1179656 | tf_op jit(solution)/shard_map/ppermute | solution.py:253
  13.8 0.0 copy-done
  13.8 0.1 copy.12
  14.0 0.0 collective-permute-done.refs_2_
  14.0 12.3 %all-to-all-done = bf16[16,64,256]{2,1,0:T(8,128)(2,1)S(1)} async-done(((bf16[16,64,256]{2,1,0:T(8,128)(2,1)}), bf16[16,64,256]{2,1,0:T(8,128)(2,1)S(1)}, u32[]{:S(2)}, u32[]{:S(2)}) %all-to-all-start) | async-done | bytes 524320 | tf_op jit(solution)/shard_map/all_to_all | solution.py:247
  26.2 0.3 project.1
  26.5 0.1 collective-permute-start.1
  26.6 1.5 %collective-permute-done.1.refs_1_ = bf16[256,512]{1,0:T(8,128)(2,1)S(1)} collective-permute-done((bf16[256,512]{1,0:T(8,128)(2,1)S(1)}, bf16[256,512]{1,0:T(8,128)(2,1)S(1)}, u32[]{:S(2)}, u32[]{:S(2)}) %collective-permute-start.1) | collective-permute-done | bytes 262176 | tf_op jit(solution)/shard_map/ppermute | solution.py:260
  28.1 0.6 %block.1 = (bf16[256,256]{1,0:T(8,128)(2,1)S(1)}, f32[256,512]{1,0:T(8,128)S(1)}, bf16[256,512]{1,0:T(8,128)(2,1)S(1)}) custom-call(f32[256,512]{1,0:T(8,128)S(1)} %get-tuple-element.14.refs_0_, bf16[256,512]{1,0:T(8,128)(2,1)S(1)} %collective-permute-done.1.refs_1_, bf16[384,512]{1,0:T(8,128)(2,1)S(1)} %collective-permute-done.refs_2_), custom_call_target="tpu_custom_call" | custom-call | tf_op jit(solution)/shard_map/block/pallas_call | solution.py:151
  28.7 0.2 collective-permute-start.2
  28.9 1.4 %collective-permute-done.2.other = bf16[256,512]{1,0:T(8,128)(2,1)S(1)} collective-permute-done((bf16[256,512]{1,0:T(8,128)(2,1)S(1)}, bf16[256,512]{1,0:T(8,128)(2,1)S(1)}, u32[]{:S(2)}, u32[]{:S(2)}) %collective-permute-start.2) | collective-permute-done | bytes 262176 | tf_op jit(solution)/shard_map/ppermute | solution.py:269
  30.3 1.1 %gradient.1 = bf16[2,8,32,256]{3,2,1,0:T(8,128)(2,1)} custom-call(bf16[2,8,64,256]{3,2,1,0:T(8,128)(2,1)S(1)} %bitcast.14, f32[256,512]{1,0:T(8,128)S(1)} %get-tuple-element.17.part, bf16[256,512]{1,0:T(8,128)(2,1)S(1)} %collective-permute-done.2.other), custom_call_target="tpu_custom_call" | custom-call | tf_op jit(solution)/shard_map/gradient/pallas_call | solution.py:198
  31.4 4.5 %all-to-all-start.1 = ((bf16[16,32,256]{2,1,0:T(8,128)(2,1)}), bf16[16,32,256]{2,1,0:T(8,128)(2,1)S(1)}, u32[]{:S(2)}, u32[]{:S(2)}) async-start(bf16[16,32,256]{2,1,0:T(8,128)(2,1)} %bitcast.10), calls=%async_computation.1 | async-start | bytes 524288 | tf_op jit(solution)/shard_map/all_to_all | solution.py:280
  35.9 0.7 %collective-permute-start.3 = (bf16[256,256]{1,0:T(8,128)(2,1)S(1)}, bf16[256,256]{1,0:T(8,128)(2,1)S(1)}, u32[]{:S(2)}, u32[]{:S(2)}) collective-permute-start(bf16[256,256]{1,0:T(8,128)(2,1)S(1)} %get-tuple-element.19), channel_id=1, source_target_pairs={{0,0},{1,2},{2,1},{3,3},{4,4},{5,6},{6,5},{7,7},{8,8},{9,10},{10,9... | collective-permute-start | bytes 393224 | tf_op jit(solution)/shard_map/ppermute | solution.py:270
  36.6 0.0 collective-permute-done.3.act
  36.6 9.5 %all-to-all-done.1.terms = bf16[16,32,256]{2,1,0:T(8,128)(2,1)S(1)} async-done(((bf16[16,32,256]{2,1,0:T(8,128)(2,1)}), bf16[16,32,256]{2,1,0:T(8,128)(2,1)S(1)}, u32[]{:S(2)}, u32[]{:S(2)}) %all-to-all-start.1) | async-done | bytes 262176 | tf_op jit(solution)/shard_map/all_to_all | solution.py:280
  46.1 0.7 %finish.1 = (f32[32,256]{1,0:T(8,128)}, bf16[256,256]{1,0:T(8,128)(2,1)}) custom-call(bf16[16,32,256]{2,1,0:T(8,128)(2,1)S(1)} %all-to-all-done.1.terms, bf16[256,256]{1,0:T(8,128)(2,1)S(1)} %collective-permute-done.3.act), custom_call_target="tpu_custom_call" | custom-call | tf_op jit(solution)/shard_map/finish/pallas_call | solution.py:220
  (1 shorter events, 0.0 us)
Async XLA Ops:
  0.6 13.1 %copy-start = (bf16[1024,256]{1,0:T(8,128)(2,1)S(1)}, bf16[1024,256]{1,0:T(8,128)(2,1)}, u32[]{:S(2)}) copy-start(bf16[1024,256]{1,0:T(8,128)(2,1)} %param.9) | copy-start | bytes 1572868
  2.6 9.2 %copy-start.1 = (bf16[1,1,8,128,128]{4,3,2,1,0:T(8,128)(2,1)S(1)}, bf16[1,1,8,128,128]{4,3,2,1,0:T(8,128)(2,1)}, u32[]{:S(2)}) copy-start(bf16[1,1,8,128,128]{4,3,2,1,0:T(8,128)(2,1)} %param.14) | copy-start | bytes 786436
  2.6 9.2 %copy-start.2 = (bf16[256,256]{1,0:T(8,128)(2,1)S(1)}, bf16[256,256]{1,0:T(8,128)(2,1)}, u32[]{:S(2)}) copy-start(bf16[256,256]{1,0:T(8,128)(2,1)} %cotangent.1) | copy-start | bytes 393220
  2.6 23.6 %all-to-all-start = ((bf16[16,64,256]{2,1,0:T(8,128)(2,1)}), bf16[16,64,256]{2,1,0:T(8,128)(2,1)S(1)}, u32[]{:S(2)}, u32[]{:S(2)}) async-start(bf16[16,64,256]{2,1,0:T(8,128)(2,1)} %bitcast.20), calls=%async_computation | async-start | bytes 1048576 | tf_op jit(solution)/shard_map/all_to_all | solution.py:247
  11.7 0.7 %copy-start.3 = (s32[1,1,8]{2,1,0:T(1,128)S(1)}, s32[1,1,8]{2,1,0:T(1,128)}, u32[]{:S(2)}) copy-start(s32[1,1,8]{2,1,0:T(1,128)} %param.10) | copy-start | bytes 100
  11.7 0.7 %copy-start.4 = (s32[1,1,8]{2,1,0:T(1,128)S(1)}, s32[1,1,8]{2,1,0:T(1,128)}, u32[]{:S(2)}) copy-start(s32[1,1,8]{2,1,0:T(1,128)} %param.11) | copy-start | bytes 100
  11.8 0.7 %copy-start.5 = (s32[1,1,8]{2,1,0:T(1,128)S(1)}, s32[1,1,8]{2,1,0:T(1,128)}, u32[]{:S(2)}) copy-start(s32[1,1,8]{2,1,0:T(1,128)} %param.12) | copy-start | bytes 100
  13.1 0.9 %collective-permute-start = (bf16[384,512]{1,0:T(8,128)(2,1)S(1)}, bf16[384,512]{1,0:T(8,128)(2,1)S(1)}, u32[]{:S(2)}, u32[]{:S(2)}) collective-permute-start(bf16[384,512]{1,0:T(8,128)(2,1)S(1)} %side_inputs.1), channel_id=1, source_target_pairs={{0,0},{1,2},{2,1},{3,3},{4,4},{5,6},{6,5},{7,7},{8,8},{9,10},{10,9... | collective-permute-start | bytes 1179656 | tf_op jit(solution)/shard_map/ppermute | solution.py:253
  26.5 1.6 %collective-permute-start.1 = (bf16[256,512]{1,0:T(8,128)(2,1)S(1)}, bf16[256,512]{1,0:T(8,128)(2,1)S(1)}, u32[]{:S(2)}, u32[]{:S(2)}) collective-permute-start(bf16[256,512]{1,0:T(8,128)(2,1)S(1)} %get-tuple-element.15), channel_id=1, source_target_pairs={{0,2},{2,0},{1,3},{3,1},{4,6},{6,4},{5,7},{7,5},{8,10},{10,8},{9,1... | collective-permute-start | bytes 786440 | tf_op jit(solution)/shard_map/ppermute | solution.py:260
  28.7 1.6 %collective-permute-start.2 = (bf16[256,512]{1,0:T(8,128)(2,1)S(1)}, bf16[256,512]{1,0:T(8,128)(2,1)S(1)}, u32[]{:S(2)}, u32[]{:S(2)}) collective-permute-start(bf16[256,512]{1,0:T(8,128)(2,1)S(1)} %get-tuple-element.18), channel_id=1, source_target_pairs={{0,2},{2,0},{1,3},{3,1},{4,6},{6,4},{5,7},{7,5},{8,10},{10,8},{9,1... | collective-permute-start | bytes 786440 | tf_op jit(solution)/shard_map/ppermute | solution.py:269
  31.4 14.7 %all-to-all-start.1 = ((bf16[16,32,256]{2,1,0:T(8,128)(2,1)}), bf16[16,32,256]{2,1,0:T(8,128)(2,1)S(1)}, u32[]{:S(2)}, u32[]{:S(2)}) async-start(bf16[16,32,256]{2,1,0:T(8,128)(2,1)} %bitcast.10), calls=%async_computation.1 | async-start | bytes 524288 | tf_op jit(solution)/shard_map/all_to_all | solution.py:280
  35.9 0.7 %collective-permute-start.3 = (bf16[256,256]{1,0:T(8,128)(2,1)S(1)}, bf16[256,256]{1,0:T(8,128)(2,1)S(1)}, u32[]{:S(2)}, u32[]{:S(2)}) collective-permute-start(bf16[256,256]{1,0:T(8,128)(2,1)S(1)} %get-tuple-element.19), channel_id=1, source_target_pairs={{0,0},{1,2},{2,1},{3,3},{4,4},{5,6},{6,5},{7,7},{8,8},{9,10},{10,9... | collective-permute-start | bytes 393224 | tf_op jit(solution)/shard_map/ppermute | solution.py:270

commit v4 on v3

--- a/solution.py
+++ b/solution.py
@@ -18,6 +18,10 @@
 PARAMS = pltpu.CompilerParams(vmem_limit_bytes=24 * 1024 * 1024)
 
 
+def middle_first(columns):
+    return sorted(range(columns), key=lambda column: abs(2 * column - columns - 1))
+
+
 def dot(left, right, left_dim, right_dim):
     return lax.dot_general(
         left, right, (((left_dim,), (right_dim,)), ((), ())), preferred_element_type=jnp.float32
@@ -26,7 +30,10 @@
 
 def chunk_kernel(feats, chunks, held, in_sems, out_sems):
     places, columns, _, rows = chunks.shape
-    spots = [(place, column) for column in range(columns) for place in range(places)]
+    rank = {column: at for at, column in enumerate(middle_first(columns))}
+    spots = [
+        (places - 1 - place, rank[column]) for column in range(columns) for place in range(places)
+    ]
     loads, stores = [], []
     for at, (place, column) in enumerate(spots):
         loads.append(
@@ -99,7 +106,7 @@
 def project_kernel(weight, arrived, part, part_out):
     places, columns, width, rows = arrived.shape
     for place in range(places):
-        nodes = arrived[place].reshape(columns * width, rows)
+        nodes = arrived[places - 1 - place].reshape(columns * width, rows)
         value = dot(weight[...], nodes, 1, 0)
         part[:, place * rows : (place + 1) * rows] = value
         part_out[:, place * rows : (place + 1) * rows] = value.astype(part_out.dtype)
@@ -122,56 +129,37 @@
     )(weight, arrived)
 
 
-def block_kernel(*refs):
-    *projected, side, act, terms, terms_out = refs
-    hidden, rows = act.shape
+def parts(side, rows, hidden):
     groups = side.shape[1] // rows
     part = hidden // groups
-    if len(projected) == 2:
-        nodes = (projected[0][...] + projected[1][...].astype(jnp.float32)).astype(jnp.bfloat16)
-    else:
-        nodes = projected[0][...]
-    adjacency = side[:rows, :]
+    cotangent = jnp.concatenate(
+        [side[rows : rows + part, group * rows : (group + 1) * rows] for group in range(groups)], 0
+    )
+    return side[:rows, :], cotangent
+
+
+def block_terms(nodes, side, rows, act=None):
+    adjacency, cotangent = parts(side, rows, nodes.shape[0])
     preact = dot(nodes, adjacency, 1, 1)
     normal_cdf = 0.5 * (1.0 + lax.erf(preact * root_half))
     normal_pdf = jnp.exp(-0.5 * preact * preact) * inv_root_two_pi
-    act[...] = (preact * normal_cdf).astype(act.dtype)
+    if act is not None:
+        act[...] = (preact * normal_cdf).astype(act.dtype)
     derivative = normal_cdf + preact * normal_pdf
-    cotangent = jnp.concatenate(
-        [side[rows : rows + part, group * rows : (group + 1) * rows] for group in range(groups)], 0
-    )
     pre_grad = (cotangent.astype(jnp.float32) * derivative).astype(jnp.bfloat16)
-    value = dot(pre_grad, adjacency, 1, 0)
-    terms[...] = value
-    terms_out[...] = value.astype(terms_out.dtype)
-
-
-def block(projected, side, rows):
-    hidden, cluster = projected[0].shape
-    return pl.pallas_call(
-        block_kernel,
-        out_shape=(
-            jax.ShapeDtypeStruct((hidden, rows), jnp.bfloat16),
-            jax.ShapeDtypeStruct((hidden, cluster), jnp.float32),
-            jax.ShapeDtypeStruct((hidden, cluster), jnp.bfloat16),
-        ),
-        in_specs=[VMEM] * (len(projected) + 1),
-        out_specs=(VMEM,) * 3,
-        compiler_params=PARAMS,
-        name="block",
-    )(*projected, side)
-
-
-def gradient_kernel(arrived, part, other, terms, held, sems):
+    return dot(pre_grad, adjacency, 1, 0)
+
+
+def gradient_terms(arrived, node_grad, terms, held, sems):
     places, columns, width, rows = arrived.shape
     count = held.shape[0]
     size = columns // count
-    node_grad = (part[...] + other[...].astype(jnp.float32)).astype(jnp.bfloat16)
     copies = []
     for group in range(count):
         total = None
         for place in range(places):
-            nodes = arrived[place, group * size : (group + 1) * size].reshape(size * width, rows)
+            source = places - 1 - place
+            nodes = arrived[source, group * size : (group + 1) * size].reshape(size * width, rows)
             value = dot(nodes, node_grad[:, place * rows : (place + 1) * rows], 1, 1)
             total = value if total is None else total + value
         if len(terms.shape) == 2:
@@ -181,7 +169,7 @@
             share = terms.shape[2]
             total = total.astype(terms.dtype).reshape(size, places, share, total.shape[1])
             for place in range(places):
-                held[group, place] = total[:, place]
+                held[group, places - 1 - place] = total[:, place]
             target = terms.at[:, pl.ds(group * size, size)]
         copies.append(pltpu.make_async_copy(held.at[group], target, sems.at[group]))
         copies[-1].start()
@@ -189,21 +177,85 @@
         copy.wait()
 
 
-def gradient(arrived, part, other, shape, dtype):
+def own_kernel(part, other, side, act, nodes, total):
+    nodes[...] = (part[...] + other[...].astype(jnp.float32)).astype(nodes.dtype)
+    total[...] = block_terms(nodes[...], side, act.shape[1], act)
+
+
+def pair_kernel(nodes, side, own_total, arrived, terms, held, sems):
+    rows = arrived.shape[3]
+    total = own_total[...] + block_terms(nodes[...], side, rows)
+    gradient_terms(arrived, total.astype(jnp.bfloat16), terms, held, sems)
+
+
+def node_kernel(nodes, own, pair, act, total):
+    rows = act.shape[1]
+    total[...] = block_terms(nodes[...], own, rows, act) + block_terms(nodes[...], pair, rows)
+
+
+def gradient_kernel(arrived, node_grad, terms, held, sems):
+    gradient_terms(arrived, node_grad[...], terms, held, sems)
+
+
+def gradient_scratch(shape, dtype):
     count = 2
     if len(shape) == 2:
         held = (count, shape[0] // count, shape[1])
     else:
         held = (count, shape[0], shape[1] // count) + shape[2:]
+    return [pltpu.VMEM(held, dtype), pltpu.SemaphoreType.DMA((count,))]
+
+
+def own_block(part, other, side, rows):
+    hidden, cluster = part.shape
+    return pl.pallas_call(
+        own_kernel,
+        out_shape=(
+            jax.ShapeDtypeStruct((hidden, rows), jnp.bfloat16),
+            jax.ShapeDtypeStruct((hidden, cluster), jnp.bfloat16),
+            jax.ShapeDtypeStruct((hidden, cluster), jnp.float32),
+        ),
+        in_specs=[VMEM] * 3,
+        out_specs=(VMEM,) * 3,
+        compiler_params=PARAMS,
+        name="own_block",
+    )(part, other, side)
+
+
+def pair_block(nodes, side, own_total, arrived, shape):
+    return pl.pallas_call(
+        pair_kernel,
+        out_shape=jax.ShapeDtypeStruct(shape, jnp.bfloat16),
+        in_specs=[VMEM] * 4,
+        out_specs=ANY,
+        scratch_shapes=gradient_scratch(shape, jnp.bfloat16),
+        compiler_params=PARAMS,
+        name="pair_block",
+    )(nodes, side, own_total, arrived)
+
+
+def node_sums(nodes, own, pair, rows):
+    act = jax.ShapeDtypeStruct((nodes.shape[0], rows), jnp.bfloat16)
+    return pl.pallas_call(
+        node_kernel,
+        out_shape=(act, jax.ShapeDtypeStruct(nodes.shape, jnp.float32)),
+        in_specs=[VMEM] * 3,
+        out_specs=(VMEM, VMEM),
+        compiler_params=PARAMS,
+        name="block",
+    )(nodes, own, pair)
+
+
+def gradient(arrived, node_grad, shape):
     return pl.pallas_call(
         gradient_kernel,
-        out_shape=jax.ShapeDtypeStruct(shape, dtype),
-        in_specs=[VMEM] * 3,
+        out_shape=jax.ShapeDtypeStruct(shape, jnp.float32),
+        in_specs=[VMEM] * 2,
         out_specs=ANY,
-        scratch_shapes=[pltpu.VMEM(held, dtype), pltpu.SemaphoreType.DMA((count,))],
+        scratch_shapes=gradient_scratch(shape, jnp.float32),
         compiler_params=PARAMS,
         name="gradient",
-    )(arrived, part, other)
+    )(arrived, node_grad)
 
 
 def finish_kernel(terms, act, total_out, act_out, total, sems):
@@ -242,9 +294,18 @@
     rows = shard_nodes // (2 * columns)
     hidden = weight.shape[1]
     bf16 = jnp.bfloat16
+    order = middle_first(columns)
+    axes = ("col", "core", "hi", "lo")
+    groups = [
+        [((column * 2 + c) * pairs + hi) * 2 + place for place in (1, 0) for column in order]
+        for c in range(2)
+        for hi in range(pairs)
+    ]
 
     chunks = by_destination(feats, 2, columns).reshape(2 * columns, width, rows)
-    arrived = lax.all_to_all(chunks, ("lo", "col"), split_axis=0, concat_axis=0, tiled=True)
+    arrived = lax.all_to_all(
+        chunks, axes, split_axis=0, concat_axis=0, tiled=True, axis_index_groups=groups
+    )
     arrived = arrived.reshape(2, columns, width, rows)
 
     side = side_inputs(
@@ -253,31 +314,32 @@
     side = lax.ppermute(side, ("core", "lo"), TRANSPOSE)
     own_weight = lax.dynamic_index_in_dim(
         weight.reshape(columns, 2, width, hidden), core, 1, keepdims=False
-    ).reshape(columns * width, hidden).T
+    )
+    own_weight = jnp.stack([own_weight[column] for column in order])
+    own_weight = own_weight.reshape(columns * width, hidden).T
     arrived, side, own_weight = lax.optimization_barrier((arrived, side, own_weight))
+    side_pair = lax.ppermute(side, "core", SWAP)
 
     part, sent = project(own_weight, arrived)
     other = lax.ppermute(sent, "core", SWAP)
-    projected = (part, other)
-    if pairs > 1:
-        total = (part + other.astype(jnp.float32)).astype(bf16)
-        projected = (lax.all_gather(total, "hi", axis=1, tiled=True),)
-    output, part, sent = block(projected, side, rows)
-    if pairs > 1:
-        part = lax.psum_scatter(part, "hi", scatter_dimension=1, tiled=True)
-        sent = part.astype(bf16)
-    other = lax.ppermute(sent, "core", SWAP)
-    act = lax.ppermute(output, ("core", "lo"), TRANSPOSE)
     share = width // (2 * pairs)
     if pairs > 1:
-        terms = gradient(arrived, part, other, (columns * width, hidden), jnp.float32)
+        nodes = (part + other.astype(jnp.float32)).astype(bf16)
+        nodes = lax.all_gather(nodes, "hi", axis=1, tiled=True)
+        output, node_grad = node_sums(nodes, side, side_pair, rows)
+        node_grad = lax.psum_scatter(node_grad, "hi", scatter_dimension=1, tiled=True)
+        terms = gradient(arrived, node_grad.astype(bf16), (columns * width, hidden))
         terms = terms.reshape(columns, pairs, 2, share, hidden)
         terms = lax.psum_scatter(terms, "hi", scatter_dimension=1, tiled=True).astype(bf16)
-        terms = terms[:, 0].transpose(1, 0, 2, 3)
+        terms = terms[:, 0, ::-1].transpose(1, 0, 2, 3)
     else:
-        terms = gradient(arrived, part, other, (2, columns, share, hidden), bf16)
+        output, nodes, total = own_block(part, other, side, rows)
+        terms = pair_block(nodes, side_pair, total, arrived, (2, columns, share, hidden))
+    act = lax.ppermute(output, ("core", "lo"), TRANSPOSE)
     terms = terms.reshape(2 * columns, share, hidden)
-    terms = lax.all_to_all(terms, ("lo", "col"), split_axis=0, concat_axis=0, tiled=True)
+    terms = lax.all_to_all(
+        terms, axes, split_axis=0, concat_axis=0, tiled=True, axis_index_groups=groups
+    )
     weight_grad, act = finish(terms, act)
     return (act, weight_grad)
 

time: 47.1 us -> 42.8 us (0.909)
  waiting for transfers between devices: 24.7 us -> 16.6 us
  starting transfers between devices: 14.6 us -> 17.7 us
    all_to_all x2, waiting for transfers between devices: 21.7 us -> 15.3 us  [the longest x1 8.59 us: per_device(): lax.all_to_all(chunks, axes, split_axis=0, concat_axis=0, tiled=True, axi...]
    all_to_all x2, starting transfers between devices: 13 us -> 15.8 us  [the longest x1 8.93 us: per_device(): lax.all_to_all(chunks, axes, split_axis=0, concat_axis=0, tiled=True, axi...]
    ppermute x2 -> x1, waiting for transfers between devices: 2.92 us -> 1.32 us  [per_device(): other = lax.ppermute(sent, 'core', SWAP)]
    pallas_call x2, Pallas kernels: 1.62 us -> 2.11 us  [the longest x1 1.55 us: pair_block(): pl.pallas_call(pair_kernel, out_shape=jax.ShapeDtypeStruct(shape, jnp.bfl...]
  transfers between devices with their start and end apart: 6 -> 6, of which waited for: 4 -> 3; matrix products, arithmetic and copies ran while one was open for 0% -> 1% of each run, Pallas kernels for 1% -> 4%
where the time goes in v4:
time: 42.8 us; the launch traced here: 42.3 us
  starting transfers between devices  17.7 us (41%)
  waiting for transfers between devices  16.6 us (39%)
  Pallas kernels  5.63 us (13%)
  between operations  1.51 us (4%)
  local copies, waits for them, and re-layouts  0.9 us (2%)
    all_to_all x1, starting transfers between devices, per_device(): lax.all_to_all(chunks, axes, split_axis=0, concat_axis=0, tiled=True, axi...  8.93 us
    all_to_all x1, waiting for transfers between devices, per_device(): lax.all_to_all(chunks, axes, split_axis=0, concat_axis=0, tiled=True, axi...  8.59 us
    all_to_all x1, starting transfers between devices, per_device(): lax.all_to_all(terms, axes, split_axis=0, concat_axis=0, tiled=True, axis...  6.82 us
    all_to_all x1, waiting for transfers between devices, per_device(): lax.all_to_all(terms, axes, split_axis=0, concat_axis=0, tiled=True, axis...  6.72 us
    pallas_call x1, Pallas kernels, by_destination(): pl.pallas_call(chunk_kernel, out_shape=jax.ShapeDtypeStruct(shape, feats....  1.91 us
    pallas_call x1, Pallas kernels, pair_block(): pl.pallas_call(pair_kernel, out_shape=jax.ShapeDtypeStruct(shape, jnp.bfl...  1.55 us
    ppermute x1, waiting for transfers between devices, per_device(): other = lax.ppermute(sent, 'core', SWAP)  1.32 us
  transfers between devices with their start and end apart: 6, of which 3 were waited for; matrix products, arithmetic and copies ran while one was open for 1% of the time, Pallas kernels for 4%

profile of v4, /device:TPU:0, one launch (start us, length us, event | category | flops | bytes accessed | tf_op | source)
XLA Modules:
  0.0 42.3 jit_solution(7237450857647815107)
XLA Ops:
  0.6 1.9 %by_destination.1 = bf16[2,8,64,256]{3,2,1,0:T(8,128)(2,1)} custom-call(bf16[64,4096]{1,0:T(8,128)(2,1)} %feats.1), custom_call_target="tpu_custom_call" | custom-call | tf_op jit(solution)/shard_map/by_destination/pallas_call | solution.py:59
  2.5 0.0 copy-start
  2.6 0.0 copy-start.1
  2.6 0.0 copy-start.5
  2.6 8.9 %all-to-all-start = ((bf16[16,64,256]{2,1,0:T(8,128)(2,1)}), bf16[16,64,256]{2,1,0:T(8,128)(2,1)S(1)}, u32[]{:S(2)}, u32[]{:S(2)}) async-start(bf16[16,64,256]{2,1,0:T(8,128)(2,1)} %bitcast.51), calls=%async_computation | async-start | bytes 1048576 | tf_op jit(solution)/shard_map/all_to_all | solution.py:306
  12.2 0.0 copy-start.2
  12.2 0.0 copy-start.3
  12.2 0.0 copy-start.4
  12.2 0.0 copy-done
  12.2 0.0 copy-done.1
  12.2 0.6 %copy-done.2 = s32[1,1,8]{2,1,0:T(1,128)S(1)} copy-done((s32[1,1,8]{2,1,0:T(1,128)S(1)}, s32[1,1,8]{2,1,0:T(1,128)}, u32[]{:S(2)}) %copy-start.2) | copy-done | bytes 56
  12.8 0.0 copy-done.3
  12.8 0.0 copy-done.4
  12.9 0.6 %side_inputs.1 = bf16[384,512]{1,0:T(8,128)(2,1)S(1)} custom-call(s32[8]{0:T(128)S(1)} %bitcast.48, s32[8]{0:T(128)S(1)} %bitcast.49, s32[8]{0:T(128)S(1)} %bitcast.50, s32[1]{0:T(128)} %bitcast.43.live, bf16[8,128,128]{2,1,0:T(8,128)(2,1)S(1)} %bitcast.47, bf16[256,256]{1,0:T(8,128)(2,1)S(1)} %copy-done.1), custom_call_target="tpu_custom_call" | custom-call | tf_op jit(solution)/shard_map/side_inputs/pallas_call | solution.py:96
  13.5 0.7 %collective-permute-start = (bf16[384,512]{1,0:T(8,128)(2,1)S(1)}, bf16[384,512]{1,0:T(8,128)(2,1)S(1)}, u32[]{:S(2)}, u32[]{:S(2)}) collective-permute-start(bf16[384,512]{1,0:T(8,128)(2,1)S(1)} %side_inputs.1), channel_id=1, source_target_pairs={{0,0},{1,2},{2,1},{3,3},{4,4},{5,6},{6,5},{7,7},{8,8},{9,10},{10,9... | collective-permute-start | bytes 1179656 | tf_op jit(solution)/shard_map/ppermute | solution.py:314
  14.2 0.0 copy-done.5
  14.4 0.1 copy.18
  14.5 0.0 collective-permute-done.side
  14.5 8.6 %all-to-all-done = bf16[16,64,256]{2,1,0:T(8,128)(2,1)S(1)} async-done(((bf16[16,64,256]{2,1,0:T(8,128)(2,1)}), bf16[16,64,256]{2,1,0:T(8,128)(2,1)S(1)}, u32[]{:S(2)}, u32[]{:S(2)}) %all-to-all-start) | async-done | bytes 524320 | tf_op jit(solution)/shard_map/all_to_all | solution.py:306
  23.1 0.3 collective-permute-start.2
  23.4 0.3 project.1
  23.7 0.3 collective-permute-start.1
  24.0 1.3 %collective-permute-done.1.other = bf16[256,512]{1,0:T(8,128)(2,1)S(1)} collective-permute-done((bf16[256,512]{1,0:T(8,128)(2,1)S(1)}, bf16[256,512]{1,0:T(8,128)(2,1)S(1)}, u32[]{:S(2)}, u32[]{:S(2)}) %collective-permute-start.1) | collective-permute-done | bytes 262176 | tf_op jit(solution)/shard_map/ppermute | solution.py:324
  25.3 0.6 %own_block.1 = (bf16[256,256]{1,0:T(8,128)(2,1)S(1)}, bf16[256,512]{1,0:T(8,128)(2,1)S(1)}, f32[256,512]{1,0:T(8,128)S(1)}) custom-call(f32[256,512]{1,0:T(8,128)S(1)} %get-tuple-element.14.part, bf16[256,512]{1,0:T(8,128)(2,1)S(1)} %collective-permute-done.1.other, bf16[384,512]{1,0:T(8,128)(2,1)S(1)} %collective-permute-done.side), custom_call_target="tpu_custom_call" | custom-call | tf_op jit(solution)/shard_map/own_block/pallas_call | solution.py:211
  25.9 0.0 collective-permute-done.2.side
  25.9 1.5 %pair_block.1 = bf16[2,8,32,256]{3,2,1,0:T(8,128)(2,1)} custom-call(bf16[256,512]{1,0:T(8,128)(2,1)S(1)} %get-tuple-element.17.nodes, bf16[384,512]{1,0:T(8,128)(2,1)S(1)} %collective-permute-done.2.side, f32[256,512]{1,0:T(8,128)S(1)} %get-tuple-element.18.own_total, bf16[2,8,64,256]{3,2,1,0:T(8,128)(2,1)S(1)} %bitcast.45), custom_call_target="tpu_custom_call" | custom-call | tf_op jit(solution)/shard_map/pair_block/pallas_call | solution.py:226
  27.4 6.8 %all-to-all-start.1 = ((bf16[16,32,256]{2,1,0:T(8,128)(2,1)}), bf16[16,32,256]{2,1,0:T(8,128)(2,1)S(1)}, u32[]{:S(2)}, u32[]{:S(2)}) async-start(bf16[16,32,256]{2,1,0:T(8,128)(2,1)} %bitcast.18), calls=%async_computation.1 | async-start | bytes 524288 | tf_op jit(solution)/shard_map/all_to_all | solution.py:340
  34.3 0.7 %collective-permute-start.3 = (bf16[256,256]{1,0:T(8,128)(2,1)S(1)}, bf16[256,256]{1,0:T(8,128)(2,1)S(1)}, u32[]{:S(2)}, u32[]{:S(2)}) collective-permute-start(bf16[256,256]{1,0:T(8,128)(2,1)S(1)} %get-tuple-element.19), channel_id=1, source_target_pairs={{0,0},{1,2},{2,1},{3,3},{4,4},{5,6},{6,5},{7,7},{8,8},{9,10},{10,9... | collective-permute-start | bytes 393224 | tf_op jit(solution)/shard_map/ppermute | solution.py:338
  34.9 0.0 collective-permute-done.3.act
  34.9 6.7 %all-to-all-done.1.terms = bf16[16,32,256]{2,1,0:T(8,128)(2,1)S(1)} async-done(((bf16[16,32,256]{2,1,0:T(8,128)(2,1)}), bf16[16,32,256]{2,1,0:T(8,128)(2,1)S(1)}, u32[]{:S(2)}, u32[]{:S(2)}) %all-to-all-start.1) | async-done | bytes 262176 | tf_op jit(solution)/shard_map/all_to_all | solution.py:340
  41.7 0.7 %finish.1 = (f32[32,256]{1,0:T(8,128)}, bf16[256,256]{1,0:T(8,128)(2,1)}) custom-call(bf16[16,32,256]{2,1,0:T(8,128)(2,1)S(1)} %all-to-all-done.1.terms, bf16[256,256]{1,0:T(8,128)(2,1)S(1)} %collective-permute-done.3.act), custom_call_target="tpu_custom_call" | custom-call | tf_op jit(solution)/shard_map/finish/pallas_call | solution.py:272
  (8 shorter events, 0.1 us)
Async XLA Ops:
  2.5 9.7 %copy-start = (bf16[1,1,8,128,128]{4,3,2,1,0:T(8,128)(2,1)S(1)}, bf16[1,1,8,128,128]{4,3,2,1,0:T(8,128)(2,1)}, u32[]{:S(2)}) copy-start(bf16[1,1,8,128,128]{4,3,2,1,0:T(8,128)(2,1)} %param.14) | copy-start | bytes 786436
  2.6 9.7 %copy-start.1 = (bf16[256,256]{1,0:T(8,128)(2,1)S(1)}, bf16[256,256]{1,0:T(8,128)(2,1)}, u32[]{:S(2)}) copy-start(bf16[256,256]{1,0:T(8,128)(2,1)} %cotangent.1) | copy-start | bytes 393220
  2.6 11.6 %copy-start.5 = (bf16[1024,256]{1,0:T(8,128)(2,1)S(1)}, bf16[1024,256]{1,0:T(8,128)(2,1)}, u32[]{:S(2)}) copy-start(bf16[1024,256]{1,0:T(8,128)(2,1)} %param.9) | copy-start | bytes 1572868
  2.6 20.5 %all-to-all-start = ((bf16[16,64,256]{2,1,0:T(8,128)(2,1)}), bf16[16,64,256]{2,1,0:T(8,128)(2,1)S(1)}, u32[]{:S(2)}, u32[]{:S(2)}) async-start(bf16[16,64,256]{2,1,0:T(8,128)(2,1)} %bitcast.51), calls=%async_computation | async-start | bytes 1048576 | tf_op jit(solution)/shard_map/all_to_all | solution.py:306
  12.2 0.7 %copy-start.2 = (s32[1,1,8]{2,1,0:T(1,128)S(1)}, s32[1,1,8]{2,1,0:T(1,128)}, u32[]{:S(2)}) copy-start(s32[1,1,8]{2,1,0:T(1,128)} %param.10) | copy-start | bytes 100
  12.2 0.7 %copy-start.3 = (s32[1,1,8]{2,1,0:T(1,128)S(1)}, s32[1,1,8]{2,1,0:T(1,128)}, u32[]{:S(2)}) copy-start(s32[1,1,8]{2,1,0:T(1,128)} %param.11) | copy-start | bytes 100
  12.2 0.7 %copy-start.4 = (s32[1,1,8]{2,1,0:T(1,128)S(1)}, s32[1,1,8]{2,1,0:T(1,128)}, u32[]{:S(2)}) copy-start(s32[1,1,8]{2,1,0:T(1,128)} %param.12) | copy-start | bytes 100
  13.5 1.0 %collective-permute-start = (bf16[384,512]{1,0:T(8,128)(2,1)S(1)}, bf16[384,512]{1,0:T(8,128)(2,1)S(1)}, u32[]{:S(2)}, u32[]{:S(2)}) collective-permute-start(bf16[384,512]{1,0:T(8,128)(2,1)S(1)} %side_inputs.1), channel_id=1, source_target_pairs={{0,0},{1,2},{2,1},{3,3},{4,4},{5,6},{6,5},{7,7},{8,8},{9,10},{10,9... | collective-permute-start | bytes 1179656 | tf_op jit(solution)/shard_map/ppermute | solution.py:314
  23.1 2.8 %collective-permute-start.2 = (bf16[384,512]{1,0:T(8,128)(2,1)S(1)}, bf16[384,512]{1,0:T(8,128)(2,1)S(1)}, u32[]{:S(2)}, u32[]{:S(2)}) collective-permute-start(bf16[384,512]{1,0:T(8,128)(2,1)S(1)} %collective-permute-done.side), channel_id=1, source_target_pairs={{0,2},{2,0},{1,3},{3,1},{4,6},{6,4},{5,7},{7,5},{8,10},{10,8},{9,1... | collective-permute-start | bytes 1179656 | tf_op jit(solution)/shard_map/ppermute | solution.py:321
  23.7 1.6 %collective-permute-start.1 = (bf16[256,512]{1,0:T(8,128)(2,1)S(1)}, bf16[256,512]{1,0:T(8,128)(2,1)S(1)}, u32[]{:S(2)}, u32[]{:S(2)}) collective-permute-start(bf16[256,512]{1,0:T(8,128)(2,1)S(1)} %get-tuple-element.15), channel_id=1, source_target_pairs={{0,2},{2,0},{1,3},{3,1},{4,6},{6,4},{5,7},{7,5},{8,10},{10,8},{9,1... | collective-permute-start | bytes 786440 | tf_op jit(solution)/shard_map/ppermute | solution.py:324
  27.4 14.2 %all-to-all-start.1 = ((bf16[16,32,256]{2,1,0:T(8,128)(2,1)}), bf16[16,32,256]{2,1,0:T(8,128)(2,1)S(1)}, u32[]{:S(2)}, u32[]{:S(2)}) async-start(bf16[16,32,256]{2,1,0:T(8,128)(2,1)} %bitcast.18), calls=%async_computation.1 | async-start | bytes 524288 | tf_op jit(solution)/shard_map/all_to_all | solution.py:340
  34.3 0.7 %collective-permute-start.3 = (bf16[256,256]{1,0:T(8,128)(2,1)S(1)}, bf16[256,256]{1,0:T(8,128)(2,1)S(1)}, u32[]{:S(2)}, u32[]{:S(2)}) collective-permute-start(bf16[256,256]{1,0:T(8,128)(2,1)S(1)} %get-tuple-element.19), channel_id=1, source_target_pairs={{0,0},{1,2},{2,1},{3,3},{4,4},{5,6},{6,5},{7,7},{8,8},{9,10},{10,9... | collective-permute-start | bytes 393224 | tf_op jit(solution)/shard_map/ppermute | solution.py:338

commit v5 on v4

--- a/solution.py
+++ b/solution.py
@@ -19,7 +19,10 @@
 
 
 def middle_first(columns):
-    return sorted(range(columns), key=lambda column: abs(2 * column - columns - 1))
+    quarter = columns // 4
+    order = [at * quarter + rest for at in (2, 1, 3, 0) for rest in reversed(range(quarter))]
+    order.remove(columns // 2)
+    return [columns // 2] + order
 
 
 def dot(left, right, left_dim, right_dim):
@@ -177,14 +180,10 @@
         copy.wait()
 
 
-def own_kernel(part, other, side, act, nodes, total):
-    nodes[...] = (part[...] + other[...].astype(jnp.float32)).astype(nodes.dtype)
-    total[...] = block_terms(nodes[...], side, act.shape[1], act)
-
-
-def pair_kernel(nodes, side, own_total, arrived, terms, held, sems):
-    rows = arrived.shape[3]
-    total = own_total[...] + block_terms(nodes[...], side, rows)
+def whole_kernel(part, other, own, pair, arrived, act, terms, held, sems):
+    rows = act.shape[1]
+    nodes = (part[...] + other[...].astype(jnp.float32)).astype(jnp.bfloat16)
+    total = block_terms(nodes, own, rows, act) + block_terms(nodes, pair, rows)
     gradient_terms(arrived, total.astype(jnp.bfloat16), terms, held, sems)
 
 
@@ -206,32 +205,17 @@
     return [pltpu.VMEM(held, dtype), pltpu.SemaphoreType.DMA((count,))]
 
 
-def own_block(part, other, side, rows):
-    hidden, cluster = part.shape
-    return pl.pallas_call(
-        own_kernel,
-        out_shape=(
-            jax.ShapeDtypeStruct((hidden, rows), jnp.bfloat16),
-            jax.ShapeDtypeStruct((hidden, cluster), jnp.bfloat16),
-            jax.ShapeDtypeStruct((hidden, cluster), jnp.float32),
-        ),
-        in_specs=[VMEM] * 3,
-        out_specs=(VMEM,) * 3,
-        compiler_params=PARAMS,
-        name="own_block",
-    )(part, other, side)
-
-
-def pair_block(nodes, side, own_total, arrived, shape):
-    return pl.pallas_call(
-        pair_kernel,
-        out_shape=jax.ShapeDtypeStruct(shape, jnp.bfloat16),
-        in_specs=[VMEM] * 4,
-        out_specs=ANY,
+def whole(part, other, own, pair, arrived, rows, shape):
+    act = jax.ShapeDtypeStruct((part.shape[0], rows), jnp.bfloat16)
+    return pl.pallas_call(
+        whole_kernel,
+        out_shape=(act, jax.ShapeDtypeStruct(shape, jnp.bfloat16)),
+        in_specs=[VMEM] * 5,
+        out_specs=(VMEM, ANY),
         scratch_shapes=gradient_scratch(shape, jnp.bfloat16),
         compiler_params=PARAMS,
-        name="pair_block",
-    )(nodes, side, own_total, arrived)
+        name="blocks_and_gradient",
+    )(part, other, own, pair, arrived)
 
 
 def node_sums(nodes, own, pair, rows):
@@ -333,8 +317,9 @@
         terms = lax.psum_scatter(terms, "hi", scatter_dimension=1, tiled=True).astype(bf16)
         terms = terms[:, 0, ::-1].transpose(1, 0, 2, 3)
     else:
-        output, nodes, total = own_block(part, other, side, rows)
-        terms = pair_block(nodes, side_pair, total, arrived, (2, columns, share, hidden))
+        output, terms = whole(
+            part, other, side, side_pair, arrived, rows, (2, columns, share, hidden)
+        )
     act = lax.ppermute(output, ("core", "lo"), TRANSPOSE)
     terms = terms.reshape(2 * columns, share, hidden)
     terms = lax.all_to_all(

time: 42.8 us -> 41.4 us (0.967)
  starting transfers between devices: 17.7 us -> 17.1 us
  Pallas kernels: 5.63 us -> 5.2 us
    all_to_all x1, starting transfers between devices: 6.82 us -> 5.87 us  [per_device(): lax.all_to_all(terms, axes, split_axis=0, concat_axis=0, tiled=True, axis...]
    ppermute x1, starting transfers between devices: 0.29 us -> 0.87 us  [per_device(): side_pair = lax.ppermute(side, 'core', SWAP)]
    all_to_all x1, waiting for transfers between devices: 6.72 us -> 6.2 us  [per_device(): lax.all_to_all(terms, axes, split_axis=0, concat_axis=0, tiled=True, axis...]
    pallas_call x2 -> x1, Pallas kernels: 2.11 us -> 1.68 us  [whole(): pl.pallas_call(whole_kernel, out_shape=(act, jax.ShapeDtypeStruct(shape,...]
  transfers between devices with their start and end apart: 6 -> 6, of which waited for: 3 -> 3; matrix products, arithmetic and copies ran while one was open for 1% -> 1% of each run, Pallas kernels for 4% -> 2%
where the time goes in v5:
time: 41.4 us; the launch traced here: 41 us
  starting transfers between devices  17.1 us (41%)
  waiting for transfers between devices  16.3 us (39%)
  Pallas kernels  5.2 us (13%)
  between operations  1.5 us (4%)
  local copies, waits for them, and re-layouts  0.9 us (2%)
    all_to_all x1, starting transfers between devices, per_device(): lax.all_to_all(chunks, axes, split_axis=0, concat_axis=0, tiled=True, axi...  8.93 us
    all_to_all x1, waiting for transfers between devices, per_device(): lax.all_to_all(chunks, axes, split_axis=0, concat_axis=0, tiled=True, axi...  8.59 us
    all_to_all x1, waiting for transfers between devices, per_device(): lax.all_to_all(terms, axes, split_axis=0, concat_axis=0, tiled=True, axis...  6.2 us
    all_to_all x1, starting transfers between devices, per_device(): lax.all_to_all(terms, axes, split_axis=0, concat_axis=0, tiled=True, axis...  5.87 us
    pallas_call x1, Pallas kernels, by_destination(): pl.pallas_call(chunk_kernel, out_shape=jax.ShapeDtypeStruct(shape, feats....  1.91 us
    pallas_call x1, Pallas kernels, whole(): pl.pallas_call(whole_kernel, out_shape=(act, jax.ShapeDtypeStruct(shape,...  1.68 us
    ppermute x1, waiting for transfers between devices, per_device(): other = lax.ppermute(sent, 'core', SWAP)  1.52 us
    ppermute x1, starting transfers between devices, per_device(): side_pair = lax.ppermute(side, 'core', SWAP)  0.87 us
  transfers between devices with their start and end apart: 6, of which 3 were waited for; matrix products, arithmetic and copies ran while one was open for 1% of the time, Pallas kernels for 2%

profile of v5, /device:TPU:0, one launch (start us, length us, event | category | flops | bytes accessed | tf_op | source)
XLA Modules:
  0.0 41.0 jit_solution(4633620409775279113)
XLA Ops:
  0.6 1.9 %by_destination.1 = bf16[2,8,64,256]{3,2,1,0:T(8,128)(2,1)} custom-call(bf16[64,4096]{1,0:T(8,128)(2,1)} %feats.1), custom_call_target="tpu_custom_call" | custom-call | tf_op jit(solution)/shard_map/by_destination/pallas_call | solution.py:62
  2.5 0.0 copy-start
  2.6 0.0 copy-start.1
  2.6 0.0 copy-start.5
  2.6 8.9 %all-to-all-start = ((bf16[16,64,256]{2,1,0:T(8,128)(2,1)}), bf16[16,64,256]{2,1,0:T(8,128)(2,1)S(1)}, u32[]{:S(2)}, u32[]{:S(2)}) async-start(bf16[16,64,256]{2,1,0:T(8,128)(2,1)} %bitcast.51), calls=%async_computation | async-start | bytes 1048576 | tf_op jit(solution)/shard_map/all_to_all | solution.py:290
  12.2 0.0 copy-start.2
  12.2 0.0 copy-start.3
  12.2 0.0 copy-start.4
  12.2 0.0 copy-done
  12.2 0.0 copy-done.1
  12.2 0.6 %copy-done.2 = s32[1,1,8]{2,1,0:T(1,128)S(1)} copy-done((s32[1,1,8]{2,1,0:T(1,128)S(1)}, s32[1,1,8]{2,1,0:T(1,128)}, u32[]{:S(2)}) %copy-start.2) | copy-done | bytes 56
  12.8 0.0 copy-done.3
  12.8 0.0 copy-done.4
  12.9 0.6 %side_inputs.1 = bf16[384,512]{1,0:T(8,128)(2,1)S(1)} custom-call(s32[8]{0:T(128)S(1)} %bitcast.48, s32[8]{0:T(128)S(1)} %bitcast.49, s32[8]{0:T(128)S(1)} %bitcast.50, s32[1]{0:T(128)} %bitcast.43.live, bf16[8,128,128]{2,1,0:T(8,128)(2,1)S(1)} %bitcast.47, bf16[256,256]{1,0:T(8,128)(2,1)S(1)} %copy-done.1), custom_call_target="tpu_custom_call" | custom-call | tf_op jit(solution)/shard_map/side_inputs/pallas_call | solution.py:99
  13.5 0.7 %collective-permute-start = (bf16[384,512]{1,0:T(8,128)(2,1)S(1)}, bf16[384,512]{1,0:T(8,128)(2,1)S(1)}, u32[]{:S(2)}, u32[]{:S(2)}) collective-permute-start(bf16[384,512]{1,0:T(8,128)(2,1)S(1)} %side_inputs.1), channel_id=1, source_target_pairs={{0,0},{1,2},{2,1},{3,3},{4,4},{5,6},{6,5},{7,7},{8,8},{9,10},{10,9... | collective-permute-start | bytes 1179656 | tf_op jit(solution)/shard_map/ppermute | solution.py:298
  14.2 0.0 copy-done.5
  14.4 0.1 copy.18
  14.5 0.0 collective-permute-done.own
  14.5 8.6 %all-to-all-done = bf16[16,64,256]{2,1,0:T(8,128)(2,1)S(1)} async-done(((bf16[16,64,256]{2,1,0:T(8,128)(2,1)}), bf16[16,64,256]{2,1,0:T(8,128)(2,1)S(1)}, u32[]{:S(2)}, u32[]{:S(2)}) %all-to-all-start) | async-done | bytes 524320 | tf_op jit(solution)/shard_map/all_to_all | solution.py:290
  23.1 0.9 %collective-permute-start.2 = (bf16[384,512]{1,0:T(8,128)(2,1)S(1)}, bf16[384,512]{1,0:T(8,128)(2,1)S(1)}, u32[]{:S(2)}, u32[]{:S(2)}) collective-permute-start(bf16[384,512]{1,0:T(8,128)(2,1)S(1)} %collective-permute-done.own), channel_id=1, source_target_pairs={{0,2},{2,0},{1,3},{3,1},{4,6},{6,4},{5,7},{7,5},{8,10},{10,8},{9,1... | collective-permute-start | bytes 1179656 | tf_op jit(solution)/shard_map/ppermute | solution.py:305
  24.0 0.3 project.1
  24.3 0.1 collective-permute-start.1
  24.4 1.5 %collective-permute-done.1.other = bf16[256,512]{1,0:T(8,128)(2,1)S(1)} collective-permute-done((bf16[256,512]{1,0:T(8,128)(2,1)S(1)}, bf16[256,512]{1,0:T(8,128)(2,1)S(1)}, u32[]{:S(2)}, u32[]{:S(2)}) %collective-permute-start.1) | collective-permute-done | bytes 262176 | tf_op jit(solution)/shard_map/ppermute | solution.py:308
  25.9 0.0 collective-permute-done.2.pair
  25.9 1.7 %blocks_and_gradient.1 = (bf16[256,256]{1,0:T(8,128)(2,1)S(1)}, bf16[2,8,32,256]{3,2,1,0:T(8,128)(2,1)}) custom-call(f32[256,512]{1,0:T(8,128)S(1)} %get-tuple-element.13.part, bf16[256,512]{1,0:T(8,128)(2,1)S(1)} %collective-permute-done.1.other, bf16[384,512]{1,0:T(8,128)(2,1)S(1)} %collective-permute-done.own, ...), custom_call_target="tpu_custom_call" | custom-call | tf_op jit(solution)/shard_map/blocks_and_gradient/pallas_call | solution.py:210
  27.6 5.9 %all-to-all-start.1 = ((bf16[16,32,256]{2,1,0:T(8,128)(2,1)}), bf16[16,32,256]{2,1,0:T(8,128)(2,1)S(1)}, u32[]{:S(2)}, u32[]{:S(2)}) async-start(bf16[16,32,256]{2,1,0:T(8,128)(2,1)} %bitcast.18), calls=%async_computation.1 | async-start | bytes 524288 | tf_op jit(solution)/shard_map/all_to_all | solution.py:325
  33.4 0.7 %collective-permute-start.3 = (bf16[256,256]{1,0:T(8,128)(2,1)S(1)}, bf16[256,256]{1,0:T(8,128)(2,1)S(1)}, u32[]{:S(2)}, u32[]{:S(2)}) collective-permute-start(bf16[256,256]{1,0:T(8,128)(2,1)S(1)} %get-tuple-element.17), channel_id=1, source_target_pairs={{0,0},{1,2},{2,1},{3,3},{4,4},{5,6},{6,5},{7,7},{8,8},{9,10},{10,9... | collective-permute-start | bytes 393224 | tf_op jit(solution)/shard_map/ppermute | solution.py:323
  34.1 0.0 collective-permute-done.3.act
  34.1 6.2 %all-to-all-done.1.terms = bf16[16,32,256]{2,1,0:T(8,128)(2,1)S(1)} async-done(((bf16[16,32,256]{2,1,0:T(8,128)(2,1)}), bf16[16,32,256]{2,1,0:T(8,128)(2,1)S(1)}, u32[]{:S(2)}, u32[]{:S(2)}) %all-to-all-start.1) | async-done | bytes 262176 | tf_op jit(solution)/shard_map/all_to_all | solution.py:325
  40.3 0.7 %finish.1 = (f32[32,256]{1,0:T(8,128)}, bf16[256,256]{1,0:T(8,128)(2,1)}) custom-call(bf16[16,32,256]{2,1,0:T(8,128)(2,1)S(1)} %all-to-all-done.1.terms, bf16[256,256]{1,0:T(8,128)(2,1)S(1)} %collective-permute-done.3.act), custom_call_target="tpu_custom_call" | custom-call | tf_op jit(solution)/shard_map/finish/pallas_call | solution.py:256
  (8 shorter events, 0.1 us)
Async XLA Ops:
  2.5 9.7 %copy-start = (bf16[1,1,8,128,128]{4,3,2,1,0:T(8,128)(2,1)S(1)}, bf16[1,1,8,128,128]{4,3,2,1,0:T(8,128)(2,1)}, u32[]{:S(2)}) copy-start(bf16[1,1,8,128,128]{4,3,2,1,0:T(8,128)(2,1)} %param.14) | copy-start | bytes 786436
  2.6 9.7 %copy-start.1 = (bf16[256,256]{1,0:T(8,128)(2,1)S(1)}, bf16[256,256]{1,0:T(8,128)(2,1)}, u32[]{:S(2)}) copy-start(bf16[256,256]{1,0:T(8,128)(2,1)} %cotangent.1) | copy-start | bytes 393220
  2.6 11.6 %copy-start.5 = (bf16[1024,256]{1,0:T(8,128)(2,1)S(1)}, bf16[1024,256]{1,0:T(8,128)(2,1)}, u32[]{:S(2)}) copy-start(bf16[1024,256]{1,0:T(8,128)(2,1)} %param.9) | copy-start | bytes 1572868
  2.6 20.5 %all-to-all-start = ((bf16[16,64,256]{2,1,0:T(8,128)(2,1)}), bf16[16,64,256]{2,1,0:T(8,128)(2,1)S(1)}, u32[]{:S(2)}, u32[]{:S(2)}) async-start(bf16[16,64,256]{2,1,0:T(8,128)(2,1)} %bitcast.51), calls=%async_computation | async-start | bytes 1048576 | tf_op jit(solution)/shard_map/all_to_all | solution.py:290
  12.2 0.7 %copy-start.2 = (s32[1,1,8]{2,1,0:T(1,128)S(1)}, s32[1,1,8]{2,1,0:T(1,128)}, u32[]{:S(2)}) copy-start(s32[1,1,8]{2,1,0:T(1,128)} %param.10) | copy-start | bytes 100
  12.2 0.7 %copy-start.3 = (s32[1,1,8]{2,1,0:T(1,128)S(1)}, s32[1,1,8]{2,1,0:T(1,128)}, u32[]{:S(2)}) copy-start(s32[1,1,8]{2,1,0:T(1,128)} %param.11) | copy-start | bytes 100
  12.2 0.7 %copy-start.4 = (s32[1,1,8]{2,1,0:T(1,128)S(1)}, s32[1,1,8]{2,1,0:T(1,128)}, u32[]{:S(2)}) copy-start(s32[1,1,8]{2,1,0:T(1,128)} %param.12) | copy-start | bytes 100
  13.5 1.0 %collective-permute-start = (bf16[384,512]{1,0:T(8,128)(2,1)S(1)}, bf16[384,512]{1,0:T(8,128)(2,1)S(1)}, u32[]{:S(2)}, u32[]{:S(2)}) collective-permute-start(bf16[384,512]{1,0:T(8,128)(2,1)S(1)} %side_inputs.1), channel_id=1, source_target_pairs={{0,0},{1,2},{2,1},{3,3},{4,4},{5,6},{6,5},{7,7},{8,8},{9,10},{10,9... | collective-permute-start | bytes 1179656 | tf_op jit(solution)/shard_map/ppermute | solution.py:298
  23.1 2.8 %collective-permute-start.2 = (bf16[384,512]{1,0:T(8,128)(2,1)S(1)}, bf16[384,512]{1,0:T(8,128)(2,1)S(1)}, u32[]{:S(2)}, u32[]{:S(2)}) collective-permute-start(bf16[384,512]{1,0:T(8,128)(2,1)S(1)} %collective-permute-done.own), channel_id=1, source_target_pairs={{0,2},{2,0},{1,3},{3,1},{4,6},{6,4},{5,7},{7,5},{8,10},{10,8},{9,1... | collective-permute-start | bytes 1179656 | tf_op jit(solution)/shard_map/ppermute | solution.py:305
  24.3 1.6 %collective-permute-start.1 = (bf16[256,512]{1,0:T(8,128)(2,1)S(1)}, bf16[256,512]{1,0:T(8,128)(2,1)S(1)}, u32[]{:S(2)}, u32[]{:S(2)}) collective-permute-start(bf16[256,512]{1,0:T(8,128)(2,1)S(1)} %get-tuple-element.14), channel_id=1, source_target_pairs={{0,2},{2,0},{1,3},{3,1},{4,6},{6,4},{5,7},{7,5},{8,10},{10,8},{9,1... | collective-permute-start | bytes 786440 | tf_op jit(solution)/shard_map/ppermute | solution.py:308
  27.6 12.7 %all-to-all-start.1 = ((bf16[16,32,256]{2,1,0:T(8,128)(2,1)}), bf16[16,32,256]{2,1,0:T(8,128)(2,1)S(1)}, u32[]{:S(2)}, u32[]{:S(2)}) async-start(bf16[16,32,256]{2,1,0:T(8,128)(2,1)} %bitcast.18), calls=%async_computation.1 | async-start | bytes 524288 | tf_op jit(solution)/shard_map/all_to_all | solution.py:325
  33.4 0.7 %collective-permute-start.3 = (bf16[256,256]{1,0:T(8,128)(2,1)S(1)}, bf16[256,256]{1,0:T(8,128)(2,1)S(1)}, u32[]{:S(2)}, u32[]{:S(2)}) collective-permute-start(bf16[256,256]{1,0:T(8,128)(2,1)S(1)} %get-tuple-element.17), channel_id=1, source_target_pairs={{0,0},{1,2},{2,1},{3,3},{4,4},{5,6},{6,5},{7,7},{8,8},{9,10},{10,9... | collective-permute-start | bytes 393224 | tf_op jit(solution)/shard_map/ppermute | solution.py:323

commit v6 on v5

--- a/solution.py
+++ b/solution.py
@@ -19,8 +19,9 @@
 
 
 def middle_first(columns):
-    quarter = columns // 4
-    order = [at * quarter + rest for at in (2, 1, 3, 0) for rest in reversed(range(quarter))]
+    quarter = max(columns // 4, 1)
+    rest = sorted(range(columns), key=lambda column: -column)
+    order = [column for at in (2, 1, 3, 0) for column in rest if min(column // quarter, 3) == at]
     order.remove(columns // 2)
     return [columns // 2] + order
 
@@ -33,25 +34,19 @@
 
 def chunk_kernel(feats, chunks, held, in_sems, out_sems):
     places, columns, _, rows = chunks.shape
-    rank = {column: at for at, column in enumerate(middle_first(columns))}
-    spots = [
-        (places - 1 - place, rank[column]) for column in range(columns) for place in range(places)
-    ]
-    loads, stores = [], []
-    for at, (place, column) in enumerate(spots):
-        loads.append(
+    for place in range(places):
+        for at, column in enumerate(middle_first(columns)):
+            source = (column * places + places - 1 - place) * rows
             pltpu.make_async_copy(
-                feats.at[:, pl.ds(at * rows, rows)], held.at[place, column], in_sems.at[at]
-            )
+                feats.at[:, pl.ds(source, rows)], held.at[place, at], in_sems.at[place]
+            ).start()
+    stores = []
+    for place in range(places):
+        pltpu.make_async_copy(held.at[place], held.at[place], in_sems.at[place]).wait()
+        stores.append(
+            pltpu.make_async_copy(held.at[place], chunks.at[place], out_sems.at[place])
         )
-        stores.append(
-            pltpu.make_async_copy(held.at[place, column], chunks.at[place, column], out_sems.at[at])
-        )
-    for load in loads:
-        load.start()
-    for load, store in zip(loads, stores):
-        load.wait()
-        store.start()
+        stores[-1].start()
     for store in stores:
         store.wait()
 
@@ -66,8 +61,8 @@
         out_specs=pl.BlockSpec(memory_space=pltpu.HBM),
         scratch_shapes=[
             pltpu.VMEM(shape, feats.dtype),
-            pltpu.SemaphoreType.DMA((places * columns,)),
-            pltpu.SemaphoreType.DMA((places * columns,)),
+            pltpu.SemaphoreType.DMA((places,)),
+            pltpu.SemaphoreType.DMA((places,)),
         ],
         compiler_params=pltpu.CompilerParams(vmem_limit_bytes=60 * 1024 * 1024),
         name="by_destination",

time: 41.4 us -> 41.3 us (level)
  no operation moved by 1% of the time
where the time goes in v6:
time: 41.3 us; the launch traced here: 40.8 us
  starting transfers between devices  17.1 us (41%)
  waiting for transfers between devices  16.3 us (39%)
  Pallas kernels  5.01 us (12%)
  between operations  1.5 us (4%)
  local copies, waits for them, and re-layouts  0.9 us (2%)
    all_to_all x1, starting transfers between devices, per_device(): lax.all_to_all(chunks, axes, split_axis=0, concat_axis=0, tiled=True, axi...  8.93 us
    all_to_all x1, waiting for transfers between devices, per_device(): lax.all_to_all(chunks, axes, split_axis=0, concat_axis=0, tiled=True, axi...  8.59 us
    all_to_all x1, waiting for transfers between devices, per_device(): lax.all_to_all(terms, axes, split_axis=0, concat_axis=0, tiled=True, axis...  6.2 us
    all_to_all x1, starting transfers between devices, per_device(): lax.all_to_all(terms, axes, split_axis=0, concat_axis=0, tiled=True, axis...  5.88 us
    pallas_call x1, Pallas kernels, by_destination(): pl.pallas_call(chunk_kernel, out_shape=jax.ShapeDtypeStruct(shape, feats....  1.73 us
    pallas_call x1, Pallas kernels, whole(): pl.pallas_call(whole_kernel, out_shape=(act, jax.ShapeDtypeStruct(shape,...  1.67 us
    ppermute x1, waiting for transfers between devices, per_device(): other = lax.ppermute(sent, 'core', SWAP)  1.52 us
    ppermute x1, starting transfers between devices, per_device(): side_pair = lax.ppermute(side, 'core', SWAP)  0.87 us
  transfers between devices with their start and end apart: 6, of which 3 were waited for; matrix products, arithmetic and copies ran while one was open for 1% of the time, Pallas kernels for 2%

profile of v6, /device:TPU:0, one launch (start us, length us, event | category | flops | bytes accessed | tf_op | source)
XLA Modules:
  0.0 40.8 jit_solution(3427591817555781472)
XLA Ops:
  0.6 1.7 %by_destination.1 = bf16[2,8,64,256]{3,2,1,0:T(8,128)(2,1)} custom-call(bf16[64,4096]{1,0:T(8,128)(2,1)} %feats.1), custom_call_target="tpu_custom_call" | custom-call | tf_op jit(solution)/shard_map/by_destination/pallas_call | solution.py:57
  2.4 0.0 copy-start
  2.4 0.0 copy-start.1
  2.4 0.0 copy-start.5
  2.4 8.9 %all-to-all-start = ((bf16[16,64,256]{2,1,0:T(8,128)(2,1)}), bf16[16,64,256]{2,1,0:T(8,128)(2,1)S(1)}, u32[]{:S(2)}, u32[]{:S(2)}) async-start(bf16[16,64,256]{2,1,0:T(8,128)(2,1)} %bitcast.51), calls=%async_computation | async-start | bytes 1048576 | tf_op jit(solution)/shard_map/all_to_all | solution.py:285
  12.0 0.0 copy-start.2
  12.0 0.0 copy-start.3
  12.0 0.0 copy-start.4
  12.0 0.0 copy-done
  12.0 0.0 copy-done.1
  12.0 0.6 %copy-done.2 = s32[1,1,8]{2,1,0:T(1,128)S(1)} copy-done((s32[1,1,8]{2,1,0:T(1,128)S(1)}, s32[1,1,8]{2,1,0:T(1,128)}, u32[]{:S(2)}) %copy-start.2) | copy-done | bytes 56
  12.6 0.0 copy-done.3
  12.7 0.0 copy-done.4
  12.7 0.6 %side_inputs.1 = bf16[384,512]{1,0:T(8,128)(2,1)S(1)} custom-call(s32[8]{0:T(128)S(1)} %bitcast.48, s32[8]{0:T(128)S(1)} %bitcast.49, s32[8]{0:T(128)S(1)} %bitcast.50, s32[1]{0:T(128)} %bitcast.43.live, bf16[8,128,128]{2,1,0:T(8,128)(2,1)S(1)} %bitcast.47, bf16[256,256]{1,0:T(8,128)(2,1)S(1)} %copy-done.1), custom_call_target="tpu_custom_call" | custom-call | tf_op jit(solution)/shard_map/side_inputs/pallas_call | solution.py:94
  13.3 0.7 %collective-permute-start = (bf16[384,512]{1,0:T(8,128)(2,1)S(1)}, bf16[384,512]{1,0:T(8,128)(2,1)S(1)}, u32[]{:S(2)}, u32[]{:S(2)}) collective-permute-start(bf16[384,512]{1,0:T(8,128)(2,1)S(1)} %side_inputs.1), channel_id=1, source_target_pairs={{0,0},{1,2},{2,1},{3,3},{4,4},{5,6},{6,5},{7,7},{8,8},{9,10},{10,9... | collective-permute-start | bytes 1179656 | tf_op jit(solution)/shard_map/ppermute | solution.py:293
  14.0 0.0 copy-done.5
  14.2 0.1 copy.18
  14.3 0.0 collective-permute-done.own
  14.4 8.6 %all-to-all-done = bf16[16,64,256]{2,1,0:T(8,128)(2,1)S(1)} async-done(((bf16[16,64,256]{2,1,0:T(8,128)(2,1)}), bf16[16,64,256]{2,1,0:T(8,128)(2,1)S(1)}, u32[]{:S(2)}, u32[]{:S(2)}) %all-to-all-start) | async-done | bytes 524320 | tf_op jit(solution)/shard_map/all_to_all | solution.py:285
  22.9 0.9 %collective-permute-start.2 = (bf16[384,512]{1,0:T(8,128)(2,1)S(1)}, bf16[384,512]{1,0:T(8,128)(2,1)S(1)}, u32[]{:S(2)}, u32[]{:S(2)}) collective-permute-start(bf16[384,512]{1,0:T(8,128)(2,1)S(1)} %collective-permute-done.own), channel_id=1, source_target_pairs={{0,2},{2,0},{1,3},{3,1},{4,6},{6,4},{5,7},{7,5},{8,10},{10,8},{9,1... | collective-permute-start | bytes 1179656 | tf_op jit(solution)/shard_map/ppermute | solution.py:300
  23.8 0.3 project.1
  24.1 0.1 collective-permute-start.1
  24.2 1.5 %collective-permute-done.1.other = bf16[256,512]{1,0:T(8,128)(2,1)S(1)} collective-permute-done((bf16[256,512]{1,0:T(8,128)(2,1)S(1)}, bf16[256,512]{1,0:T(8,128)(2,1)S(1)}, u32[]{:S(2)}, u32[]{:S(2)}) %collective-permute-start.1) | collective-permute-done | bytes 262176 | tf_op jit(solution)/shard_map/ppermute | solution.py:303
  25.7 0.0 collective-permute-done.2.pair
  25.7 1.7 %blocks_and_gradient.1 = (bf16[256,256]{1,0:T(8,128)(2,1)S(1)}, bf16[2,8,32,256]{3,2,1,0:T(8,128)(2,1)}) custom-call(f32[256,512]{1,0:T(8,128)S(1)} %get-tuple-element.13.part, bf16[256,512]{1,0:T(8,128)(2,1)S(1)} %collective-permute-done.1.other, bf16[384,512]{1,0:T(8,128)(2,1)S(1)} %collective-permute-done.own, ...), custom_call_target="tpu_custom_call" | custom-call | tf_op jit(solution)/shard_map/blocks_and_gradient/pallas_call | solution.py:205
  27.4 5.9 %all-to-all-start.1 = ((bf16[16,32,256]{2,1,0:T(8,128)(2,1)}), bf16[16,32,256]{2,1,0:T(8,128)(2,1)S(1)}, u32[]{:S(2)}, u32[]{:S(2)}) async-start(bf16[16,32,256]{2,1,0:T(8,128)(2,1)} %bitcast.18), calls=%async_computation.1 | async-start | bytes 524288 | tf_op jit(solution)/shard_map/all_to_all | solution.py:320
  33.3 0.7 %collective-permute-start.3 = (bf16[256,256]{1,0:T(8,128)(2,1)S(1)}, bf16[256,256]{1,0:T(8,128)(2,1)S(1)}, u32[]{:S(2)}, u32[]{:S(2)}) collective-permute-start(bf16[256,256]{1,0:T(8,128)(2,1)S(1)} %get-tuple-element.17), channel_id=1, source_target_pairs={{0,0},{1,2},{2,1},{3,3},{4,4},{5,6},{6,5},{7,7},{8,8},{9,10},{10,9... | collective-permute-start | bytes 393224 | tf_op jit(solution)/shard_map/ppermute | solution.py:318
  33.9 0.0 collective-permute-done.3.act
  34.0 6.2 %all-to-all-done.1.terms = bf16[16,32,256]{2,1,0:T(8,128)(2,1)S(1)} async-done(((bf16[16,32,256]{2,1,0:T(8,128)(2,1)}), bf16[16,32,256]{2,1,0:T(8,128)(2,1)S(1)}, u32[]{:S(2)}, u32[]{:S(2)}) %all-to-all-start.1) | async-done | bytes 262176 | tf_op jit(solution)/shard_map/all_to_all | solution.py:320
  40.2 0.7 %finish.1 = (f32[32,256]{1,0:T(8,128)}, bf16[256,256]{1,0:T(8,128)(2,1)}) custom-call(bf16[16,32,256]{2,1,0:T(8,128)(2,1)S(1)} %all-to-all-done.1.terms, bf16[256,256]{1,0:T(8,128)(2,1)S(1)} %collective-permute-done.3.act), custom_call_target="tpu_custom_call" | custom-call | tf_op jit(solution)/shard_map/finish/pallas_call | solution.py:251
  (8 shorter events, 0.1 us)
Async XLA Ops:
  2.4 9.7 %copy-start = (bf16[1,1,8,128,128]{4,3,2,1,0:T(8,128)(2,1)S(1)}, bf16[1,1,8,128,128]{4,3,2,1,0:T(8,128)(2,1)}, u32[]{:S(2)}) copy-start(bf16[1,1,8,128,128]{4,3,2,1,0:T(8,128)(2,1)} %param.14) | copy-start | bytes 786436
  2.4 9.7 %copy-start.1 = (bf16[256,256]{1,0:T(8,128)(2,1)S(1)}, bf16[256,256]{1,0:T(8,128)(2,1)}, u32[]{:S(2)}) copy-start(bf16[256,256]{1,0:T(8,128)(2,1)} %cotangent.1) | copy-start | bytes 393220
  2.4 11.6 %copy-start.5 = (bf16[1024,256]{1,0:T(8,128)(2,1)S(1)}, bf16[1024,256]{1,0:T(8,128)(2,1)}, u32[]{:S(2)}) copy-start(bf16[1024,256]{1,0:T(8,128)(2,1)} %param.9) | copy-start | bytes 1572868
  2.4 20.5 %all-to-all-start = ((bf16[16,64,256]{2,1,0:T(8,128)(2,1)}), bf16[16,64,256]{2,1,0:T(8,128)(2,1)S(1)}, u32[]{:S(2)}, u32[]{:S(2)}) async-start(bf16[16,64,256]{2,1,0:T(8,128)(2,1)} %bitcast.51), calls=%async_computation | async-start | bytes 1048576 | tf_op jit(solution)/shard_map/all_to_all | solution.py:285
  12.0 0.7 %copy-start.2 = (s32[1,1,8]{2,1,0:T(1,128)S(1)}, s32[1,1,8]{2,1,0:T(1,128)}, u32[]{:S(2)}) copy-start(s32[1,1,8]{2,1,0:T(1,128)} %param.10) | copy-start | bytes 100
  12.0 0.7 %copy-start.3 = (s32[1,1,8]{2,1,0:T(1,128)S(1)}, s32[1,1,8]{2,1,0:T(1,128)}, u32[]{:S(2)}) copy-start(s32[1,1,8]{2,1,0:T(1,128)} %param.11) | copy-start | bytes 100
  12.0 0.7 %copy-start.4 = (s32[1,1,8]{2,1,0:T(1,128)S(1)}, s32[1,1,8]{2,1,0:T(1,128)}, u32[]{:S(2)}) copy-start(s32[1,1,8]{2,1,0:T(1,128)} %param.12) | copy-start | bytes 100
  13.3 1.0 %collective-permute-start = (bf16[384,512]{1,0:T(8,128)(2,1)S(1)}, bf16[384,512]{1,0:T(8,128)(2,1)S(1)}, u32[]{:S(2)}, u32[]{:S(2)}) collective-permute-start(bf16[384,512]{1,0:T(8,128)(2,1)S(1)} %side_inputs.1), channel_id=1, source_target_pairs={{0,0},{1,2},{2,1},{3,3},{4,4},{5,6},{6,5},{7,7},{8,8},{9,10},{10,9... | collective-permute-start | bytes 1179656 | tf_op jit(solution)/shard_map/ppermute | solution.py:293
  22.9 2.8 %collective-permute-start.2 = (bf16[384,512]{1,0:T(8,128)(2,1)S(1)}, bf16[384,512]{1,0:T(8,128)(2,1)S(1)}, u32[]{:S(2)}, u32[]{:S(2)}) collective-permute-start(bf16[384,512]{1,0:T(8,128)(2,1)S(1)} %collective-permute-done.own), channel_id=1, source_target_pairs={{0,2},{2,0},{1,3},{3,1},{4,6},{6,4},{5,7},{7,5},{8,10},{10,8},{9,1... | collective-permute-start | bytes 1179656 | tf_op jit(solution)/shard_map/ppermute | solution.py:300
  24.1 1.6 %collective-permute-start.1 = (bf16[256,512]{1,0:T(8,128)(2,1)S(1)}, bf16[256,512]{1,0:T(8,128)(2,1)S(1)}, u32[]{:S(2)}, u32[]{:S(2)}) collective-permute-start(bf16[256,512]{1,0:T(8,128)(2,1)S(1)} %get-tuple-element.14), channel_id=1, source_target_pairs={{0,2},{2,0},{1,3},{3,1},{4,6},{6,4},{5,7},{7,5},{8,10},{10,8},{9,1... | collective-permute-start | bytes 786440 | tf_op jit(solution)/shard_map/ppermute | solution.py:303
  27.4 12.8 %all-to-all-start.1 = ((bf16[16,32,256]{2,1,0:T(8,128)(2,1)}), bf16[16,32,256]{2,1,0:T(8,128)(2,1)S(1)}, u32[]{:S(2)}, u32[]{:S(2)}) async-start(bf16[16,32,256]{2,1,0:T(8,128)(2,1)} %bitcast.18), calls=%async_computation.1 | async-start | bytes 524288 | tf_op jit(solution)/shard_map/all_to_all | solution.py:320
  33.3 0.7 %collective-permute-start.3 = (bf16[256,256]{1,0:T(8,128)(2,1)S(1)}, bf16[256,256]{1,0:T(8,128)(2,1)S(1)}, u32[]{:S(2)}, u32[]{:S(2)}) collective-permute-start(bf16[256,256]{1,0:T(8,128)(2,1)S(1)} %get-tuple-element.17), channel_id=1, source_target_pairs={{0,0},{1,2},{2,1},{3,3},{4,4},{5,6},{6,5},{7,7},{8,8},{9,10},{10,9... | collective-permute-start | bytes 393224 | tf_op jit(solution)/shard_map/ppermute | solution.py:318

commit v7 on v6

--- a/solution.py
+++ b/solution.py
@@ -136,7 +136,7 @@
     return side[:rows, :], cotangent
 
 
-def block_terms(nodes, side, rows, act=None):
+def block_grads(nodes, side, rows, act=None):
     adjacency, cotangent = parts(side, rows, nodes.shape[0])
     preact = dot(nodes, adjacency, 1, 1)
     normal_cdf = 0.5 * (1.0 + lax.erf(preact * root_half))
@@ -144,8 +144,39 @@
     if act is not None:
         act[...] = (preact * normal_cdf).astype(act.dtype)
     derivative = normal_cdf + preact * normal_pdf
-    pre_grad = (cotangent.astype(jnp.float32) * derivative).astype(jnp.bfloat16)
-    return dot(pre_grad, adjacency, 1, 0)
+    return (cotangent.astype(jnp.float32) * derivative).astype(jnp.bfloat16)
+
+
+def block_terms(nodes, side, rows, act=None):
+    return dot(block_grads(nodes, side, rows, act), side[:rows, :], 1, 0)
+
+
+def spread_kernel(arrived, *refs):
+    *sides, out = refs
+    places, columns, width, rows = arrived.shape
+    for at, side in enumerate(sides):
+        total = None
+        for place in range(places):
+            nodes = arrived[places - 1 - place].reshape(columns * width, rows)
+            value = dot(nodes, side[:rows, place * rows : (place + 1) * rows], 1, 1)
+            total = value if total is None else total + value
+        out[:, at * rows : (at + 1) * rows] = total.astype(out.dtype)
+
+
+def spread(arrived, sides):
+    _, columns, width, rows = arrived.shape
+    shape = (columns * width, len(sides) * rows)
+    return pl.pallas_call(
+        spread_kernel,
+        out_shape=jax.ShapeDtypeStruct(shape, arrived.dtype),
+        in_specs=[VMEM] * (1 + len(sides)),
+        out_specs=VMEM,
+        compiler_params=PARAMS,
+        cost_estimate=pl.CostEstimate(
+            flops=4 * shape[0] * shape[1] * rows, bytes_accessed=4 * shape[0] * shape[1], transcendentals=0
+        ),
+        name="spread",
+    )(arrived, *sides)
 
 
 def gradient_terms(arrived, node_grad, terms, held, sems):
@@ -175,11 +206,24 @@
         copy.wait()
 
 
-def whole_kernel(part, other, own, pair, arrived, act, terms, held, sems):
+def whole_kernel(part, other, own, pair, hidden, act, terms, held, sems):
     rows = act.shape[1]
     nodes = (part[...] + other[...].astype(jnp.float32)).astype(jnp.bfloat16)
-    total = block_terms(nodes, own, rows, act) + block_terms(nodes, pair, rows)
-    gradient_terms(arrived, total.astype(jnp.bfloat16), terms, held, sems)
+    grads = [block_grads(nodes, own, rows, act), block_grads(nodes, pair, rows)]
+    count, places, size, share, units = held.shape
+    height = hidden.shape[0] // count
+    copies = []
+    for group in range(count):
+        taken = hidden[group * height : (group + 1) * height, :]
+        total = dot(taken[:, :rows], grads[0], 1, 1) + dot(taken[:, rows:], grads[1], 1, 1)
+        total = total.astype(terms.dtype).reshape(size, places, share, units)
+        for place in range(places):
+            held[group, places - 1 - place] = total[:, place]
+        target = terms.at[:, pl.ds(group * size, size)]
+        copies.append(pltpu.make_async_copy(held.at[group], target, sems.at[group]))
+        copies[-1].start()
+    for copy in copies:
+        copy.wait()
 
 
 def node_kernel(nodes, own, pair, act, total):
@@ -200,7 +244,7 @@
     return [pltpu.VMEM(held, dtype), pltpu.SemaphoreType.DMA((count,))]
 
 
-def whole(part, other, own, pair, arrived, rows, shape):
+def whole(part, other, own, pair, hidden, rows, shape):
     act = jax.ShapeDtypeStruct((part.shape[0], rows), jnp.bfloat16)
     return pl.pallas_call(
         whole_kernel,
@@ -210,7 +254,7 @@
         scratch_shapes=gradient_scratch(shape, jnp.bfloat16),
         compiler_params=PARAMS,
         name="blocks_and_gradient",
-    )(part, other, own, pair, arrived)
+    )(part, other, own, pair, hidden)
 
 
 def node_sums(nodes, own, pair, rows):
@@ -300,6 +344,7 @@
     side_pair = lax.ppermute(side, "core", SWAP)
 
     part, sent = project(own_weight, arrived)
+    sent, arrived = lax.optimization_barrier((sent, arrived))
     other = lax.ppermute(sent, "core", SWAP)
     share = width // (2 * pairs)
     if pairs > 1:
@@ -312,8 +357,9 @@
         terms = lax.psum_scatter(terms, "hi", scatter_dimension=1, tiled=True).astype(bf16)
         terms = terms[:, 0, ::-1].transpose(1, 0, 2, 3)
     else:
+        summed = spread(arrived, (side, side_pair))
         output, terms = whole(
-            part, other, side, side_pair, arrived, rows, (2, columns, share, hidden)
+            part, other, side, side_pair, summed, rows, (2, columns, share, hidden)
         )
     act = lax.ppermute(output, ("core", "lo"), TRANSPOSE)
     terms = terms.reshape(2 * columns, share, hidden)

time: 41.3 us -> 41.1 us (level)
  waiting for transfers between devices: 16.3 us -> 15.7 us
    ppermute x1, waiting for transfers between devices: 1.52 us -> 0.09 us  [per_device(): other = lax.ppermute(sent, 'core', SWAP)]
    ppermute x1, waiting for transfers between devices: 0.01 us -> 0.96 us  [per_device(): side_pair = lax.ppermute(side, 'core', SWAP)]
    pallas_call x0 -> x1, Pallas kernels: none -> 0.46 us  [spread(): pl.pallas_call(spread_kernel, out_shape=jax.ShapeDtypeStruct(shape, arriv...]
  transfers between devices with their start and end apart: 6 -> 6, of which waited for: 3 -> 4; matrix products, arithmetic and copies ran while one was open for 1% -> 1% of each run, Pallas kernels for 2% -> 3%
where the time goes in v7:
time: 41.1 us; the launch traced here: 40.6 us
  starting transfers between devices  17.2 us (42%)
  waiting for transfers between devices  15.7 us (38%)
  Pallas kernels  5.29 us (13%)
  between operations  1.51 us (4%)
  local copies, waits for them, and re-layouts  0.9 us (2%)
    all_to_all x1, starting transfers between devices, per_device(): lax.all_to_all(chunks, axes, split_axis=0, concat_axis=0, tiled=True, axi...  8.93 us
    all_to_all x1, waiting for transfers between devices, per_device(): lax.all_to_all(chunks, axes, split_axis=0, concat_axis=0, tiled=True, axi...  8.59 us
    all_to_all x1, waiting for transfers between devices, per_device(): lax.all_to_all(terms, axes, split_axis=0, concat_axis=0, tiled=True, axis...  6.08 us
    all_to_all x1, starting transfers between devices, per_device(): lax.all_to_all(terms, axes, split_axis=0, concat_axis=0, tiled=True, axis...  6 us
    pallas_call x1, Pallas kernels, by_destination(): pl.pallas_call(chunk_kernel, out_shape=jax.ShapeDtypeStruct(shape, feats....  1.73 us
    pallas_call x1, Pallas kernels, whole(): pl.pallas_call(whole_kernel, out_shape=(act, jax.ShapeDtypeStruct(shape,...  1.48 us
    ppermute x1, waiting for transfers between devices, per_device(): side_pair = lax.ppermute(side, 'core', SWAP)  0.96 us
    ppermute x1, starting transfers between devices, per_device(): side_pair = lax.ppermute(side, 'core', SWAP)  0.87 us
  transfers between devices with their start and end apart: 6, of which 4 were waited for; matrix products, arithmetic and copies ran while one was open for 1% of the time, Pallas kernels for 3%

profile of v7, /device:TPU:0, one launch (start us, length us, event | category | flops | bytes accessed | tf_op | source)
XLA Modules:
  0.0 40.6 jit_solution(8620572559513147730)
XLA Ops:
  0.6 1.7 %by_destination.1 = bf16[2,8,64,256]{3,2,1,0:T(8,128)(2,1)} custom-call(bf16[64,4096]{1,0:T(8,128)(2,1)} %feats.1), custom_call_target="tpu_custom_call" | custom-call | tf_op jit(solution)/shard_map/by_destination/pallas_call | solution.py:57
  2.4 0.0 copy-start
  2.4 0.0 copy-start.1
  2.4 0.0 copy-start.5
  2.4 8.9 %all-to-all-start = ((bf16[16,64,256]{2,1,0:T(8,128)(2,1)}), bf16[16,64,256]{2,1,0:T(8,128)(2,1)S(1)}, u32[]{:S(2)}, u32[]{:S(2)}) async-start(bf16[16,64,256]{2,1,0:T(8,128)(2,1)} %bitcast.51), calls=%async_computation | async-start | bytes 1048576 | tf_op jit(solution)/shard_map/all_to_all | solution.py:329
  12.0 0.0 copy-start.2
  12.0 0.0 copy-start.3
  12.0 0.0 copy-start.4
  12.0 0.0 copy-done
  12.0 0.0 copy-done.1
  12.0 0.6 %copy-done.2 = s32[1,1,8]{2,1,0:T(1,128)S(1)} copy-done((s32[1,1,8]{2,1,0:T(1,128)S(1)}, s32[1,1,8]{2,1,0:T(1,128)}, u32[]{:S(2)}) %copy-start.2) | copy-done | bytes 56
  12.6 0.0 copy-done.3
  12.7 0.0 copy-done.4
  12.7 0.6 %side_inputs.1 = bf16[384,512]{1,0:T(8,128)(2,1)S(1)} custom-call(s32[8]{0:T(128)S(1)} %bitcast.48, s32[8]{0:T(128)S(1)} %bitcast.49, s32[8]{0:T(128)S(1)} %bitcast.50, s32[1]{0:T(128)} %bitcast.43.live, bf16[8,128,128]{2,1,0:T(8,128)(2,1)S(1)} %bitcast.47, bf16[256,256]{1,0:T(8,128)(2,1)S(1)} %copy-done.1), custom_call_target="tpu_custom_call" | custom-call | tf_op jit(solution)/shard_map/side_inputs/pallas_call | solution.py:94
  13.3 0.7 %collective-permute-start = (bf16[384,512]{1,0:T(8,128)(2,1)S(1)}, bf16[384,512]{1,0:T(8,128)(2,1)S(1)}, u32[]{:S(2)}, u32[]{:S(2)}) collective-permute-start(bf16[384,512]{1,0:T(8,128)(2,1)S(1)} %side_inputs.1), channel_id=1, source_target_pairs={{0,0},{1,2},{2,1},{3,3},{4,4},{5,6},{6,5},{7,7},{8,8},{9,10},{10,9... | collective-permute-start | bytes 1179656 | tf_op jit(solution)/shard_map/ppermute | solution.py:337
  14.0 0.0 copy-done.5
  14.2 0.1 copy.18
  14.3 0.0 collective-permute-done.refs_0_.own
  14.4 8.6 %all-to-all-done = bf16[16,64,256]{2,1,0:T(8,128)(2,1)S(1)} async-done(((bf16[16,64,256]{2,1,0:T(8,128)(2,1)}), bf16[16,64,256]{2,1,0:T(8,128)(2,1)S(1)}, u32[]{:S(2)}, u32[]{:S(2)}) %all-to-all-start) | async-done | bytes 524320 | tf_op jit(solution)/shard_map/all_to_all | solution.py:329
  22.9 0.9 %collective-permute-start.2 = (bf16[384,512]{1,0:T(8,128)(2,1)S(1)}, bf16[384,512]{1,0:T(8,128)(2,1)S(1)}, u32[]{:S(2)}, u32[]{:S(2)}) collective-permute-start(bf16[384,512]{1,0:T(8,128)(2,1)S(1)} %collective-permute-done.refs_0_.own), channel_id=1, source_target_pairs={{0,2},{2,0},{1,3},{3,1},{4,6},{6,4},{5,7},{7,5},{8,10},{10,8},{9,1... | collective-permute-start | bytes 1179656 | tf_op jit(solution)/shard_map/ppermute | solution.py:344
  23.8 0.3 project.1
  24.1 0.1 collective-permute-start.1
  24.2 1.0 %collective-permute-done.2.refs_1_.pair = bf16[384,512]{1,0:T(8,128)(2,1)S(1)} collective-permute-done((bf16[384,512]{1,0:T(8,128)(2,1)S(1)}, bf16[384,512]{1,0:T(8,128)(2,1)S(1)}, u32[]{:S(2)}, u32[]{:S(2)}) %collective-permute-start.2) | collective-permute-done | bytes 393248 | tf_op jit(solution)/shard_map/ppermute | solution.py:344
  25.2 0.5 %spread.1.hidden = bf16[512,512]{1,0:T(8,128)(2,1)S(1)} custom-call(bf16[2,8,64,256]{3,2,1,0:T(8,128)(2,1)S(1)} %bitcast.45, bf16[384,512]{1,0:T(8,128)(2,1)S(1)} %collective-permute-done.refs_0_.own, bf16[384,512]{1,0:T(8,128)(2,1)S(1)} %collective-permute-done.2.refs_1_.pair), custom_call_target="tpu_custom_call" | custom-call | flops 268435456 | bytes 1048576 | tf_op jit(solution)/shard_map/spread/pallas_call | solution.py:169
  25.6 0.1 collective-permute-done.1.other
  25.7 1.5 %blocks_and_gradient.1 = (bf16[256,256]{1,0:T(8,128)(2,1)S(1)}, bf16[2,8,32,256]{3,2,1,0:T(8,128)(2,1)}) custom-call(f32[256,512]{1,0:T(8,128)S(1)} %get-tuple-element.15.part, bf16[256,512]{1,0:T(8,128)(2,1)S(1)} %collective-permute-done.1.other, bf16[384,512]{1,0:T(8,128)(2,1)S(1)} %collective-permute-done.refs_0_.own, ...), custom_call_target="tpu_custom_call" | custom-call | tf_op jit(solution)/shard_map/blocks_and_gradient/pallas_call | solution.py:249
  27.2 6.0 %all-to-all-start.1 = ((bf16[16,32,256]{2,1,0:T(8,128)(2,1)}), bf16[16,32,256]{2,1,0:T(8,128)(2,1)S(1)}, u32[]{:S(2)}, u32[]{:S(2)}) async-start(bf16[16,32,256]{2,1,0:T(8,128)(2,1)} %bitcast.18), calls=%async_computation.1 | async-start | bytes 524288 | tf_op jit(solution)/shard_map/all_to_all | solution.py:366
  33.2 0.7 %collective-permute-start.3 = (bf16[256,256]{1,0:T(8,128)(2,1)S(1)}, bf16[256,256]{1,0:T(8,128)(2,1)S(1)}, u32[]{:S(2)}, u32[]{:S(2)}) collective-permute-start(bf16[256,256]{1,0:T(8,128)(2,1)S(1)} %get-tuple-element.21), channel_id=1, source_target_pairs={{0,0},{1,2},{2,1},{3,3},{4,4},{5,6},{6,5},{7,7},{8,8},{9,10},{10,9... | collective-permute-start | bytes 393224 | tf_op jit(solution)/shard_map/ppermute | solution.py:364
  33.9 0.0 collective-permute-done.3.act
  33.9 6.1 %all-to-all-done.1.terms = bf16[16,32,256]{2,1,0:T(8,128)(2,1)S(1)} async-done(((bf16[16,32,256]{2,1,0:T(8,128)(2,1)}), bf16[16,32,256]{2,1,0:T(8,128)(2,1)S(1)}, u32[]{:S(2)}, u32[]{:S(2)}) %all-to-all-start.1) | async-done | bytes 262176 | tf_op jit(solution)/shard_map/all_to_all | solution.py:366
  40.0 0.7 %finish.1 = (f32[32,256]{1,0:T(8,128)}, bf16[256,256]{1,0:T(8,128)(2,1)}) custom-call(bf16[16,32,256]{2,1,0:T(8,128)(2,1)S(1)} %all-to-all-done.1.terms, bf16[256,256]{1,0:T(8,128)(2,1)S(1)} %collective-permute-done.3.act), custom_call_target="tpu_custom_call" | custom-call | tf_op jit(solution)/shard_map/finish/pallas_call | solution.py:295
  (8 shorter events, 0.1 us)
Async XLA Ops:
  2.4 9.7 %copy-start = (bf16[1,1,8,128,128]{4,3,2,1,0:T(8,128)(2,1)S(1)}, bf16[1,1,8,128,128]{4,3,2,1,0:T(8,128)(2,1)}, u32[]{:S(2)}) copy-start(bf16[1,1,8,128,128]{4,3,2,1,0:T(8,128)(2,1)} %param.14) | copy-start | bytes 786436
  2.4 9.7 %copy-start.1 = (bf16[256,256]{1,0:T(8,128)(2,1)S(1)}, bf16[256,256]{1,0:T(8,128)(2,1)}, u32[]{:S(2)}) copy-start(bf16[256,256]{1,0:T(8,128)(2,1)} %cotangent.1) | copy-start | bytes 393220
  2.4 11.6 %copy-start.5 = (bf16[1024,256]{1,0:T(8,128)(2,1)S(1)}, bf16[1024,256]{1,0:T(8,128)(2,1)}, u32[]{:S(2)}) copy-start(bf16[1024,256]{1,0:T(8,128)(2,1)} %param.9) | copy-start | bytes 1572868
  2.4 20.5 %all-to-all-start = ((bf16[16,64,256]{2,1,0:T(8,128)(2,1)}), bf16[16,64,256]{2,1,0:T(8,128)(2,1)S(1)}, u32[]{:S(2)}, u32[]{:S(2)}) async-start(bf16[16,64,256]{2,1,0:T(8,128)(2,1)} %bitcast.51), calls=%async_computation | async-start | bytes 1048576 | tf_op jit(solution)/shard_map/all_to_all | solution.py:329
  12.0 0.7 %copy-start.2 = (s32[1,1,8]{2,1,0:T(1,128)S(1)}, s32[1,1,8]{2,1,0:T(1,128)}, u32[]{:S(2)}) copy-start(s32[1,1,8]{2,1,0:T(1,128)} %param.10) | copy-start | bytes 100
  12.0 0.7 %copy-start.3 = (s32[1,1,8]{2,1,0:T(1,128)S(1)}, s32[1,1,8]{2,1,0:T(1,128)}, u32[]{:S(2)}) copy-start(s32[1,1,8]{2,1,0:T(1,128)} %param.11) | copy-start | bytes 100
  12.0 0.7 %copy-start.4 = (s32[1,1,8]{2,1,0:T(1,128)S(1)}, s32[1,1,8]{2,1,0:T(1,128)}, u32[]{:S(2)}) copy-start(s32[1,1,8]{2,1,0:T(1,128)} %param.12) | copy-start | bytes 100
  13.3 1.0 %collective-permute-start = (bf16[384,512]{1,0:T(8,128)(2,1)S(1)}, bf16[384,512]{1,0:T(8,128)(2,1)S(1)}, u32[]{:S(2)}, u32[]{:S(2)}) collective-permute-start(bf16[384,512]{1,0:T(8,128)(2,1)S(1)} %side_inputs.1), channel_id=1, source_target_pairs={{0,0},{1,2},{2,1},{3,3},{4,4},{5,6},{6,5},{7,7},{8,8},{9,10},{10,9... | collective-permute-start | bytes 1179656 | tf_op jit(solution)/shard_map/ppermute | solution.py:337
  22.9 2.2 %collective-permute-start.2 = (bf16[384,512]{1,0:T(8,128)(2,1)S(1)}, bf16[384,512]{1,0:T(8,128)(2,1)S(1)}, u32[]{:S(2)}, u32[]{:S(2)}) collective-permute-start(bf16[384,512]{1,0:T(8,128)(2,1)S(1)} %collective-permute-done.refs_0_.own), channel_id=1, source_target_pairs={{0,2},{2,0},{1,3},{3,1},{4,6},{6,4},{5,7},{7,5},{8,10},{10,8},{9,1... | collective-permute-start | bytes 1179656 | tf_op jit(solution)/shard_map/ppermute | solution.py:344
  24.1 1.6 %collective-permute-start.1 = (bf16[256,512]{1,0:T(8,128)(2,1)S(1)}, bf16[256,512]{1,0:T(8,128)(2,1)S(1)}, u32[]{:S(2)}, u32[]{:S(2)}) collective-permute-start(bf16[256,512]{1,0:T(8,128)(2,1)S(1)} %get-tuple-element.17), channel_id=1, source_target_pairs={{0,2},{2,0},{1,3},{3,1},{4,6},{6,4},{5,7},{7,5},{8,10},{10,8},{9,1... | collective-permute-start | bytes 786440 | tf_op jit(solution)/shard_map/ppermute | solution.py:348
  27.2 12.8 %all-to-all-start.1 = ((bf16[16,32,256]{2,1,0:T(8,128)(2,1)}), bf16[16,32,256]{2,1,0:T(8,128)(2,1)S(1)}, u32[]{:S(2)}, u32[]{:S(2)}) async-start(bf16[16,32,256]{2,1,0:T(8,128)(2,1)} %bitcast.18), calls=%async_computation.1 | async-start | bytes 524288 | tf_op jit(solution)/shard_map/all_to_all | solution.py:366
  33.2 0.7 %collective-permute-start.3 = (bf16[256,256]{1,0:T(8,128)(2,1)S(1)}, bf16[256,256]{1,0:T(8,128)(2,1)S(1)}, u32[]{:S(2)}, u32[]{:S(2)}) collective-permute-start(bf16[256,256]{1,0:T(8,128)(2,1)S(1)} %get-tuple-element.21), channel_id=1, source_target_pairs={{0,0},{1,2},{2,1},{3,3},{4,4},{5,6},{6,5},{7,7},{8,8},{9,10},{10,9... | collective-permute-start | bytes 393224 | tf_op jit(solution)/shard_map/ppermute | solution.py:364

commit v8 on v7

--- a/solution.py
+++ b/solution.py
@@ -18,12 +18,15 @@
 PARAMS = pltpu.CompilerParams(vmem_limit_bytes=24 * 1024 * 1024)
 
 
-def middle_first(columns):
+def middle_first(columns, quarters=(2, 1, 0, 3)):
     quarter = max(columns // 4, 1)
     rest = sorted(range(columns), key=lambda column: -column)
-    order = [column for at in (2, 1, 3, 0) for column in rest if min(column // quarter, 3) == at]
+    order = [column for at in quarters for column in rest if min(column // quarter, 3) == at]
     order.remove(columns // 2)
     return [columns // 2] + order
+
+
+SECOND = (2, 1, 3, 0)
 
 
 def dot(left, right, left_dim, right_dim):
@@ -206,24 +209,26 @@
         copy.wait()
 
 
-def whole_kernel(part, other, own, pair, hidden, act, terms, held, sems):
+def whole_kernel(part, other, own, pair, hidden, act, terms, held, sem):
     rows = act.shape[1]
     nodes = (part[...] + other[...].astype(jnp.float32)).astype(jnp.bfloat16)
     grads = [block_grads(nodes, own, rows, act), block_grads(nodes, pair, rows)]
-    count, places, size, share, units = held.shape
+    places, columns, share, units = held.shape
+    count = 2
+    size = columns // count
+    order = middle_first(columns)
+    rank = {column: at for at, column in enumerate(middle_first(columns, SECOND))}
     height = hidden.shape[0] // count
-    copies = []
     for group in range(count):
         taken = hidden[group * height : (group + 1) * height, :]
         total = dot(taken[:, :rows], grads[0], 1, 1) + dot(taken[:, rows:], grads[1], 1, 1)
         total = total.astype(terms.dtype).reshape(size, places, share, units)
-        for place in range(places):
-            held[group, places - 1 - place] = total[:, place]
-        target = terms.at[:, pl.ds(group * size, size)]
-        copies.append(pltpu.make_async_copy(held.at[group], target, sems.at[group]))
-        copies[-1].start()
-    for copy in copies:
-        copy.wait()
+        for at in range(size):
+            for place in range(places):
+                held[places - 1 - place, rank[order[group * size + at]]] = total[at, place]
+    copy = pltpu.make_async_copy(held, terms, sem)
+    copy.start()
+    copy.wait()
 
 
 def node_kernel(nodes, own, pair, act, total):
@@ -251,7 +256,7 @@
         out_shape=(act, jax.ShapeDtypeStruct(shape, jnp.bfloat16)),
         in_specs=[VMEM] * 5,
         out_specs=(VMEM, ANY),
-        scratch_shapes=gradient_scratch(shape, jnp.bfloat16),
+        scratch_shapes=[pltpu.VMEM(shape, jnp.bfloat16), pltpu.SemaphoreType.DMA],
         compiler_params=PARAMS,
         name="blocks_and_gradient",
     )(part, other, own, pair, hidden)
@@ -319,15 +324,19 @@
     bf16 = jnp.bfloat16
     order = middle_first(columns)
     axes = ("col", "core", "hi", "lo")
-    groups = [
-        [((column * 2 + c) * pairs + hi) * 2 + place for place in (1, 0) for column in order]
-        for c in range(2)
-        for hi in range(pairs)
-    ]
+
+    def groups(listed):
+        return [
+            [((column * 2 + c) * pairs + hi) * 2 + place for place in (1, 0) for column in listed]
+            for c in range(2)
+            for hi in range(pairs)
+        ]
+
+    second = middle_first(columns, SECOND)
 
     chunks = by_destination(feats, 2, columns).reshape(2 * columns, width, rows)
     arrived = lax.all_to_all(
-        chunks, axes, split_axis=0, concat_axis=0, tiled=True, axis_index_groups=groups
+        chunks, axes, split_axis=0, concat_axis=0, tiled=True, axis_index_groups=groups(order)
     )
     arrived = arrived.reshape(2, columns, width, rows)
 
@@ -355,7 +364,7 @@
         terms = gradient(arrived, node_grad.astype(bf16), (columns * width, hidden))
         terms = terms.reshape(columns, pairs, 2, share, hidden)
         terms = lax.psum_scatter(terms, "hi", scatter_dimension=1, tiled=True).astype(bf16)
-        terms = terms[:, 0, ::-1].transpose(1, 0, 2, 3)
+        terms = jnp.stack([terms[order.index(column), 0, ::-1] for column in second], 1)
     else:
         summed = spread(arrived, (side, side_pair))
         output, terms = whole(
@@ -364,7 +373,7 @@
     act = lax.ppermute(output, ("core", "lo"), TRANSPOSE)
     terms = terms.reshape(2 * columns, share, hidden)
     terms = lax.all_to_all(
-        terms, axes, split_axis=0, concat_axis=0, tiled=True, axis_index_groups=groups
+        terms, axes, split_axis=0, concat_axis=0, tiled=True, axis_index_groups=groups(second)
     )
     weight_grad, act = finish(terms, act)
     return (act, weight_grad)

time: 41.1 us -> 40.9 us (level)
  no operation moved by 1% of the time
where the time goes in v8:
time: 40.9 us; the launch traced here: 40.4 us
  starting transfers between devices  17 us (42%)
  waiting for transfers between devices  15.8 us (39%)
  Pallas kernels  5.28 us (13%)
  between operations  1.51 us (4%)
  local copies, waits for them, and re-layouts  0.9 us (2%)
    all_to_all x1, starting transfers between devices, per_device(): lax.all_to_all(chunks, axes, split_axis=0, concat_axis=0, tiled=True, axi...  8.93 us
    all_to_all x1, waiting for transfers between devices, per_device(): lax.all_to_all(chunks, axes, split_axis=0, concat_axis=0, tiled=True, axi...  8.59 us
    all_to_all x1, waiting for transfers between devices, per_device(): lax.all_to_all(terms, axes, split_axis=0, concat_axis=0, tiled=True, axis...  6.14 us
    all_to_all x1, starting transfers between devices, per_device(): lax.all_to_all(terms, axes, split_axis=0, concat_axis=0, tiled=True, axis...  5.96 us
    pallas_call x1, Pallas kernels, by_destination(): pl.pallas_call(chunk_kernel, out_shape=jax.ShapeDtypeStruct(shape, feats....  1.73 us
    pallas_call x1, Pallas kernels, whole(): pl.pallas_call(whole_kernel, out_shape=(act, jax.ShapeDtypeStruct(shape,...  1.47 us
    ppermute x1, waiting for transfers between devices, per_device(): side_pair = lax.ppermute(side, 'core', SWAP)  0.96 us
  transfers between devices with their start and end apart: 6, of which 4 were waited for; matrix products, arithmetic and copies ran while one was open for 1% of the time, Pallas kernels for 3%

profile of v8, /device:TPU:0, one launch (start us, length us, event | category | flops | bytes accessed | tf_op | source)
XLA Modules:
  0.0 40.4 jit_solution(16045274699622194593)
XLA Ops:
  0.6 1.7 %by_destination.1 = bf16[2,8,64,256]{3,2,1,0:T(8,128)(2,1)} custom-call(bf16[64,4096]{1,0:T(8,128)(2,1)} %feats.1), custom_call_target="tpu_custom_call" | custom-call | tf_op jit(solution)/shard_map/by_destination/pallas_call | solution.py:60
  2.4 0.0 copy-start
  2.4 0.0 copy-start.1
  2.4 0.0 copy-start.5
  2.4 8.9 %all-to-all-start = ((bf16[16,64,256]{2,1,0:T(8,128)(2,1)}), bf16[16,64,256]{2,1,0:T(8,128)(2,1)S(1)}, u32[]{:S(2)}, u32[]{:S(2)}) async-start(bf16[16,64,256]{2,1,0:T(8,128)(2,1)} %bitcast.51), calls=%async_computation | async-start | bytes 1048576 | tf_op jit(solution)/shard_map/all_to_all | solution.py:338
  12.0 0.0 copy-start.2
  12.0 0.0 copy-start.3
  12.0 0.0 copy-start.4
  12.0 0.0 copy-done
  12.0 0.0 copy-done.1
  12.0 0.6 %copy-done.2 = s32[1,1,8]{2,1,0:T(1,128)S(1)} copy-done((s32[1,1,8]{2,1,0:T(1,128)S(1)}, s32[1,1,8]{2,1,0:T(1,128)}, u32[]{:S(2)}) %copy-start.2) | copy-done | bytes 56
  12.6 0.0 copy-done.3
  12.7 0.0 copy-done.4
  12.7 0.6 %side_inputs.1 = bf16[384,512]{1,0:T(8,128)(2,1)S(1)} custom-call(s32[8]{0:T(128)S(1)} %bitcast.48, s32[8]{0:T(128)S(1)} %bitcast.49, s32[8]{0:T(128)S(1)} %bitcast.50, s32[1]{0:T(128)} %bitcast.43.live, bf16[8,128,128]{2,1,0:T(8,128)(2,1)S(1)} %bitcast.47, bf16[256,256]{1,0:T(8,128)(2,1)S(1)} %copy-done.1), custom_call_target="tpu_custom_call" | custom-call | tf_op jit(solution)/shard_map/side_inputs/pallas_call | solution.py:97
  13.3 0.7 %collective-permute-start = (bf16[384,512]{1,0:T(8,128)(2,1)S(1)}, bf16[384,512]{1,0:T(8,128)(2,1)S(1)}, u32[]{:S(2)}, u32[]{:S(2)}) collective-permute-start(bf16[384,512]{1,0:T(8,128)(2,1)S(1)} %side_inputs.1), channel_id=1, source_target_pairs={{0,0},{1,2},{2,1},{3,3},{4,4},{5,6},{6,5},{7,7},{8,8},{9,10},{10,9... | collective-permute-start | bytes 1179656 | tf_op jit(solution)/shard_map/ppermute | solution.py:346
  14.0 0.0 copy-done.5
  14.2 0.1 copy.18
  14.3 0.0 collective-permute-done.refs_0_.own
  14.3 8.6 %all-to-all-done = bf16[16,64,256]{2,1,0:T(8,128)(2,1)S(1)} async-done(((bf16[16,64,256]{2,1,0:T(8,128)(2,1)}), bf16[16,64,256]{2,1,0:T(8,128)(2,1)S(1)}, u32[]{:S(2)}, u32[]{:S(2)}) %all-to-all-start) | async-done | bytes 524320 | tf_op jit(solution)/shard_map/all_to_all | solution.py:338
  22.9 0.6 %collective-permute-start.2 = (bf16[384,512]{1,0:T(8,128)(2,1)S(1)}, bf16[384,512]{1,0:T(8,128)(2,1)S(1)}, u32[]{:S(2)}, u32[]{:S(2)}) collective-permute-start(bf16[384,512]{1,0:T(8,128)(2,1)S(1)} %collective-permute-done.refs_0_.own), channel_id=1, source_target_pairs={{0,2},{2,0},{1,3},{3,1},{4,6},{6,4},{5,7},{7,5},{8,10},{10,8},{9,1... | collective-permute-start | bytes 1179656 | tf_op jit(solution)/shard_map/ppermute | solution.py:353
  23.6 0.3 project.1
  23.9 0.1 collective-permute-start.1
  24.0 1.0 %collective-permute-done.2.refs_1_.pair = bf16[384,512]{1,0:T(8,128)(2,1)S(1)} collective-permute-done((bf16[384,512]{1,0:T(8,128)(2,1)S(1)}, bf16[384,512]{1,0:T(8,128)(2,1)S(1)}, u32[]{:S(2)}, u32[]{:S(2)}) %collective-permute-start.2) | collective-permute-done | bytes 393248 | tf_op jit(solution)/shard_map/ppermute | solution.py:353
  24.9 0.5 %spread.1.hidden = bf16[512,512]{1,0:T(8,128)(2,1)S(1)} custom-call(bf16[2,8,64,256]{3,2,1,0:T(8,128)(2,1)S(1)} %bitcast.45, bf16[384,512]{1,0:T(8,128)(2,1)S(1)} %collective-permute-done.refs_0_.own, bf16[384,512]{1,0:T(8,128)(2,1)S(1)} %collective-permute-done.2.refs_1_.pair), custom_call_target="tpu_custom_call" | custom-call | flops 268435456 | bytes 1048576 | tf_op jit(solution)/shard_map/spread/pallas_call | solution.py:172
  25.4 0.1 collective-permute-done.1.other
  25.5 1.5 %blocks_and_gradient.1 = (bf16[256,256]{1,0:T(8,128)(2,1)S(1)}, bf16[2,8,32,256]{3,2,1,0:T(8,128)(2,1)}) custom-call(f32[256,512]{1,0:T(8,128)S(1)} %get-tuple-element.15.part, bf16[256,512]{1,0:T(8,128)(2,1)S(1)} %collective-permute-done.1.other, bf16[384,512]{1,0:T(8,128)(2,1)S(1)} %collective-permute-done.refs_0_.own, ...), custom_call_target="tpu_custom_call" | custom-call | tf_op jit(solution)/shard_map/blocks_and_gradient/pallas_call | solution.py:254
  27.0 6.0 %all-to-all-start.1 = ((bf16[16,32,256]{2,1,0:T(8,128)(2,1)}), bf16[16,32,256]{2,1,0:T(8,128)(2,1)S(1)}, u32[]{:S(2)}, u32[]{:S(2)}) async-start(bf16[16,32,256]{2,1,0:T(8,128)(2,1)} %bitcast.18), calls=%async_computation.1 | async-start | bytes 524288 | tf_op jit(solution)/shard_map/all_to_all | solution.py:375
  32.9 0.7 %collective-permute-start.3 = (bf16[256,256]{1,0:T(8,128)(2,1)S(1)}, bf16[256,256]{1,0:T(8,128)(2,1)S(1)}, u32[]{:S(2)}, u32[]{:S(2)}) collective-permute-start(bf16[256,256]{1,0:T(8,128)(2,1)S(1)} %get-tuple-element.21), channel_id=1, source_target_pairs={{0,0},{1,2},{2,1},{3,3},{4,4},{5,6},{6,5},{7,7},{8,8},{9,10},{10,9... | collective-permute-start | bytes 393224 | tf_op jit(solution)/shard_map/ppermute | solution.py:373
  33.6 0.0 collective-permute-done.3.act
  33.6 6.1 %all-to-all-done.1.terms = bf16[16,32,256]{2,1,0:T(8,128)(2,1)S(1)} async-done(((bf16[16,32,256]{2,1,0:T(8,128)(2,1)}), bf16[16,32,256]{2,1,0:T(8,128)(2,1)S(1)}, u32[]{:S(2)}, u32[]{:S(2)}) %all-to-all-start.1) | async-done | bytes 262176 | tf_op jit(solution)/shard_map/all_to_all | solution.py:375
  39.7 0.7 %finish.1 = (f32[32,256]{1,0:T(8,128)}, bf16[256,256]{1,0:T(8,128)(2,1)}) custom-call(bf16[16,32,256]{2,1,0:T(8,128)(2,1)S(1)} %all-to-all-done.1.terms, bf16[256,256]{1,0:T(8,128)(2,1)S(1)} %collective-permute-done.3.act), custom_call_target="tpu_custom_call" | custom-call | tf_op jit(solution)/shard_map/finish/pallas_call | solution.py:300
  (8 shorter events, 0.1 us)
Async XLA Ops:
  2.4 9.7 %copy-start = (bf16[1,1,8,128,128]{4,3,2,1,0:T(8,128)(2,1)S(1)}, bf16[1,1,8,128,128]{4,3,2,1,0:T(8,128)(2,1)}, u32[]{:S(2)}) copy-start(bf16[1,1,8,128,128]{4,3,2,1,0:T(8,128)(2,1)} %param.14) | copy-start | bytes 786436
  2.4 9.7 %copy-start.1 = (bf16[256,256]{1,0:T(8,128)(2,1)S(1)}, bf16[256,256]{1,0:T(8,128)(2,1)}, u32[]{:S(2)}) copy-start(bf16[256,256]{1,0:T(8,128)(2,1)} %cotangent.1) | copy-start | bytes 393220
  2.4 11.6 %copy-start.5 = (bf16[1024,256]{1,0:T(8,128)(2,1)S(1)}, bf16[1024,256]{1,0:T(8,128)(2,1)}, u32[]{:S(2)}) copy-start(bf16[1024,256]{1,0:T(8,128)(2,1)} %param.9) | copy-start | bytes 1572868
  2.4 20.5 %all-to-all-start = ((bf16[16,64,256]{2,1,0:T(8,128)(2,1)}), bf16[16,64,256]{2,1,0:T(8,128)(2,1)S(1)}, u32[]{:S(2)}, u32[]{:S(2)}) async-start(bf16[16,64,256]{2,1,0:T(8,128)(2,1)} %bitcast.51), calls=%async_computation | async-start | bytes 1048576 | tf_op jit(solution)/shard_map/all_to_all | solution.py:338
  12.0 0.7 %copy-start.2 = (s32[1,1,8]{2,1,0:T(1,128)S(1)}, s32[1,1,8]{2,1,0:T(1,128)}, u32[]{:S(2)}) copy-start(s32[1,1,8]{2,1,0:T(1,128)} %param.10) | copy-start | bytes 100
  12.0 0.7 %copy-start.3 = (s32[1,1,8]{2,1,0:T(1,128)S(1)}, s32[1,1,8]{2,1,0:T(1,128)}, u32[]{:S(2)}) copy-start(s32[1,1,8]{2,1,0:T(1,128)} %param.11) | copy-start | bytes 100
  12.0 0.7 %copy-start.4 = (s32[1,1,8]{2,1,0:T(1,128)S(1)}, s32[1,1,8]{2,1,0:T(1,128)}, u32[]{:S(2)}) copy-start(s32[1,1,8]{2,1,0:T(1,128)} %param.12) | copy-start | bytes 100
  13.3 1.0 %collective-permute-start = (bf16[384,512]{1,0:T(8,128)(2,1)S(1)}, bf16[384,512]{1,0:T(8,128)(2,1)S(1)}, u32[]{:S(2)}, u32[]{:S(2)}) collective-permute-start(bf16[384,512]{1,0:T(8,128)(2,1)S(1)} %side_inputs.1), channel_id=1, source_target_pairs={{0,0},{1,2},{2,1},{3,3},{4,4},{5,6},{6,5},{7,7},{8,8},{9,10},{10,9... | collective-permute-start | bytes 1179656 | tf_op jit(solution)/shard_map/ppermute | solution.py:346
  22.9 2.0 %collective-permute-start.2 = (bf16[384,512]{1,0:T(8,128)(2,1)S(1)}, bf16[384,512]{1,0:T(8,128)(2,1)S(1)}, u32[]{:S(2)}, u32[]{:S(2)}) collective-permute-start(bf16[384,512]{1,0:T(8,128)(2,1)S(1)} %collective-permute-done.refs_0_.own), channel_id=1, source_target_pairs={{0,2},{2,0},{1,3},{3,1},{4,6},{6,4},{5,7},{7,5},{8,10},{10,8},{9,1... | collective-permute-start | bytes 1179656 | tf_op jit(solution)/shard_map/ppermute | solution.py:353
  23.9 1.6 %collective-permute-start.1 = (bf16[256,512]{1,0:T(8,128)(2,1)S(1)}, bf16[256,512]{1,0:T(8,128)(2,1)S(1)}, u32[]{:S(2)}, u32[]{:S(2)}) collective-permute-start(bf16[256,512]{1,0:T(8,128)(2,1)S(1)} %get-tuple-element.17), channel_id=1, source_target_pairs={{0,2},{2,0},{1,3},{3,1},{4,6},{6,4},{5,7},{7,5},{8,10},{10,8},{9,1... | collective-permute-start | bytes 786440 | tf_op jit(solution)/shard_map/ppermute | solution.py:357
  27.0 12.8 %all-to-all-start.1 = ((bf16[16,32,256]{2,1,0:T(8,128)(2,1)}), bf16[16,32,256]{2,1,0:T(8,128)(2,1)S(1)}, u32[]{:S(2)}, u32[]{:S(2)}) async-start(bf16[16,32,256]{2,1,0:T(8,128)(2,1)} %bitcast.18), calls=%async_computation.1 | async-start | bytes 524288 | tf_op jit(solution)/shard_map/all_to_all | solution.py:375
  32.9 0.7 %collective-permute-start.3 = (bf16[256,256]{1,0:T(8,128)(2,1)S(1)}, bf16[256,256]{1,0:T(8,128)(2,1)S(1)}, u32[]{:S(2)}, u32[]{:S(2)}) collective-permute-start(bf16[256,256]{1,0:T(8,128)(2,1)S(1)} %get-tuple-element.21), channel_id=1, source_target_pairs={{0,0},{1,2},{2,1},{3,3},{4,4},{5,6},{6,5},{7,7},{8,8},{9,10},{10,9... | collective-permute-start | bytes 393224 | tf_op jit(solution)/shard_map/ppermute | solution.py:373

commit v9 on v8

--- a/solution.py
+++ b/solution.py
@@ -82,7 +82,7 @@
         col = pl.multiple_of(col_tile[slot] * tile, tile)
         block = blocks[block_index[slot]]
         out[pl.ds(row, tile), pl.ds(col, tile)] = jnp.where(
-            slot < live[0], block, jnp.zeros_like(block)
+            slot < live[...], block, jnp.zeros_like(block)
         )
     for group in range(groups):
         out[rows : rows + part, group * rows : (group + 1) * rows] = cotangent[
@@ -97,7 +97,7 @@
     return pl.pallas_call(
         side_kernel,
         out_shape=jax.ShapeDtypeStruct((rows + hidden * rows // cluster, cluster), blocks.dtype),
-        in_specs=[SMEM] * 4 + [VMEM] * 2,
+        in_specs=[SMEM] * 3 + [VMEM] * 3,
         out_specs=VMEM,
         compiler_params=PARAMS,
         name="side_inputs",
@@ -341,7 +341,7 @@
     arrived = arrived.reshape(2, columns, width, rows)
 
     side = side_inputs(
-        tile_row[0, 0], tile_col[0, 0], tile_block[0, 0], tile_count[0], edge_blocks[0, 0], cotangent
+        tile_row[0, 0], tile_col[0, 0], tile_block[0, 0], tile_count, edge_blocks[0, 0], cotangent
     )
     side = lax.ppermute(side, ("core", "lo"), TRANSPOSE)
     own_weight = lax.dynamic_index_in_dim(

time: 40.9 us -> 40.9 us (level)
  transfers between devices with their start and end apart: 6 -> 6, of which waited for: 4 -> 4; matrix products, arithmetic and copies ran while one was open for 1% -> 1% of each run, Pallas kernels for 3% -> 4%
where the time goes in v9:
time: 40.9 us; the launch traced here: 40.4 us
  starting transfers between devices  17 us (42%)
  waiting for transfers between devices  15.7 us (38%)
  Pallas kernels  5.33 us (13%)
  between operations  1.51 us (4%)
  local copies, waits for them, and re-layouts  0.9 us (2%)
    all_to_all x1, starting transfers between devices, per_device(): lax.all_to_all(chunks, axes, split_axis=0, concat_axis=0, tiled=True, axi...  8.93 us
    all_to_all x1, waiting for transfers between devices, per_device(): lax.all_to_all(chunks, axes, split_axis=0, concat_axis=0, tiled=True, axi...  8.54 us
    all_to_all x1, waiting for transfers between devices, per_device(): lax.all_to_all(terms, axes, split_axis=0, concat_axis=0, tiled=True, axis...  6.13 us
    all_to_all x1, starting transfers between devices, per_device(): lax.all_to_all(terms, axes, split_axis=0, concat_axis=0, tiled=True, axis...  5.96 us
    pallas_call x1, Pallas kernels, by_destination(): pl.pallas_call(chunk_kernel, out_shape=jax.ShapeDtypeStruct(shape, feats....  1.73 us
    pallas_call x1, Pallas kernels, whole(): pl.pallas_call(whole_kernel, out_shape=(act, jax.ShapeDtypeStruct(shape,...  1.47 us
    ppermute x1, waiting for transfers between devices, per_device(): side_pair = lax.ppermute(side, 'core', SWAP)  0.96 us
  transfers between devices with their start and end apart: 6, of which 4 were waited for; matrix products, arithmetic and copies ran while one was open for 1% of the time, Pallas kernels for 4%

profile of v9, /device:TPU:0, one launch (start us, length us, event | category | flops | bytes accessed | tf_op | source)
XLA Modules:
  0.0 40.4 jit_solution(12873534287855798322)
XLA Ops:
  0.6 1.7 %by_destination.1 = bf16[2,8,64,256]{3,2,1,0:T(8,128)(2,1)} custom-call(bf16[64,4096]{1,0:T(8,128)(2,1)} %feats.1), custom_call_target="tpu_custom_call" | custom-call | tf_op jit(solution)/shard_map/by_destination/pallas_call | solution.py:60
  2.4 0.0 copy-start
  2.4 0.0 copy-start.1
  2.4 0.0 copy-start.5
  2.4 8.9 %all-to-all-start = ((bf16[16,64,256]{2,1,0:T(8,128)(2,1)}), bf16[16,64,256]{2,1,0:T(8,128)(2,1)S(1)}, u32[]{:S(2)}, u32[]{:S(2)}) async-start(bf16[16,64,256]{2,1,0:T(8,128)(2,1)} %bitcast.49), calls=%async_computation | async-start | bytes 1048576 | tf_op jit(solution)/shard_map/all_to_all | solution.py:338
  12.0 0.0 copy-start.2
  12.0 0.0 copy-start.3
  12.0 0.0 copy-start.4
  12.0 0.0 copy-done
  12.0 0.0 copy-done.1
  12.0 0.6 %copy-done.2 = s32[1,1,8]{2,1,0:T(1,128)S(1)} copy-done((s32[1,1,8]{2,1,0:T(1,128)S(1)}, s32[1,1,8]{2,1,0:T(1,128)}, u32[]{:S(2)}) %copy-start.2) | copy-done | bytes 56
  12.6 0.0 copy-done.3
  12.7 0.0 copy-done.4
  12.7 0.7 %side_inputs.1 = bf16[384,512]{1,0:T(8,128)(2,1)S(1)} custom-call(s32[8]{0:T(128)S(1)} %bitcast.46, s32[8]{0:T(128)S(1)} %bitcast.47, s32[8]{0:T(128)S(1)} %bitcast.48, s32[1,1]{1,0:T(1,128)S(6)} %copy.26.live, bf16[8,128,128]{2,1,0:T(8,128)(2,1)S(1)} %bitcast.45, bf16[256,256]{1,0:T(8,128)(2,1)S(1)} %copy-done.1), custom_call_target="tpu_custom_call" | custom-call | tf_op jit(solution)/shard_map/side_inputs/pallas_call | solution.py:97
  13.4 0.7 %collective-permute-start = (bf16[384,512]{1,0:T(8,128)(2,1)S(1)}, bf16[384,512]{1,0:T(8,128)(2,1)S(1)}, u32[]{:S(2)}, u32[]{:S(2)}) collective-permute-start(bf16[384,512]{1,0:T(8,128)(2,1)S(1)} %side_inputs.1), channel_id=1, source_target_pairs={{0,0},{1,2},{2,1},{3,3},{4,4},{5,6},{6,5},{7,7},{8,8},{9,10},{10,9... | collective-permute-start | bytes 1179656 | tf_op jit(solution)/shard_map/ppermute | solution.py:346
  14.1 0.0 copy-done.5
  14.2 0.1 copy.18
  14.4 0.0 collective-permute-done.refs_0_.own
  14.4 8.5 %all-to-all-done = bf16[16,64,256]{2,1,0:T(8,128)(2,1)S(1)} async-done(((bf16[16,64,256]{2,1,0:T(8,128)(2,1)}), bf16[16,64,256]{2,1,0:T(8,128)(2,1)S(1)}, u32[]{:S(2)}, u32[]{:S(2)}) %all-to-all-start) | async-done | bytes 524320 | tf_op jit(solution)/shard_map/all_to_all | solution.py:338
  22.9 0.6 %collective-permute-start.2 = (bf16[384,512]{1,0:T(8,128)(2,1)S(1)}, bf16[384,512]{1,0:T(8,128)(2,1)S(1)}, u32[]{:S(2)}, u32[]{:S(2)}) collective-permute-start(bf16[384,512]{1,0:T(8,128)(2,1)S(1)} %collective-permute-done.refs_0_.own), channel_id=1, source_target_pairs={{0,2},{2,0},{1,3},{3,1},{4,6},{6,4},{5,7},{7,5},{8,10},{10,8},{9,1... | collective-permute-start | bytes 1179656 | tf_op jit(solution)/shard_map/ppermute | solution.py:353
  23.6 0.3 project.1
  23.9 0.1 collective-permute-start.1
  24.0 1.0 %collective-permute-done.2.refs_1_.pair = bf16[384,512]{1,0:T(8,128)(2,1)S(1)} collective-permute-done((bf16[384,512]{1,0:T(8,128)(2,1)S(1)}, bf16[384,512]{1,0:T(8,128)(2,1)S(1)}, u32[]{:S(2)}, u32[]{:S(2)}) %collective-permute-start.2) | collective-permute-done | bytes 393248 | tf_op jit(solution)/shard_map/ppermute | solution.py:353
  24.9 0.5 %spread.1.hidden = bf16[512,512]{1,0:T(8,128)(2,1)S(1)} custom-call(bf16[2,8,64,256]{3,2,1,0:T(8,128)(2,1)S(1)} %bitcast.43, bf16[384,512]{1,0:T(8,128)(2,1)S(1)} %collective-permute-done.refs_0_.own, bf16[384,512]{1,0:T(8,128)(2,1)S(1)} %collective-permute-done.2.refs_1_.pair), custom_call_target="tpu_custom_call" | custom-call | flops 268435456 | bytes 1048576 | tf_op jit(solution)/shard_map/spread/pallas_call | solution.py:172
  25.4 0.1 collective-permute-done.1.other
  25.5 1.5 %blocks_and_gradient.1 = (bf16[256,256]{1,0:T(8,128)(2,1)S(1)}, bf16[2,8,32,256]{3,2,1,0:T(8,128)(2,1)}) custom-call(f32[256,512]{1,0:T(8,128)S(1)} %get-tuple-element.15.part, bf16[256,512]{1,0:T(8,128)(2,1)S(1)} %collective-permute-done.1.other, bf16[384,512]{1,0:T(8,128)(2,1)S(1)} %collective-permute-done.refs_0_.own, ...), custom_call_target="tpu_custom_call" | custom-call | tf_op jit(solution)/shard_map/blocks_and_gradient/pallas_call | solution.py:254
  27.0 6.0 %all-to-all-start.1 = ((bf16[16,32,256]{2,1,0:T(8,128)(2,1)}), bf16[16,32,256]{2,1,0:T(8,128)(2,1)S(1)}, u32[]{:S(2)}, u32[]{:S(2)}) async-start(bf16[16,32,256]{2,1,0:T(8,128)(2,1)} %bitcast.17), calls=%async_computation.1 | async-start | bytes 524288 | tf_op jit(solution)/shard_map/all_to_all | solution.py:375
  32.9 0.7 %collective-permute-start.3 = (bf16[256,256]{1,0:T(8,128)(2,1)S(1)}, bf16[256,256]{1,0:T(8,128)(2,1)S(1)}, u32[]{:S(2)}, u32[]{:S(2)}) collective-permute-start(bf16[256,256]{1,0:T(8,128)(2,1)S(1)} %get-tuple-element.21), channel_id=1, source_target_pairs={{0,0},{1,2},{2,1},{3,3},{4,4},{5,6},{6,5},{7,7},{8,8},{9,10},{10,9... | collective-permute-start | bytes 393224 | tf_op jit(solution)/shard_map/ppermute | solution.py:373
  33.6 0.0 collective-permute-done.3.act
  33.6 6.1 %all-to-all-done.1.terms = bf16[16,32,256]{2,1,0:T(8,128)(2,1)S(1)} async-done(((bf16[16,32,256]{2,1,0:T(8,128)(2,1)}), bf16[16,32,256]{2,1,0:T(8,128)(2,1)S(1)}, u32[]{:S(2)}, u32[]{:S(2)}) %all-to-all-start.1) | async-done | bytes 262176 | tf_op jit(solution)/shard_map/all_to_all | solution.py:375
  39.7 0.7 %finish.1 = (f32[32,256]{1,0:T(8,128)}, bf16[256,256]{1,0:T(8,128)(2,1)}) custom-call(bf16[16,32,256]{2,1,0:T(8,128)(2,1)S(1)} %all-to-all-done.1.terms, bf16[256,256]{1,0:T(8,128)(2,1)S(1)} %collective-permute-done.3.act), custom_call_target="tpu_custom_call" | custom-call | tf_op jit(solution)/shard_map/finish/pallas_call | solution.py:300
  (8 shorter events, 0.1 us)
Async XLA Ops:
  2.4 9.7 %copy-start = (bf16[1,1,8,128,128]{4,3,2,1,0:T(8,128)(2,1)S(1)}, bf16[1,1,8,128,128]{4,3,2,1,0:T(8,128)(2,1)}, u32[]{:S(2)}) copy-start(bf16[1,1,8,128,128]{4,3,2,1,0:T(8,128)(2,1)} %param.14) | copy-start | bytes 786436
  2.4 9.7 %copy-start.1 = (bf16[256,256]{1,0:T(8,128)(2,1)S(1)}, bf16[256,256]{1,0:T(8,128)(2,1)}, u32[]{:S(2)}) copy-start(bf16[256,256]{1,0:T(8,128)(2,1)} %cotangent.1) | copy-start | bytes 393220
  2.4 11.7 %copy-start.5 = (bf16[1024,256]{1,0:T(8,128)(2,1)S(1)}, bf16[1024,256]{1,0:T(8,128)(2,1)}, u32[]{:S(2)}) copy-start(bf16[1024,256]{1,0:T(8,128)(2,1)} %param.9) | copy-start | bytes 1572868
  2.4 20.5 %all-to-all-start = ((bf16[16,64,256]{2,1,0:T(8,128)(2,1)}), bf16[16,64,256]{2,1,0:T(8,128)(2,1)S(1)}, u32[]{:S(2)}, u32[]{:S(2)}) async-start(bf16[16,64,256]{2,1,0:T(8,128)(2,1)} %bitcast.49), calls=%async_computation | async-start | bytes 1048576 | tf_op jit(solution)/shard_map/all_to_all | solution.py:338
  12.0 0.7 %copy-start.2 = (s32[1,1,8]{2,1,0:T(1,128)S(1)}, s32[1,1,8]{2,1,0:T(1,128)}, u32[]{:S(2)}) copy-start(s32[1,1,8]{2,1,0:T(1,128)} %param.10) | copy-start | bytes 100
  12.0 0.7 %copy-start.3 = (s32[1,1,8]{2,1,0:T(1,128)S(1)}, s32[1,1,8]{2,1,0:T(1,128)}, u32[]{:S(2)}) copy-start(s32[1,1,8]{2,1,0:T(1,128)} %param.11) | copy-start | bytes 100
  12.0 0.7 %copy-start.4 = (s32[1,1,8]{2,1,0:T(1,128)S(1)}, s32[1,1,8]{2,1,0:T(1,128)}, u32[]{:S(2)}) copy-start(s32[1,1,8]{2,1,0:T(1,128)} %param.12) | copy-start | bytes 100
  13.4 1.0 %collective-permute-start = (bf16[384,512]{1,0:T(8,128)(2,1)S(1)}, bf16[384,512]{1,0:T(8,128)(2,1)S(1)}, u32[]{:S(2)}, u32[]{:S(2)}) collective-permute-start(bf16[384,512]{1,0:T(8,128)(2,1)S(1)} %side_inputs.1), channel_id=1, source_target_pairs={{0,0},{1,2},{2,1},{3,3},{4,4},{5,6},{6,5},{7,7},{8,8},{9,10},{10,9... | collective-permute-start | bytes 1179656 | tf_op jit(solution)/shard_map/ppermute | solution.py:346
  22.9 2.0 %collective-permute-start.2 = (bf16[384,512]{1,0:T(8,128)(2,1)S(1)}, bf16[384,512]{1,0:T(8,128)(2,1)S(1)}, u32[]{:S(2)}, u32[]{:S(2)}) collective-permute-start(bf16[384,512]{1,0:T(8,128)(2,1)S(1)} %collective-permute-done.refs_0_.own), channel_id=1, source_target_pairs={{0,2},{2,0},{1,3},{3,1},{4,6},{6,4},{5,7},{7,5},{8,10},{10,8},{9,1... | collective-permute-start | bytes 1179656 | tf_op jit(solution)/shard_map/ppermute | solution.py:353
  23.9 1.6 %collective-permute-start.1 = (bf16[256,512]{1,0:T(8,128)(2,1)S(1)}, bf16[256,512]{1,0:T(8,128)(2,1)S(1)}, u32[]{:S(2)}, u32[]{:S(2)}) collective-permute-start(bf16[256,512]{1,0:T(8,128)(2,1)S(1)} %get-tuple-element.17), channel_id=1, source_target_pairs={{0,2},{2,0},{1,3},{3,1},{4,6},{6,4},{5,7},{7,5},{8,10},{10,8},{9,1... | collective-permute-start | bytes 786440 | tf_op jit(solution)/shard_map/ppermute | solution.py:357
  27.0 12.8 %all-to-all-start.1 = ((bf16[16,32,256]{2,1,0:T(8,128)(2,1)}), bf16[16,32,256]{2,1,0:T(8,128)(2,1)S(1)}, u32[]{:S(2)}, u32[]{:S(2)}) async-start(bf16[16,32,256]{2,1,0:T(8,128)(2,1)} %bitcast.17), calls=%async_computation.1 | async-start | bytes 524288 | tf_op jit(solution)/shard_map/all_to_all | solution.py:375
  32.9 0.7 %collective-permute-start.3 = (bf16[256,256]{1,0:T(8,128)(2,1)S(1)}, bf16[256,256]{1,0:T(8,128)(2,1)S(1)}, u32[]{:S(2)}, u32[]{:S(2)}) collective-permute-start(bf16[256,256]{1,0:T(8,128)(2,1)S(1)} %get-tuple-element.21), channel_id=1, source_target_pairs={{0,0},{1,2},{2,1},{3,3},{4,4},{5,6},{6,5},{7,7},{8,8},{9,10},{10,9... | collective-permute-start | bytes 393224 | tf_op jit(solution)/shard_map/ppermute | solution.py:373

commit v10 on v8

--- a/solution.py
+++ b/solution.py
@@ -212,7 +212,9 @@
 def whole_kernel(part, other, own, pair, hidden, act, terms, held, sem):
     rows = act.shape[1]
     nodes = (part[...] + other[...].astype(jnp.float32)).astype(jnp.bfloat16)
-    grads = [block_grads(nodes, own, rows, act), block_grads(nodes, pair, rows)]
+    grads = jnp.concatenate(
+        [block_grads(nodes, own, rows, act), block_grads(nodes, pair, rows)], 1
+    )
     places, columns, share, units = held.shape
     count = 2
     size = columns // count
@@ -221,7 +223,7 @@
     height = hidden.shape[0] // count
     for group in range(count):
         taken = hidden[group * height : (group + 1) * height, :]
-        total = dot(taken[:, :rows], grads[0], 1, 1) + dot(taken[:, rows:], grads[1], 1, 1)
+        total = dot(taken, grads, 1, 1)
         total = total.astype(terms.dtype).reshape(size, places, share, units)
         for at in range(size):
             for place in range(places):

time: 40.9 us -> 40.9 us (level)
  no operation moved by 1% of the time
where the time goes in v10:
time: 40.9 us; the launch traced here: 40.4 us
  starting transfers between devices  16.9 us (41%)
  waiting for transfers between devices  15.8 us (39%)
  Pallas kernels  5.3 us (13%)
  between operations  1.51 us (4%)
  local copies, waits for them, and re-layouts  0.9 us (2%)
    all_to_all x1, starting transfers between devices, per_device(): lax.all_to_all(chunks, axes, split_axis=0, concat_axis=0, tiled=True, axi...  8.93 us
    all_to_all x1, waiting for transfers between devices, per_device(): lax.all_to_all(chunks, axes, split_axis=0, concat_axis=0, tiled=True, axi...  8.59 us
    all_to_all x1, waiting for transfers between devices, per_device(): lax.all_to_all(terms, axes, split_axis=0, concat_axis=0, tiled=True, axis...  6.16 us
    all_to_all x1, starting transfers between devices, per_device(): lax.all_to_all(terms, axes, split_axis=0, concat_axis=0, tiled=True, axis...  5.95 us
    pallas_call x1, Pallas kernels, by_destination(): pl.pallas_call(chunk_kernel, out_shape=jax.ShapeDtypeStruct(shape, feats....  1.73 us
    pallas_call x1, Pallas kernels, whole(): pl.pallas_call(whole_kernel, out_shape=(act, jax.ShapeDtypeStruct(shape,...  1.49 us
    ppermute x1, waiting for transfers between devices, per_device(): side_pair = lax.ppermute(side, 'core', SWAP)  0.96 us
  transfers between devices with their start and end apart: 6, of which 4 were waited for; matrix products, arithmetic and copies ran while one was open for 1% of the time, Pallas kernels for 3%

profile of v10, /device:TPU:0, one launch (start us, length us, event | category | flops | bytes accessed | tf_op | source)
XLA Modules:
  0.0 40.4 jit_solution(11775704828295030620)
XLA Ops:
  0.6 1.7 %by_destination.1 = bf16[2,8,64,256]{3,2,1,0:T(8,128)(2,1)} custom-call(bf16[64,4096]{1,0:T(8,128)(2,1)} %feats.1), custom_call_target="tpu_custom_call" | custom-call | tf_op jit(solution)/shard_map/by_destination/pallas_call | solution.py:60
  2.4 0.0 copy-start
  2.4 0.0 copy-start.1
  2.4 0.0 copy-start.5
  2.4 8.9 %all-to-all-start = ((bf16[16,64,256]{2,1,0:T(8,128)(2,1)}), bf16[16,64,256]{2,1,0:T(8,128)(2,1)S(1)}, u32[]{:S(2)}, u32[]{:S(2)}) async-start(bf16[16,64,256]{2,1,0:T(8,128)(2,1)} %bitcast.51), calls=%async_computation | async-start | bytes 1048576 | tf_op jit(solution)/shard_map/all_to_all | solution.py:340
  12.0 0.0 copy-start.2
  12.0 0.0 copy-start.3
  12.0 0.0 copy-start.4
  12.0 0.0 copy-done
  12.0 0.0 copy-done.1
  12.0 0.6 %copy-done.2 = s32[1,1,8]{2,1,0:T(1,128)S(1)} copy-done((s32[1,1,8]{2,1,0:T(1,128)S(1)}, s32[1,1,8]{2,1,0:T(1,128)}, u32[]{:S(2)}) %copy-start.2) | copy-done | bytes 56
  12.6 0.0 copy-done.3
  12.7 0.0 copy-done.4
  12.7 0.6 %side_inputs.1 = bf16[384,512]{1,0:T(8,128)(2,1)S(1)} custom-call(s32[8]{0:T(128)S(1)} %bitcast.48, s32[8]{0:T(128)S(1)} %bitcast.49, s32[8]{0:T(128)S(1)} %bitcast.50, s32[1]{0:T(128)} %bitcast.43.live, bf16[8,128,128]{2,1,0:T(8,128)(2,1)S(1)} %bitcast.47, bf16[256,256]{1,0:T(8,128)(2,1)S(1)} %copy-done.1), custom_call_target="tpu_custom_call" | custom-call | tf_op jit(solution)/shard_map/side_inputs/pallas_call | solution.py:97
  13.3 0.7 %collective-permute-start = (bf16[384,512]{1,0:T(8,128)(2,1)S(1)}, bf16[384,512]{1,0:T(8,128)(2,1)S(1)}, u32[]{:S(2)}, u32[]{:S(2)}) collective-permute-start(bf16[384,512]{1,0:T(8,128)(2,1)S(1)} %side_inputs.1), channel_id=1, source_target_pairs={{0,0},{1,2},{2,1},{3,3},{4,4},{5,6},{6,5},{7,7},{8,8},{9,10},{10,9... | collective-permute-start | bytes 1179656 | tf_op jit(solution)/shard_map/ppermute | solution.py:348
  14.0 0.0 copy-done.5
  14.2 0.1 copy.18
  14.3 0.0 collective-permute-done.refs_0_.own
  14.3 8.6 %all-to-all-done = bf16[16,64,256]{2,1,0:T(8,128)(2,1)S(1)} async-done(((bf16[16,64,256]{2,1,0:T(8,128)(2,1)}), bf16[16,64,256]{2,1,0:T(8,128)(2,1)S(1)}, u32[]{:S(2)}, u32[]{:S(2)}) %all-to-all-start) | async-done | bytes 524320 | tf_op jit(solution)/shard_map/all_to_all | solution.py:340
  22.9 0.6 %collective-permute-start.2 = (bf16[384,512]{1,0:T(8,128)(2,1)S(1)}, bf16[384,512]{1,0:T(8,128)(2,1)S(1)}, u32[]{:S(2)}, u32[]{:S(2)}) collective-permute-start(bf16[384,512]{1,0:T(8,128)(2,1)S(1)} %collective-permute-done.refs_0_.own), channel_id=1, source_target_pairs={{0,2},{2,0},{1,3},{3,1},{4,6},{6,4},{5,7},{7,5},{8,10},{10,8},{9,1... | collective-permute-start | bytes 1179656 | tf_op jit(solution)/shard_map/ppermute | solution.py:355
  23.6 0.3 project.1
  23.9 0.1 collective-permute-start.1
  24.0 1.0 %collective-permute-done.2.refs_1_.pair = bf16[384,512]{1,0:T(8,128)(2,1)S(1)} collective-permute-done((bf16[384,512]{1,0:T(8,128)(2,1)S(1)}, bf16[384,512]{1,0:T(8,128)(2,1)S(1)}, u32[]{:S(2)}, u32[]{:S(2)}) %collective-permute-start.2) | collective-permute-done | bytes 393248 | tf_op jit(solution)/shard_map/ppermute | solution.py:355
  24.9 0.5 %spread.1.hidden = bf16[512,512]{1,0:T(8,128)(2,1)S(1)} custom-call(bf16[2,8,64,256]{3,2,1,0:T(8,128)(2,1)S(1)} %bitcast.45, bf16[384,512]{1,0:T(8,128)(2,1)S(1)} %collective-permute-done.refs_0_.own, bf16[384,512]{1,0:T(8,128)(2,1)S(1)} %collective-permute-done.2.refs_1_.pair), custom_call_target="tpu_custom_call" | custom-call | flops 268435456 | bytes 1048576 | tf_op jit(solution)/shard_map/spread/pallas_call | solution.py:172
  25.4 0.1 collective-permute-done.1.other
  25.5 1.5 %blocks_and_gradient.1 = (bf16[256,256]{1,0:T(8,128)(2,1)S(1)}, bf16[2,8,32,256]{3,2,1,0:T(8,128)(2,1)}) custom-call(f32[256,512]{1,0:T(8,128)S(1)} %get-tuple-element.15.part, bf16[256,512]{1,0:T(8,128)(2,1)S(1)} %collective-permute-done.1.other, bf16[384,512]{1,0:T(8,128)(2,1)S(1)} %collective-permute-done.refs_0_.own, ...), custom_call_target="tpu_custom_call" | custom-call | tf_op jit(solution)/shard_map/blocks_and_gradient/pallas_call | solution.py:256
  27.0 5.9 %all-to-all-start.1 = ((bf16[16,32,256]{2,1,0:T(8,128)(2,1)}), bf16[16,32,256]{2,1,0:T(8,128)(2,1)S(1)}, u32[]{:S(2)}, u32[]{:S(2)}) async-start(bf16[16,32,256]{2,1,0:T(8,128)(2,1)} %bitcast.18), calls=%async_computation.1 | async-start | bytes 524288 | tf_op jit(solution)/shard_map/all_to_all | solution.py:377
  32.9 0.7 %collective-permute-start.3 = (bf16[256,256]{1,0:T(8,128)(2,1)S(1)}, bf16[256,256]{1,0:T(8,128)(2,1)S(1)}, u32[]{:S(2)}, u32[]{:S(2)}) collective-permute-start(bf16[256,256]{1,0:T(8,128)(2,1)S(1)} %get-tuple-element.21), channel_id=1, source_target_pairs={{0,0},{1,2},{2,1},{3,3},{4,4},{5,6},{6,5},{7,7},{8,8},{9,10},{10,9... | collective-permute-start | bytes 393224 | tf_op jit(solution)/shard_map/ppermute | solution.py:375
  33.6 0.0 collective-permute-done.3.act
  33.6 6.2 %all-to-all-done.1.terms = bf16[16,32,256]{2,1,0:T(8,128)(2,1)S(1)} async-done(((bf16[16,32,256]{2,1,0:T(8,128)(2,1)}), bf16[16,32,256]{2,1,0:T(8,128)(2,1)S(1)}, u32[]{:S(2)}, u32[]{:S(2)}) %all-to-all-start.1) | async-done | bytes 262176 | tf_op jit(solution)/shard_map/all_to_all | solution.py:377
  39.8 0.7 %finish.1 = (f32[32,256]{1,0:T(8,128)}, bf16[256,256]{1,0:T(8,128)(2,1)}) custom-call(bf16[16,32,256]{2,1,0:T(8,128)(2,1)S(1)} %all-to-all-done.1.terms, bf16[256,256]{1,0:T(8,128)(2,1)S(1)} %collective-permute-done.3.act), custom_call_target="tpu_custom_call" | custom-call | tf_op jit(solution)/shard_map/finish/pallas_call | solution.py:302
  (8 shorter events, 0.1 us)
Async XLA Ops:
  2.4 9.7 %copy-start = (bf16[1,1,8,128,128]{4,3,2,1,0:T(8,128)(2,1)S(1)}, bf16[1,1,8,128,128]{4,3,2,1,0:T(8,128)(2,1)}, u32[]{:S(2)}) copy-start(bf16[1,1,8,128,128]{4,3,2,1,0:T(8,128)(2,1)} %param.14) | copy-start | bytes 786436
  2.4 9.7 %copy-start.1 = (bf16[256,256]{1,0:T(8,128)(2,1)S(1)}, bf16[256,256]{1,0:T(8,128)(2,1)}, u32[]{:S(2)}) copy-start(bf16[256,256]{1,0:T(8,128)(2,1)} %cotangent.1) | copy-start | bytes 393220
  2.4 11.6 %copy-start.5 = (bf16[1024,256]{1,0:T(8,128)(2,1)S(1)}, bf16[1024,256]{1,0:T(8,128)(2,1)}, u32[]{:S(2)}) copy-start(bf16[1024,256]{1,0:T(8,128)(2,1)} %param.9) | copy-start | bytes 1572868
  2.4 20.5 %all-to-all-start = ((bf16[16,64,256]{2,1,0:T(8,128)(2,1)}), bf16[16,64,256]{2,1,0:T(8,128)(2,1)S(1)}, u32[]{:S(2)}, u32[]{:S(2)}) async-start(bf16[16,64,256]{2,1,0:T(8,128)(2,1)} %bitcast.51), calls=%async_computation | async-start | bytes 1048576 | tf_op jit(solution)/shard_map/all_to_all | solution.py:340
  12.0 0.7 %copy-start.2 = (s32[1,1,8]{2,1,0:T(1,128)S(1)}, s32[1,1,8]{2,1,0:T(1,128)}, u32[]{:S(2)}) copy-start(s32[1,1,8]{2,1,0:T(1,128)} %param.10) | copy-start | bytes 100
  12.0 0.7 %copy-start.3 = (s32[1,1,8]{2,1,0:T(1,128)S(1)}, s32[1,1,8]{2,1,0:T(1,128)}, u32[]{:S(2)}) copy-start(s32[1,1,8]{2,1,0:T(1,128)} %param.11) | copy-start | bytes 100
  12.0 0.7 %copy-start.4 = (s32[1,1,8]{2,1,0:T(1,128)S(1)}, s32[1,1,8]{2,1,0:T(1,128)}, u32[]{:S(2)}) copy-start(s32[1,1,8]{2,1,0:T(1,128)} %param.12) | copy-start | bytes 100
  13.3 1.0 %collective-permute-start = (bf16[384,512]{1,0:T(8,128)(2,1)S(1)}, bf16[384,512]{1,0:T(8,128)(2,1)S(1)}, u32[]{:S(2)}, u32[]{:S(2)}) collective-permute-start(bf16[384,512]{1,0:T(8,128)(2,1)S(1)} %side_inputs.1), channel_id=1, source_target_pairs={{0,0},{1,2},{2,1},{3,3},{4,4},{5,6},{6,5},{7,7},{8,8},{9,10},{10,9... | collective-permute-start | bytes 1179656 | tf_op jit(solution)/shard_map/ppermute | solution.py:348
  22.9 2.0 %collective-permute-start.2 = (bf16[384,512]{1,0:T(8,128)(2,1)S(1)}, bf16[384,512]{1,0:T(8,128)(2,1)S(1)}, u32[]{:S(2)}, u32[]{:S(2)}) collective-permute-start(bf16[384,512]{1,0:T(8,128)(2,1)S(1)} %collective-permute-done.refs_0_.own), channel_id=1, source_target_pairs={{0,2},{2,0},{1,3},{3,1},{4,6},{6,4},{5,7},{7,5},{8,10},{10,8},{9,1... | collective-permute-start | bytes 1179656 | tf_op jit(solution)/shard_map/ppermute | solution.py:355
  23.9 1.6 %collective-permute-start.1 = (bf16[256,512]{1,0:T(8,128)(2,1)S(1)}, bf16[256,512]{1,0:T(8,128)(2,1)S(1)}, u32[]{:S(2)}, u32[]{:S(2)}) collective-permute-start(bf16[256,512]{1,0:T(8,128)(2,1)S(1)} %get-tuple-element.17), channel_id=1, source_target_pairs={{0,2},{2,0},{1,3},{3,1},{4,6},{6,4},{5,7},{7,5},{8,10},{10,8},{9,1... | collective-permute-start | bytes 786440 | tf_op jit(solution)/shard_map/ppermute | solution.py:359
  27.0 12.8 %all-to-all-start.1 = ((bf16[16,32,256]{2,1,0:T(8,128)(2,1)}), bf16[16,32,256]{2,1,0:T(8,128)(2,1)S(1)}, u32[]{:S(2)}, u32[]{:S(2)}) async-start(bf16[16,32,256]{2,1,0:T(8,128)(2,1)} %bitcast.18), calls=%async_computation.1 | async-start | bytes 524288 | tf_op jit(solution)/shard_map/all_to_all | solution.py:377
  32.9 0.7 %collective-permute-start.3 = (bf16[256,256]{1,0:T(8,128)(2,1)S(1)}, bf16[256,256]{1,0:T(8,128)(2,1)S(1)}, u32[]{:S(2)}, u32[]{:S(2)}) collective-permute-start(bf16[256,256]{1,0:T(8,128)(2,1)S(1)} %get-tuple-element.21), channel_id=1, source_target_pairs={{0,0},{1,2},{2,1},{3,3},{4,4},{5,6},{6,5},{7,7},{8,8},{9,10},{10,9... | collective-permute-start | bytes 393224 | tf_op jit(solution)/shard_map/ppermute | solution.py:375
